TPU v7x, 32 devices: a whole 2x2x4 slice. The times are simulated.
32 devices in a mesh: enc: 4 (over z), kr: 2 (over y), kc: 4 (over x, core).
Axes of the slice: x: 2, y: 2, z: 4, core: 2. Of those that a mesh axis runs over, the one named last changes fastest.
Arguments:
- inputs: bfloat16 [6144, 1024], P(('enc', 'kr', 'kc')), may hold values from -6 to 6
- w_first: bfloat16 [1024, 1024], replicated, may hold values from -0.1875 to 0.1875
- w_second: bfloat16 [1024, 64], replicated, may hold values from -0.1875 to 0.1875
- inv_length: float32 [64], replicated, may hold values from 0.05 to 1.8
- probes: bfloat16 [6144, 128], P(('enc', 'kr', 'kc')), may hold values from -6 to 6
- solves: bfloat16 [6144, 128], P(('enc', 'kr', 'kc')), may hold values from -6 to 6
Outputs:
- products: bfloat16 [6144, 128], P(('enc', 'kr', 'kc'))
- grad_first: float32 [1024, 1024], P(('enc', 'kr', 'kc'))
- grad_second: float32 [1024, 64], P(('enc', 'kr', 'kc'))
All inputs are finite; a program needn't handle non-finite values.
Results may differ from a plain program's by a relative error of at most 0.007.
The roundings to bfloat16 on the way count: a program that leaves them out, or rounds other values in their place, can miss the bound.
Values may be sent and summed in bfloat16 or wider, within the bound.
No kernel may reach another device: no remote copies, remote signals or barrier semaphores. Data moves between devices by JAX's collectives and lax.ppermute only.
A program may use at most 64 MiB of HBM per device.

v0:
```python
import math

import jax
import jax.numpy as jnp
from jax import lax
from jax.sharding import PartitionSpec as P

probe_gain = 0.5
loss_gain = 0.02


def contract_inner(left, right):
    return lax.dot_general(
        left, right, (((1,), (1,)), ((), ())), preferred_element_type=jnp.float32
    )


def contract_outer(left, right):
    return lax.dot_general(
        left, right, (((0,), (0,)), ((), ())), preferred_element_type=jnp.float32
    )


def kernel_tile(row_feat, row_norm, col_feat):
    col_wide = col_feat.astype(jnp.float32)
    col_norm = jnp.sum(col_wide * col_wide, axis=1)
    cross = contract_inner(row_feat, col_feat)
    return jnp.exp(-0.5 * (row_norm[:, None] + col_norm[None, :] - 2.0 * cross))


def split_blocks(array):
    length = array.shape[0]
    candidates = [
        option_width
        for option_width in (1024, 768, 512, 384, 256, 192, 128)
        if length % option_width == 0
    ]
    width = candidates[0]
    return array.reshape(length // width, width, array.shape[1])


def row_totals(parts):
    return (
        lax.psum_scatter(parts[0], "kc", scatter_dimension=0, tiled=True),
        lax.psum_scatter(parts[1], "kc", scatter_dimension=0, tiled=True),
        lax.psum_scatter(parts[2], "kc", scatter_dimension=0, tiled=True),
    )


def local(inputs, w_first, w_second, inv_length, probes, solves):
    pre = jnp.dot(inputs, w_first, preferred_element_type=jnp.float32)
    hidden = jax.nn.silu(pre).astype(jnp.bfloat16)
    features = jnp.dot(hidden, w_second, preferred_element_type=jnp.float32)
    scaled = (features * inv_length[None, :]).astype(jnp.bfloat16)
    own_wide = scaled.astype(jnp.float32)
    own_rows = inputs.shape[0]
    row_count = own_rows * lax.axis_size("kc")
    feat_width = scaled.shape[1]
    probe_width = probes.shape[1]
    zeros_init = (
        jnp.zeros((row_count, probe_width), jnp.float32),
        jnp.zeros((row_count, feat_width), jnp.float32),
        jnp.zeros((row_count,), jnp.float32),
    )
    row_feat, row_probe, row_solve = (
        lax.all_gather(scaled, "kc", axis=0, tiled=True),
        lax.all_gather(probes, "kc", axis=0, tiled=True),
        lax.all_gather(solves, "kc", axis=0, tiled=True),
    )
    row_wide = row_feat.astype(jnp.float32)
    row_norm = jnp.sum(row_wide * row_wide, axis=1)
    portion = (
        lax.all_gather(scaled, ("enc", "kr"), axis=0, tiled=True),
        lax.all_gather(probes, ("enc", "kr"), axis=0, tiled=True),
        lax.all_gather(solves, ("enc", "kr"), axis=0, tiled=True),
    )

    def advance(totals, columns):
        col_feat, col_probe, col_solve = columns
        kernel = kernel_tile(row_feat, row_norm, col_feat)
        first = kernel * contract_inner(row_solve, col_probe)
        second = kernel * contract_inner(row_probe, col_solve)
        mixed_part = jnp.dot(
            first.astype(jnp.bfloat16), col_feat, preferred_element_type=jnp.float32
        ) + jnp.dot(second.astype(jnp.bfloat16), col_feat, preferred_element_type=jnp.float32)
        vpart = jnp.dot(kernel.astype(jnp.bfloat16), col_probe, preferred_element_type=jnp.float32)
        return (
            (
                totals[0] + vpart,
                totals[1] + mixed_part,
                totals[2] + jnp.sum(first, axis=1) + jnp.sum(second, axis=1),
            ),
            None,
        )

    stacked = tuple((split_blocks(item) for item in portion))
    result, _ = lax.scan(advance, zeros_init, stacked)
    vsum, mixed, sums = row_totals(result)
    products = (vsum * probe_gain).astype(jnp.bfloat16)
    lscale = loss_gain / math.sqrt(probe_width)
    dfeat = -lscale * inv_length[None, :] * (sums[:, None] * own_wide - mixed)
    dfeat_half = dfeat.astype(jnp.bfloat16)
    second_term = contract_outer(hidden, dfeat_half)
    back_hidden = contract_inner(dfeat_half, w_second)
    sigma = jax.nn.sigmoid(pre)
    dpre = (back_hidden * sigma * (1.0 + pre * (1.0 - sigma))).astype(jnp.bfloat16)
    first_term = contract_outer(inputs, dpre)
    grad_first, grad_second = (
        lax.psum_scatter(first_term, ("enc", "kr", "kc"), scatter_dimension=0, tiled=True),
        lax.psum_scatter(second_term, ("enc", "kr", "kc"), scatter_dimension=0, tiled=True),
    )
    return (products, grad_first, grad_second)


def solution(mesh):
    in_specs = (
        P(("enc", "kr", "kc"), None),
        P(),
        P(),
        P(),
        P(("enc", "kr", "kc"), None),
        P(("enc", "kr", "kc"), None),
    )
    out_specs = (
        P(("enc", "kr", "kc"), None),
        P(("enc", "kr", "kc"), None),
        P(("enc", "kr", "kc"), None),
    )
    return jax.shard_map(local, mesh=mesh, in_specs=in_specs, out_specs=out_specs, check_vma=False)
```

profile of v0, /device:TPU:0, one launch (start us, length us, event | category | flops | bytes accessed | tf_op | source)
XLA Modules:
  0.0 472.0 jit_solution(6461383394210116299)
XLA Ops:
  7.2 0.0 copy-start
  7.2 0.0 reduce-scatter.13.cloned.1.call-start
  7.2 7.2 %all_gather.23 = bf16[768,128]{1,0:T(8,128)(2,1)S(1)} all-gather(bf16[192,128]{1,0:T(8,128)(2,1)} %param.12), channel_id=1, replica_groups=mesh['enc'=4,'kr'=2,'kc'=4] {'kc'}, dimensions={0}, use_global_device_ids=true | all-gather | bytes 245760 | tf_op jit(solution)/shard_map/all_gather | solution.py:67
  14.4 32.0 %all_gather.20 = bf16[1536,128]{1,0:T(8,128)(2,1)S(1)} all-gather(bf16[192,128]{1,0:T(8,128)(2,1)} %param.12), channel_id=1, replica_groups=mesh['enc'=4,'kr'=2,'kc'=4] {'enc','kr'}, dimensions={0}, use_global_device_ids=true | all-gather | bytes 442368 | tf_op jit(solution)/shard_map/all_gather | solution.py:74
  46.4 7.1 %all_gather.21 = bf16[768,128]{1,0:T(8,128)(2,1)} all-gather(bf16[192,128]{1,0:T(8,128)(2,1)} %param.13), channel_id=1, replica_groups=mesh['enc'=4,'kr'=2,'kc'=4] {'kc'}, dimensions={0}, use_global_device_ids=true | all-gather | bytes 245760 | tf_op jit(solution)/shard_map/all_gather | solution.py:68
  53.5 33.5 %all_gather.22 = bf16[1536,128]{1,0:T(8,128)(2,1)} all-gather(bf16[192,128]{1,0:T(8,128)(2,1)} %param.13), channel_id=1, replica_groups=mesh['enc'=4,'kr'=2,'kc'=4] {'enc','kr'}, dimensions={0}, use_global_device_ids=true | all-gather | bytes 442368 | tf_op jit(solution)/shard_map/all_gather | solution.py:75
  87.0 0.0 copy-start.9
  87.0 2.5 multiply_convert_fusion
  89.5 0.7 copy-done.6
  90.3 0.0 copy-done.7
  90.3 0.2 fusion.34
  90.5 5.4 %all-gather = bf16[4,192,64]{1,2,0:T(8,128)(2,1)S(1)} all-gather(bf16[1,192,64]{1,2,0:T(8,128)(2,1)S(1)} %bitcast.84), channel_id=1, replica_groups=mesh['enc'=4,'kr'=2,'kc'=4] {'kc'}, dimensions={0}, use_global_device_ids=true | all-gather | bytes 122880 | tf_op jit(solution)/shard_map/all_gather | solution.py:66
  95.9 0.1 copy.15
  96.0 0.1 reshape.25
  96.2 0.8 copy.18
  97.0 32.9 %all-gather.1 = bf16[8,192,64]{1,2,0:T(8,128)(2,1)} all-gather(bf16[1,192,64]{1,2,0:T(8,128)(2,1)S(1)} %bitcast.85), channel_id=1, replica_groups=mesh['enc'=4,'kr'=2,'kc'=4] {'enc','kr'}, dimensions={0}, use_global_device_ids=true | all-gather | bytes 221184 | tf_op jit(solution)/shard_map/all_gather | solution.py:73
  130.0 1.2 copy.20
  131.2 0.0 copy-start.11
  131.2 11.4 %while.15 = (s32[]{:T(128)}, f32[768,128]{1,0:T(8,128)S(1)}, f32[768,64]{0,1:T(8,128)}, f32[768]{0:T(1024)S(1)}, f32[768]{0:T(1024)S(1)}, /*index=5*/bf16[2,768,...) while((s32[]{:T(128)}, f32[768,128]{1,0:T(8,128)S(1)}, ...), condition=%wide.region_5.6_spmd.clone, body=%wide.region_1.5_spmd.clone.sunk | while | flops 686456832 | bytes 21460252 | solution.py:97
  131.2 0.2 multiply_reduce_fusion.3
  131.4 1.6 fusion.83
  133.0 0.6 convolution_add_fusion.2
  133.6 0.3 copy-done.2
  133.9 0.5 fusion.86
  134.4 0.5 copy-done.5
  134.9 0.5 fusion.84
  135.4 0.4 fusion.85
  135.8 0.0 copy-done.3
  135.8 0.4 fusion.87
  136.2 0.0 copy-start.4
  136.2 0.6 copy-done.4
  136.9 0.2 multiply_reduce_fusion.3
  137.1 1.6 fusion.83
  138.7 0.0 copy-start.2
  138.7 0.6 convolution_add_fusion.2
  139.3 0.3 copy-done.2
  139.6 0.5 fusion.86
  140.1 0.5 copy-done.5
  140.6 0.5 fusion.84
  141.1 0.4 fusion.85
  141.5 0.0 copy-done.3
  141.5 0.4 fusion.87
  141.9 0.6 copy-done.4
  142.6 2.0 copy.21
  144.6 0.0 reduce-scatter.13.cloned.1.call-update
  144.6 0.0 reduce-scatter.9.cloned.1.call-start
  144.7 0.7 reduce-scatter.9.cloned.1.call-update
  145.4 0.0 reduce-scatter.11.cloned.1.call-start
  145.5 0.6 dynamic-slice
  146.7 6.0 %all-reduce = f32[768]{0:T(1024)S(1)} all-reduce(f32[768]{0:T(1024)S(1)} %get-tuple-element.63), channel_id=3, replica_groups=mesh['enc'=4,'kr'=2,'kc'=4] {'kc'}, use_global_device_ids=true, to_apply=%region_7.8.clone | all-reduce | flops 768 | bytes 6144
  152.7 0.1 dynamic-slice.1
  152.7 12.8 %reduce-scatter.13.cloned.1.call-done = f32[192,64]{1,0:T(8,128)} async-done(((f32[768,64]{1,0:T(8,128)}), f32[192,64]{1,0:T(8,128)}) %reduce-scatter.13.cloned.1.call-update) | async-done | bytes 49168
  165.6 1.0 copy.22
  166.5 0.1 multiply_convert_fusion.2
  166.6 2.2 fusion.42
  168.8 0.0 reduce-scatter.11.cloned.1.call-update
  168.8 0.0 reduce-scatter.15.cloned.1.call-start
  168.9 4.1 convolution_bitcast_fusion
  173.0 5.4 %copy.23 = f32[1024,1024]{1,0:T(8,128)} copy(f32[1024,1024]{0,1:T(8,128)} %convolution_bitcast_fusion) | data formatting | bytes 8388608
  178.4 0.0 reduce-scatter.15.cloned.1.call-update
  178.4 10.5 %reduce-scatter.9.cloned.1.call-done = f32[192,128]{1,0:T(8,128)} async-done(((f32[768,128]{1,0:T(8,128)}), f32[192,128]{1,0:T(8,128)}) %reduce-scatter.9.cloned.1.call-update) | async-done | bytes 98320 | tf_op jit(solution)/shard_map/reduce_scatter | solution.py:44
  188.9 1.5 multiply_convert_fusion.1
  190.4 135.4 %reduce-scatter.11.cloned.1.call-done = f32[32,64]{1,0:T(8,128)} async-done(((f32[1024,64]{1,0:T(8,128)}), f32[32,64]{1,0:T(8,128)}) %reduce-scatter.11.cloned.1.call-update) | async-done | bytes 8208 | tf_op jit(solution)/shard_map/reduce_scatter | solution.py:110
  325.8 139.7 %reduce-scatter.15.cloned.1.call-done = f32[32,1024]{1,0:T(8,128)} async-done(((f32[1024,1024]{1,0:T(8,128)}), f32[32,1024]{1,0:T(8,128)}) %reduce-scatter.15.cloned.1.call-update) | async-done | bytes 131088
  (24 shorter events, 0.1 us)
Async XLA Ops:
  7.2 79.8 %copy-start = (bf16[1024,1024]{1,0:T(8,128)(2,1)S(1)}, bf16[1024,1024]{1,0:T(8,128)(2,1)}, u32[]{:S(2)}) copy-start(bf16[1024,1024]{1,0:T(8,128)(2,1)} %param.9) | copy-start | bytes 6291460
  7.2 158.4 %reduce-scatter.13.cloned.1.call-start = ((), (), s32[]{:S(2)}) async-start(), calls=%async_computation.6 | async-start | bytes 491520
  87.0 3.3 copy-start.7
  87.0 3.3 copy-start.9
  89.5 0.7 copy-start.6
  131.2 14.3 %copy-start.11 = (u32[32]{0:T(128)S(1)}, u32[32]{0:T(128)}, u32[]{:S(2)}) copy-start(u32[32]{0:T(128)} %constant.33) | copy-start | bytes 388
  133.0 0.9 copy-start.2
  133.9 1.0 copy-start.5
  134.9 0.9 copy-start.3
  136.2 0.7 copy-start.4
  138.7 0.9 copy-start.2
  139.6 1.0 copy-start.5
  140.6 0.9 copy-start.3
  141.9 0.7 copy-start.4
  142.6 2.1 copy-start.1
  142.6 26.3 %copy-start.8 = (bf16[1024,64]{0,1:T(8,128)(2,1)S(1)}, bf16[1024,64]{0,1:T(8,128)(2,1)}, u32[]{:S(2)}) copy-start(bf16[1024,64]{0,1:T(8,128)(2,1)} %param.10) | copy-start | bytes 393220
  142.6 26.3 %copy-start.10 = (bf16[192,1024]{1,0:T(8,128)(2,1)S(1)}, bf16[192,1024]{1,0:T(8,128)(2,1)}, u32[]{:S(2)}) copy-start(bf16[192,1024]{1,0:T(8,128)(2,1)} %param.8) | copy-start | bytes 1179652
  144.6 44.3 %reduce-scatter.9.cloned.1.call-start = ((), (), s32[]{:S(2)}) async-start(), calls=%async_computation.4 | async-start | bytes 491520 | tf_op jit(solution)/shard_map/reduce_scatter | solution.py:44
  145.4 180.4 %reduce-scatter.11.cloned.1.call-start = ((), (), s32[]{:S(2)}) async-start(), calls=%async_computation.5 | async-start | bytes 540672 | tf_op jit(solution)/shard_map/reduce_scatter | solution.py:110
  168.8 296.7 %reduce-scatter.15.cloned.1.call-start = ((), (), s32[]{:S(2)}) async-start(), calls=%async_computation.7 | async-start | bytes 4325376
Sparse Core Ops, SparseCore 0:
  144.8 20.7 reduce-scatter.12
  168.0 20.8 reduce-scatter.8
  191.7 134.0 reduce-scatter.10
  328.6 136.8 reduce-scatter.14
where the time goes:
time: 473 us; the launch traced here: 472 us
  waiting for transfers between devices  299 us (63%)
  blocking collectives  124 us (26%)
  matrix products  16.9 us (4%)
  local copies, waits for them, and re-layouts  15.1 us (3%)
  between operations  14.5 us (3%)
    unnamed x6, waiting for transfers between devices  153 us
    reduce_scatter x1, waiting for transfers between devices, local(): lax.psum_scatter(second_term, ('enc', 'kr', 'kc'), scatter_dimension=0, t...  135 us
    all_gather x1, blocking collectives, local(): lax.all_gather(solves, ('enc', 'kr'), axis=0, tiled=True)  33.5 us
    all_gather x1, blocking collectives, local(): lax.all_gather(scaled, ('enc', 'kr'), axis=0, tiled=True)  32.9 us
    all_gather x1, blocking collectives, local(): lax.all_gather(probes, ('enc', 'kr'), axis=0, tiled=True)  32 us
    unnamed x24, local copies, waits for them, and re-layouts  12 us
    reduce_scatter x1, waiting for transfers between devices, row_totals(): lax.psum_scatter(parts[0], 'kc', scatter_dimension=0, tiled=True)  10.5 us
  transfers between devices with their start and end apart: 4, of which 4 were waited for; matrix products, arithmetic and copies ran while one was open for 3% of the time, Pallas kernels for 0%

commit v1 on v0

v1 whole, which is shorter than its diff:
```python
import math

import jax
import jax.numpy as jnp
from jax import lax
from jax.experimental import pallas as pl
from jax.experimental.pallas import tpu as pltpu
from jax.sharding import PartitionSpec as P

probe_gain = 0.5
loss_gain = 0.02
F32 = jnp.float32
BF16 = jnp.bfloat16
VMEM_LIMIT = 48 * 1024 * 1024


def dot_nn(left, right):
    return lax.dot_general(left, right, (((1,), (0,)), ((), ())), preferred_element_type=F32)


def dot_nt(left, right):
    return lax.dot_general(left, right, (((1,), (1,)), ((), ())), preferred_element_type=F32)


def swap(x, axis, mask):
    size = lax.axis_size(axis)
    return lax.ppermute(x, axis, [(i, i ^ mask) for i in range(size)])


def gather_direct(x, axis):
    return jnp.concatenate([x] + [swap(x, axis, m) for m in range(1, lax.axis_size(axis))], axis=0)


def gather_double(x, axis):
    mask = lax.axis_size(axis) // 2
    while mask:
        x = jnp.concatenate([x, swap(x, axis, mask)], axis=0)
        mask //= 2
    return x


def pack(x):
    half = x.shape[0] // 2
    return jnp.concatenate([x[:half], x[half:]], axis=1)


def unpack_blocks(packed, rows):
    width = packed.shape[1] // 2
    p = packed.reshape(packed.shape[0] // rows, rows, packed.shape[1])
    u = jnp.concatenate([p[:, :, :width], p[:, :, width:]], axis=1)
    return u.reshape(packed.shape[0] * 2, width)


def whole_specs(n):
    return [pl.BlockSpec(memory_space=pltpu.VMEM)] * n


def encode_body(x_ref, w1_ref, w2_ref, inv_ref, out_ref, acc_ref):
    step = pl.program_id(0)
    pre = dot_nn(x_ref[...], w1_ref[...])
    hidden = (pre * jax.nn.sigmoid(pre)).astype(BF16)
    part = dot_nn(hidden, w2_ref[...])

    @pl.when(step == 0)
    def _():
        acc_ref[...] = part

    @pl.when(step > 0)
    def _():
        acc_ref[...] += part

    @pl.when(step == pl.num_programs(0) - 1)
    def _():
        out_ref[...] = pack((acc_ref[...] * inv_ref[...]).astype(BF16))


def encode(inputs, w_first, w_second, inv_row):
    rows, width = inputs.shape
    hid, feat = w_second.shape
    block = 256
    return pl.pallas_call(
        encode_body,
        grid=(hid // block,),
        in_specs=[
            pl.BlockSpec((rows, width), lambda j: (0, 0)),
            pl.BlockSpec((width, block), lambda j: (0, j)),
            pl.BlockSpec((block, feat), lambda j: (j, 0)),
            pl.BlockSpec((1, feat), lambda j: (0, 0)),
        ],
        out_specs=pl.BlockSpec((rows // 2, 2 * feat), lambda j: (0, 0)),
        out_shape=jax.ShapeDtypeStruct((rows // 2, 2 * feat), BF16),
        scratch_shapes=[pltpu.VMEM((rows, feat), F32)],
        compiler_params=pltpu.CompilerParams(vmem_limit_bytes=VMEM_LIMIT),
        name="encode",
    )(inputs, w_first, w_second, inv_row)


def pair_body(own_rows, rowf_ref, rowp_ref, colf_ref, colp_ref, v_ref, keep_ref, send_ref, rowa, cola, colu, m_acc, s_acc):
    half = own_rows // 2
    probe = v_ref.shape[1]
    ru = unpack_blocks(rowf_ref[...], half)
    rows, feat = ru.shape
    ru32 = ru.astype(F32)
    h = -0.5 * jnp.sum(ru32 * ru32, axis=1, keepdims=True)
    h1 = h.astype(BF16).astype(F32)
    h2 = (h - h1).astype(BF16).astype(F32)
    h3 = h - h1 - h2
    lane = lax.broadcasted_iota(jnp.int32, (rows, feat), 1)
    tail = jnp.where(lane == 0, h1, jnp.where(lane == 1, h2, jnp.where(lane == 2, h3, 0.0)))
    minus = jnp.full((rows, 2 * feat), -0.5, BF16)
    rowa[...] = jnp.concatenate([ru, minus, tail.astype(BF16)], axis=1)

    cu = unpack_blocks(colf_ref[...], half)
    cols = cu.shape[0]
    cu32 = cu.astype(F32)
    sq = cu32 * cu32
    hi = sq.astype(BF16)
    lo = (sq - hi.astype(F32)).astype(BF16)
    clane = lax.broadcasted_iota(jnp.int32, (cols, feat), 1)
    ones = jnp.where(clane < 3, 1.0, 0.0).astype(BF16)
    cola[...] = jnp.concatenate([cu, hi, lo, ones], axis=1)
    colu[...] = cu

    rp = rowp_ref[...]
    rsp = jnp.concatenate([rp[:, probe:], rp[:, :probe]], axis=1)
    v_ref[...] = jnp.zeros(v_ref.shape, F32)
    m_acc[...] = jnp.zeros(m_acc.shape, F32)
    s_acc[...] = jnp.zeros(s_acc.shape, F32)
    tile = 256

    def step(j, carry):
        at = pl.ds(pl.multiple_of(j * tile, tile), tile)
        kern = jnp.exp(dot_nt(rowa[...], cola[at, :]))
        ps = colp_ref[at, :]
        both = kern * dot_nt(rsp, ps)
        s_acc[...] += both[:, : tile // 2] + both[:, tile // 2 :]
        v_ref[...] += dot_nn(kern.astype(BF16), ps[:, :probe])
        m_acc[...] += dot_nn(both.astype(BF16), colu[at, :])
        return carry

    lax.fori_loop(0, cols // tile, step, 0)
    t = jnp.sum(s_acc[...], axis=1, keepdims=True) * ru32 - m_acc[...]
    q = rows // 4
    keep_ref[...] = jnp.concatenate([t[:q], t[q : 2 * q]], axis=1)
    send_ref[...] = jnp.concatenate([t[2 * q : 3 * q], t[3 * q :]], axis=1)


def pairs(own_rows, row_feat, row_probe, col_feat, col_probe):
    rows, cols = row_probe.shape[0], col_probe.shape[0]
    width = row_feat.shape[1]
    probe = row_probe.shape[1] // 2
    feat = width // 2
    out = jax.ShapeDtypeStruct((rows // 4, width), F32)
    return pl.pallas_call(
        lambda *refs: pair_body(own_rows, *refs),
        in_specs=whole_specs(4),
        out_specs=tuple(whole_specs(3)),
        out_shape=(jax.ShapeDtypeStruct((rows, probe), F32), out, out),
        scratch_shapes=[
            pltpu.VMEM((rows, 4 * feat), BF16),
            pltpu.VMEM((cols, 4 * feat), BF16),
            pltpu.VMEM((cols, feat), BF16),
            pltpu.VMEM((rows, feat), F32),
            pltpu.VMEM((rows, 128), F32),
        ],
        compiler_params=pltpu.CompilerParams(vmem_limit_bytes=VMEM_LIMIT),
        cost_estimate=pl.CostEstimate(flops=2 * rows * cols * 640, bytes_accessed=2 * (rows + cols) * 384, transcendentals=rows * cols),
        name="pairs",
    )(row_feat, row_probe, col_feat, col_probe)


def prepare_body(x_ref, w1_ref, sel_ref, slope_ref, xt_ref, ht_ref, xacc, hacc):
    step = pl.program_id(0)
    block = w1_ref.shape[1]
    pre = dot_nn(x_ref[...], w1_ref[...])
    sig = jax.nn.sigmoid(pre)
    hidden = (pre * sig).astype(BF16)
    slope_ref[...] = sig * (1.0 + pre * (1.0 - sig))
    at = pl.ds(pl.multiple_of(step * block, block), block)
    xt = dot_nt(sel_ref[...], x_ref[:, at])
    ht = dot_nt(sel_ref[...], hidden)

    @pl.when(step == 0)
    def _():
        xacc[...] = xt
        hacc[...] = ht

    @pl.when(step > 0)
    def _():
        xacc[...] += xt
        hacc[...] += ht

    @pl.when(step == pl.num_programs(0) - 1)
    def _():
        xt_ref[...] = xacc[...].astype(BF16)
        ht_ref[...] = hacc[...].astype(BF16)


def prepare(x_group, w_first, select):
    rows, width = x_group.shape
    hid = w_first.shape[1]
    mine = select.shape[0]
    block = 256
    return pl.pallas_call(
        prepare_body,
        grid=(hid // block,),
        in_specs=[
            pl.BlockSpec((rows, width), lambda j: (0, 0)),
            pl.BlockSpec((width, block), lambda j: (0, j)),
            pl.BlockSpec((mine, block), lambda j: (0, j)),
        ],
        out_specs=(
            pl.BlockSpec((rows, block), lambda j: (0, j)),
            pl.BlockSpec((mine, rows), lambda j: (0, 0)),
            pl.BlockSpec((mine, rows), lambda j: (0, 0)),
        ),
        out_shape=(
            jax.ShapeDtypeStruct((rows, hid), F32),
            jax.ShapeDtypeStruct((mine, rows), BF16),
            jax.ShapeDtypeStruct((mine, rows), BF16),
        ),
        scratch_shapes=[pltpu.VMEM((mine, rows), F32), pltpu.VMEM((mine, rows), F32)],
        compiler_params=pltpu.CompilerParams(vmem_limit_bytes=VMEM_LIMIT),
        cost_estimate=pl.CostEstimate(flops=2 * rows * width * hid, bytes_accessed=8 * 2**20, transcendentals=rows * hid),
        name="prepare",
    )(x_group, w_first, select)


def grads_body(d_ref, e_ref, w2_ref, slope_ref, xt_ref, ht_ref, out_ref):
    feat = w2_ref.shape[1]
    d, e = d_ref[...], e_ref[...]
    dfeat = jnp.concatenate([d[:, :feat], d[:, feat:], e[:, :feat], e[:, feat:]], axis=0)
    hid = slope_ref.shape[1]
    block = 256
    for j in range(hid // block):
        at = slice(j * block, (j + 1) * block)
        dpre = (dot_nt(dfeat, w2_ref[at, :]) * slope_ref[:, at]).astype(BF16)
        out_ref[:, at] = dot_nn(xt_ref[...], dpre).astype(BF16)
    out_ref[:, hid:] = dot_nn(ht_ref[...], dfeat).astype(BF16)


def grads(d, e, w_second, slope, xt, ht):
    rows, hid = slope.shape
    feat = w_second.shape[1]
    mine = xt.shape[0]
    return pl.pallas_call(
        grads_body,
        in_specs=whole_specs(6),
        out_specs=pl.BlockSpec(memory_space=pltpu.VMEM),
        out_shape=jax.ShapeDtypeStruct((mine, hid + feat), BF16),
        compiler_params=pltpu.CompilerParams(vmem_limit_bytes=VMEM_LIMIT),
        name="grads",
    )(d, e, w_second, slope, xt, ht)


def local(inputs, w_first, w_second, inv_length, probes, solves):
    own_rows, width = inputs.shape
    hid, feat = w_second.shape
    probe_width = probes.shape[1]
    line = lax.axis_size("kc")
    lines = lax.axis_size("enc") * lax.axis_size("kr")
    share = width // (line * lines)
    mine = width // line
    inv_row = inv_length[None, :]

    both = jnp.concatenate([probes, solves], axis=1)
    col_probe = gather_direct(gather_direct(both, "enc"), "kr")
    row_probe = gather_double(both, "kc")
    x_group = gather_double(inputs, "kc")

    scaled = encode(inputs, w_first, w_second, inv_row)
    col_feat = gather_direct(gather_direct(scaled, "enc"), "kr")
    row_feat = gather_double(scaled, "kc")

    at_row = lax.broadcasted_iota(jnp.int32, (mine, width), 0)
    at_col = lax.broadcasted_iota(jnp.int32, (mine, width), 1)
    owner = share * (line * (at_row // share) + lax.axis_index("kc")) + at_row % share
    select = (at_col == owner).astype(BF16)
    slope, xt, ht = prepare(x_group, w_first, select)

    vsum, keep, send = pairs(own_rows, row_feat, row_probe, col_feat, col_probe)
    term = keep + swap(send, "kc", 1)
    far = swap(term, "kc", 2)
    term = term + jnp.concatenate([far[:, feat:], far[:, :feat]], axis=1)
    lscale = loss_gain / math.sqrt(probe_width)
    inv_two = jnp.concatenate([inv_row, inv_row], axis=1)
    dfeat = (-lscale * inv_two * term).astype(BF16)
    other = swap(dfeat, "kc", 1)
    part = grads(dfeat, other, w_second, slope, xt, ht)
    got = lax.all_to_all(part, ("enc", "kr"), 0, 0, tiled=True)
    total = jnp.sum(got.reshape(lines, share, hid + feat).astype(F32), axis=0)

    half = vsum.shape[0] // 2
    v = vsum[:half] + swap(vsum[half:], "kc", 1)
    v = v[:own_rows] + swap(v[own_rows:], "kc", 2)
    products = (v * probe_gain).astype(BF16)
    return products, total[:, :hid], total[:, hid:]


def solution(mesh):
    rows = P(("enc", "kr", "kc"), None)
    return jax.shard_map(
        local,
        mesh=mesh,
        in_specs=(rows, P(), P(), P(), rows, rows),
        out_specs=(rows, rows, rows),
        check_vma=False,
    )
```

time: 473 us -> 88.2 us (0.19)
  waiting for transfers between devices: 299 us -> 35.4 us
  blocking collectives: 124 us -> 0 us
  starting transfers between devices: 0.16 us -> 25.1 us
  matrix products: 16.9 us -> 0 us
  Pallas kernels: 0 us -> 15.7 us
  between operations: 14.5 us -> 0.9 us
  local copies, waits for them, and re-layouts: 15.1 us -> 7.11 us
    unnamed x6 -> x0, waiting for transfers between devices: 153 us -> none
    reduce_scatter x2 -> x0, waiting for transfers between devices: 146 us -> none  [the longest x1 135 us: local(): lax.psum_scatter(second_term, ('enc', 'kr', 'kc'), scatter_dimension=0, t...]
    all_gather x6 -> x0, blocking collectives: 118 us -> none  [the longest x1 33.5 us: local(): lax.all_gather(solves, ('enc', 'kr'), axis=0, tiled=True)]
    ppermute x0 -> x19, waiting for transfers between devices: none -> 26.4 us  [swap(): return lax.ppermute(x, axis, [(i, i ^ mask) for i in range(size)])]
    ppermute x0 -> x19, starting transfers between devices: none -> 19.4 us  [swap(): return lax.ppermute(x, axis, [(i, i ^ mask) for i in range(size)])]
    dot_general x16 -> x0, matrix products: 16.9 us -> none  [the longest x2 6.31 us: contract_outer(): lax.dot_general(left, right, (((0,), (0,)), ((), ())), preferred_element_...]
    pallas_call x0 -> x4, Pallas kernels: none -> 15.7 us  [the longest x1 5.93 us: prepare(): pl.pallas_call(prepare_body, grid=(hid // block,), in_specs=[pl.BlockSpec...]
    all_to_all x0 -> x1, waiting for transfers between devices: none -> 8.97 us  [local(): got = lax.all_to_all(part, ('enc', 'kr'), 0, 0, tiled=True)]
  transfers between devices with their start and end apart: 4 -> 20, of which waited for: 4 -> 10; matrix products, arithmetic and copies ran while one was open for 3% -> 4% of each run, Pallas kernels for 0% -> 12%
where the time goes in v1:
time: 88.2 us; the launch traced here: 87.8 us
  waiting for transfers between devices  35.4 us (40%)
  starting transfers between devices  25.1 us (28%)
  Pallas kernels  15.7 us (18%)
  local copies, waits for them, and re-layouts  7.11 us (8%)
  other arithmetic  3.63 us (4%)
  between operations  0.9 us (1%)
    ppermute x19, waiting for transfers between devices, swap(): return lax.ppermute(x, axis, [(i, i ^ mask) for i in range(size)])  26.4 us
    ppermute x19, starting transfers between devices, swap(): return lax.ppermute(x, axis, [(i, i ^ mask) for i in range(size)])  19.4 us
    all_to_all x1, waiting for transfers between devices, local(): got = lax.all_to_all(part, ('enc', 'kr'), 0, 0, tiled=True)  8.97 us
    pallas_call x1, Pallas kernels, prepare(): pl.pallas_call(prepare_body, grid=(hid // block,), in_specs=[pl.BlockSpec...  5.93 us
    all_to_all x1, starting transfers between devices, local(): got = lax.all_to_all(part, ('enc', 'kr'), 0, 0, tiled=True)  5.71 us
    unnamed x24, local copies, waits for them, and re-layouts  5.69 us
    pallas_call x1, Pallas kernels, pairs(): pl.pallas_call(lambda *refs: pair_body(own_rows, *refs), in_specs=whole_s...  4.63 us
    pallas_call x1, Pallas kernels, encode(): pl.pallas_call(encode_body, grid=(hid // block,), in_specs=[pl.BlockSpec(...  3.14 us
  transfers between devices with their start and end apart: 20, of which 10 were waited for; matrix products, arithmetic and copies ran while one was open for 4% of the time, Pallas kernels for 12%

profile of v1, /device:TPU:0, one launch (start us, length us, event | category | flops | bytes accessed | tf_op | source)
XLA Modules:
  0.0 87.8 jit_solution(1612564857694091126)
XLA Ops:
  0.6 0.0 copy-start.5
  0.6 1.1 %copy.9.w2_ref = bf16[1024,64]{1,0:T(8,128)(2,1)S(1)} copy(bf16[1024,64]{0,1:T(8,128)(2,1)} %param.8) | data formatting | bytes 262144 | tf_op args[2]
  1.7 0.0 copy-start.1
  1.7 1.6 %copy-done.1 = bf16[1024,1024]{1,0:T(8,128)(2,1)S(1)} copy-done((bf16[1024,1024]{1,0:T(8,128)(2,1)S(1)}, bf16[1024,1024]{1,0:T(8,128)(2,1)}, u32[]{:S(2)}) %copy-start.1) | copy-done | bytes 2097176
  3.3 0.7 copy-done.3
  4.0 3.1 %encode.1 = bf16[96,128]{1,0:T(8,128)(2,1)S(1)} custom-call(bf16[192,1024]{1,0:T(8,128)(2,1)} %x_ref.1, bf16[1024,1024]{1,0:T(8,128)(2,1)S(1)} %copy-done.1, bf16[1024,64]{1,0:T(8,128)(2,1)S(1)} %copy.9.w2_ref, f32[1,64]{1,0:T(1,128)S(1)} %bitcast.2), custom_call_target="tpu_custom_call" | custom-call | tf_op jit(solution)/shard_map/encode/pallas_call | solution.py:81
  7.1 5.1 %collective-permute-start.6 = (bf16[96,128]{1,0:T(8,128)(2,1)S(1)}, bf16[96,128]{1,0:T(8,128)(2,1)S(1)}, u32[]{:S(2)}, u32[]{:S(2)}) collective-permute-start(bf16[96,128]{1,0:T(8,128)(2,1)S(1)} %encode.1), channel_id=1, source_target_pairs={{0,24},{8,16},{16,8},{24,0},{1,25},{9,17},{17,9},{25,1},{2,26},{10... | collective-permute-start | bytes 73736 | tf_op jit(solution)/shard_map/ppermute | solution.py:27
  12.2 0.0 collective-permute-start.5
  12.2 0.6 collective-permute-start.4
  12.9 1.6 %collective-permute-start = (bf16[96,128]{1,0:T(8,128)(2,1)S(1)}, bf16[96,128]{1,0:T(8,128)(2,1)S(1)}, u32[]{:S(2)}, u32[]{:S(2)}) collective-permute-start(bf16[96,128]{1,0:T(8,128)(2,1)S(1)} %encode.1), channel_id=1, source_target_pairs={{0,2},{1,3},{2,0},{3,1},{4,6},{5,7},{6,4},{7,5},{8,10},{9,11},{10,... | collective-permute-start | bytes 73736 | tf_op jit(solution)/shard_map/ppermute | solution.py:27
  14.5 0.4 collective-permute-start.17
  15.0 2.0 %collective-permute-done = bf16[96,128]{1,0:T(8,128)(2,1)S(1)} collective-permute-done((bf16[96,128]{1,0:T(8,128)(2,1)S(1)}, bf16[96,128]{1,0:T(8,128)(2,1)S(1)}, u32[]{:S(2)}, u32[]{:S(2)}) %collective-permute-start) | collective-permute-done | bytes 24608 | tf_op jit(solution)/shard_map/ppermute | solution.py:27
  16.9 3.7 %collective-permute-start.10 = (bf16[192,256]{1,0:T(8,128)(2,1)S(1)}, bf16[192,256]{1,0:T(8,128)(2,1)S(1)}, u32[]{:S(2)}, u32[]{:S(2)}) collective-permute-start(bf16[192,256]{1,0:T(8,128)(2,1)S(1)} %get-tuple-element.20), channel_id=1, source_target_pairs={{0,24},{8,16},{16,8},{24,0},{1,25},{9,17},{17,9},{25,1},{2,26},{10... | collective-permute-start | bytes 294920 | tf_op jit(solution)/shard_map/ppermute | solution.py:27
  20.6 0.0 collective-permute-done.4
  20.6 0.1 collective-permute-start.9
  20.7 0.0 collective-permute-done.5
  20.7 0.7 collective-permute-start.8
  21.5 0.0 collective-permute-done.6
  21.5 1.8 %collective-permute-start.2 = (bf16[192,256]{1,0:T(8,128)(2,1)S(1)}, bf16[192,256]{1,0:T(8,128)(2,1)S(1)}, u32[]{:S(2)}, u32[]{:S(2)}) collective-permute-start(bf16[192,256]{1,0:T(8,128)(2,1)S(1)} %get-tuple-element.20), channel_id=1, source_target_pairs={{0,2},{1,3},{2,0},{3,1},{4,6},{5,7},{6,4},{7,5},{8,10},{9,11},{10,... | collective-permute-start | bytes 294920 | tf_op jit(solution)/shard_map/ppermute | solution.py:27
  23.3 3.7 %collective-permute-done.2 = bf16[192,256]{1,0:T(8,128)(2,1)S(1)} collective-permute-done((bf16[192,256]{1,0:T(8,128)(2,1)S(1)}, bf16[192,256]{1,0:T(8,128)(2,1)S(1)}, u32[]{:S(2)}, u32[]{:S(2)}) %collective-permute-start.2) | collective-permute-done | bytes 98336 | tf_op jit(solution)/shard_map/ppermute | solution.py:27
  26.9 0.0 collective-permute-start.1
  27.0 1.2 %collective-permute-done.1 = bf16[192,128]{1,0:T(8,128)(2,1)S(1)} collective-permute-done((bf16[192,128]{1,0:T(8,128)(2,1)S(1)}, bf16[192,128]{1,0:T(8,128)(2,1)S(1)}, u32[]{:S(2)}, u32[]{:S(2)}) %collective-permute-start.1) | collective-permute-done | bytes 49184 | tf_op jit(solution)/shard_map/ppermute | solution.py:27
  28.2 0.2 collective-permute-start.3
  28.4 0.0 collective-permute-done.8
  28.4 1.6 %collective-permute-start.7 = (bf16[384,128]{1,0:T(8,128)(2,1)S(1)}, bf16[384,128]{1,0:T(8,128)(2,1)S(1)}, u32[]{:S(2)}, u32[]{:S(2)}) collective-permute-start(bf16[384,128]{1,0:T(8,128)(2,1)S(1)} %get-tuple-element.23), channel_id=1, source_target_pairs={{0,4},{4,0},{1,5},{5,1},{2,6},{6,2},{3,7},{7,3},{8,12},{12,8},{9,1... | collective-permute-start | bytes 294920 | tf_op jit(solution)/shard_map/ppermute | solution.py:27
  30.0 0.0 collective-permute-done.10
  30.0 0.0 collective-permute-done.9
  30.0 0.0 collective-permute-done.3
  30.0 0.1 fusion.3
  30.1 1.2 %collective-permute-start.11 = (bf16[768,256]{1,0:T(8,128)(2,1)S(1)}, bf16[768,256]{1,0:T(8,128)(2,1)S(1)}, u32[]{:S(2)}, u32[]{:S(2)}) collective-permute-start(bf16[768,256]{1,0:T(8,128)(2,1)S(1)} %get-tuple-element.17), channel_id=1, source_target_pairs={{0,4},{4,0},{1,5},{5,1},{2,6},{6,2},{3,7},{7,3},{8,12},{12,8},{9,1... | collective-permute-start | bytes 1179656 | tf_op jit(solution)/shard_map/ppermute | solution.py:27
  31.3 2.8 %collective-permute-done.7 = bf16[384,128]{1,0:T(8,128)(2,1)S(1)} collective-permute-done((bf16[384,128]{1,0:T(8,128)(2,1)S(1)}, bf16[384,128]{1,0:T(8,128)(2,1)S(1)}, u32[]{:S(2)}, u32[]{:S(2)}) %collective-permute-start.7) | collective-permute-done | bytes 98336 | tf_op jit(solution)/shard_map/ppermute | solution.py:27
  34.1 0.0 collective-permute-done.17
  34.1 1.1 %pad_maximum_fusion.1 = bf16[384,1024]{1,0:T(8,128)(2,1)S(1)} fusion(bf16[192,1024]{1,0:T(8,128)(2,1)S(1)} %collective-permute-done.17, bf16[192,1024]{1,0:T(8,128)(2,1)} %x_ref.1), kind=kLoop, calls=%fused_computation.4 | loop fusion | flops 1572864 | bytes 1572864 | tf_op jit(solution)/shard_map/concatenate | solution.py:37
  35.1 0.1 collective-permute-start.18
  35.2 6.7 %collective-permute-done.11 = bf16[768,256]{1,0:T(8,128)(2,1)S(1)} collective-permute-done((bf16[768,256]{1,0:T(8,128)(2,1)S(1)}, bf16[768,256]{1,0:T(8,128)(2,1)S(1)}, u32[]{:S(2)}, u32[]{:S(2)}) %collective-permute-start.11) | collective-permute-done | bytes 393248 | tf_op jit(solution)/shard_map/ppermute | solution.py:27
  41.9 0.0 copy-start.4
  42.0 4.6 %pairs.1 = (f32[768,128]{1,0:T(8,128)S(1)}, f32[192,128]{1,0:T(8,128)S(1)}, f32[192,128]{1,0:T(8,128)S(1)}) custom-call(bf16[384,128]{1,0:T(8,128)(2,1)S(1)} %get-tuple-element.24.refs_0_, bf16[768,256]{1,0:T(8,128)(2,1)S(1)} %get-tuple-element.18.refs_1_, bf16[768,128]{1,0:T(8,128)(2,1)S(1)} %constant_dynamic-update-slice_fusion.2.refs_2_, ...), custom_call_target="tpu_custom_call" | custom-call | flops 1509949440 | bytes 1769472 | tf_op jit(solution)/shard_map/pairs/pallas_call | solution.py:154
  46.6 0.1 collective-permute-start.14
  46.7 0.3 fusion.sel_ref
  47.0 1.0 %collective-permute-done.14 = f32[192,128]{1,0:T(8,128)S(1)} collective-permute-done((f32[192,128]{1,0:T(8,128)S(1)}, f32[192,128]{1,0:T(8,128)S(1)}, u32[]{:S(2)}, u32[]{:S(2)}) %collective-permute-start.14) | collective-permute-done | bytes 98336 | tf_op jit(solution)/shard_map/ppermute | solution.py:27
  48.0 1.0 %collective-permute-start.15 = (f32[192,128]{1,0:T(8,128)S(1)}, f32[192,128]{1,0:T(8,128)S(1)}, u32[]{:S(2)}, u32[]{:S(2)}) collective-permute-start(f32[192,128]{1,0:T(8,128)S(1)} %add.32), channel_id=1, source_target_pairs={{0,2},{1,3},{2,0},{3,1},{4,6},{5,7},{6,4},{7,5},{8,10},{9,11},{10,... | collective-permute-start | bytes 294920 | tf_op jit(solution)/shard_map/ppermute | solution.py:27
  49.0 0.1 maximum_multiply_fusion
  49.0 3.9 %collective-permute-done.15 = f32[192,128]{1,0:T(8,128)S(1)} collective-permute-done((f32[192,128]{1,0:T(8,128)S(1)}, f32[192,128]{1,0:T(8,128)S(1)}, u32[]{:S(2)}, u32[]{:S(2)}) %collective-permute-start.15) | collective-permute-done | bytes 98336 | tf_op jit(solution)/shard_map/ppermute | solution.py:27
  52.9 0.1 fusion.13
  53.0 0.1 fusion.10.d_ref
  53.1 0.0 copy-start.2
  53.1 0.1 collective-permute-start.16
  53.2 0.0 collective-permute-done.18
  53.2 1.2 %pad_maximum_fusion.x_ref = bf16[768,1024]{1,0:T(8,128)(2,1)S(1)} fusion(bf16[384,1024]{1,0:T(8,128)(2,1)S(1)} %collective-permute-done.18, bf16[192,1024]{1,0:T(8,128)(2,1)S(1)} %collective-permute-done.17, bf16[192,1024]{1,0:T(8,128)(2,1)} %x_ref.1), kind=kLoop, calls=%fused_computation | loop fusion | flops 4718592 | bytes 3145728 | tf_op jit(solution)/shard_map/concatenate | solution.py:37
  54.4 0.4 copy-done.2
  54.8 5.9 %prepare.1 = (f32[768,1024]{1,0:T(8,128)}, bf16[256,768]{1,0:T(8,128)(2,1)S(1)}, bf16[256,768]{1,0:T(8,128)(2,1)S(1)}) custom-call(bf16[768,1024]{1,0:T(8,128)(2,1)S(1)} %pad_maximum_fusion.x_ref, bf16[1024,1024]{1,0:T(8,128)(2,1)S(1)} %copy-done.2, bf16[256,1024]{1,0:T(8,128)(2,1)S(1)} %fusion.sel_ref), custom_call_target="tpu_custom_call" | custom-call | flops 1610612736 | bytes 8388608 | tf_op jit(solution)/shard_map/prepare/pallas_call | solution.py:204
  60.7 0.0 collective-permute-done.16.e_ref
  60.7 1.9 %copy-done = f32[768,1024]{1,0:T(8,128)S(1)} copy-done((f32[768,1024]{1,0:T(8,128)S(1)}, f32[768,1024]{1,0:T(8,128)}, u32[]{:S(2)}) %copy-start) | copy-done | bytes 3145752
  62.6 2.0 %grads.1 = bf16[256,1088]{1,0:T(8,128)(2,1)} custom-call(bf16[192,128]{1,0:T(8,128)(2,1)S(1)} %fusion.10.d_ref, bf16[192,128]{1,0:T(8,128)(2,1)S(1)} %collective-permute-done.16.e_ref, bf16[1024,64]{1,0:T(8,128)(2,1)S(1)} %copy.9.w2_ref, f32[768,1024]{1,0:T(8,128)S(1)} %copy-done, bf16[256,768]{1,0:T(8,128)(2,1)S(1)} %get-tuple-element.13.xt_ref, ...), custom_call_target="tpu_custom_call" | custom-call | tf_op jit(solution)/shard_map/grads/pallas_call | solution.py:246
  64.7 5.7 %all-to-all-start = ((bf16[8,32,1088]{2,1,0:T(8,128)(2,1)}), bf16[8,32,1088]{2,1,0:T(8,128)(2,1)S(1)}, u32[]{:S(2)}, u32[]{:S(2)}) async-start(bf16[8,32,1088]{2,1,0:T(8,128)(2,1)} %bitcast.1), calls=%async_computation | async-start | bytes 1179648 | tf_op jit(solution)/shard_map/all_to_all | solution.py:290
  70.4 0.1 collective-permute-start.12
  70.5 1.4 %collective-permute-done.12 = f32[384,128]{1,0:T(8,128)S(1)} collective-permute-done((f32[384,128]{1,0:T(8,128)S(1)}, f32[384,128]{1,0:T(8,128)S(1)}, u32[]{:S(2)}, u32[]{:S(2)}) %collective-permute-start.12) | collective-permute-done | bytes 196640 | tf_op jit(solution)/shard_map/ppermute | solution.py:27
  71.9 1.1 %collective-permute-start.13 = (f32[192,128]{1,0:T(8,128)S(1)}, f32[192,128]{1,0:T(8,128)S(1)}, u32[]{:S(2)}, u32[]{:S(2)}) collective-permute-start(f32[192,128]{1,0:T(8,128)S(1)} %slice.33), channel_id=1, source_target_pairs={{0,2},{1,3},{2,0},{3,1},{4,6},{5,7},{6,4},{7,5},{8,10},{9,11},{10,... | collective-permute-start | bytes 294920 | tf_op jit(solution)/shard_map/ppermute | solution.py:27
  73.1 3.8 %collective-permute-done.13 = f32[192,128]{1,0:T(8,128)S(1)} collective-permute-done((f32[192,128]{1,0:T(8,128)S(1)}, f32[192,128]{1,0:T(8,128)S(1)}, u32[]{:S(2)}, u32[]{:S(2)}) %collective-permute-start.13) | collective-permute-done | bytes 98336 | tf_op jit(solution)/shard_map/ppermute | solution.py:27
  76.9 0.6 fusion.8
  77.5 9.0 %all-to-all-done = bf16[8,32,1088]{2,1,0:T(8,128)(2,1)S(1)} async-done(((bf16[8,32,1088]{2,1,0:T(8,128)(2,1)}), bf16[8,32,1088]{2,1,0:T(8,128)(2,1)S(1)}, u32[]{:S(2)}, u32[]{:S(2)}) %all-to-all-start) | async-done | bytes 557088 | tf_op jit(solution)/shard_map/all_to_all | solution.py:290
  86.5 0.1 convert_reduce_fusion
  86.5 0.6 slice.37
  87.2 0.7 slice.36
  (27 shorter events, 0.3 us)
Async XLA Ops:
  0.6 14.3 %copy-start.5 = (bf16[192,128]{1,0:T(8,128)(2,1)S(1)}, bf16[192,128]{1,0:T(8,128)(2,1)}, u32[]{:S(2)}) copy-start(bf16[192,128]{1,0:T(8,128)(2,1)} %param.10) | copy-start | bytes 147460
  1.7 1.6 %copy-start.1 = (bf16[1024,1024]{1,0:T(8,128)(2,1)S(1)}, bf16[1024,1024]{1,0:T(8,128)(2,1)}, u32[]{:S(2)}) copy-start(bf16[1024,1024]{1,0:T(8,128)(2,1)} %w1_ref.3) | copy-start | bytes 6291460
  3.3 0.7 copy-start.3
  4.0 11.0 %copy-start.6 = (bf16[192,128]{1,0:T(8,128)(2,1)S(1)}, bf16[192,128]{1,0:T(8,128)(2,1)}, u32[]{:S(2)}) copy-start(bf16[192,128]{1,0:T(8,128)(2,1)} %param.11) | copy-start | bytes 147460
  7.1 14.4 %collective-permute-start.6 = (bf16[96,128]{1,0:T(8,128)(2,1)S(1)}, bf16[96,128]{1,0:T(8,128)(2,1)S(1)}, u32[]{:S(2)}, u32[]{:S(2)}) collective-permute-start(bf16[96,128]{1,0:T(8,128)(2,1)S(1)} %encode.1), channel_id=1, source_target_pairs={{0,24},{8,16},{16,8},{24,0},{1,25},{9,17},{17,9},{25,1},{2,26},{10... | collective-permute-start | bytes 73736 | tf_op jit(solution)/shard_map/ppermute | solution.py:27
  12.2 8.5 %collective-permute-start.5 = (bf16[96,128]{1,0:T(8,128)(2,1)S(1)}, bf16[96,128]{1,0:T(8,128)(2,1)S(1)}, u32[]{:S(2)}, u32[]{:S(2)}) collective-permute-start(bf16[96,128]{1,0:T(8,128)(2,1)S(1)} %encode.1), channel_id=1, source_target_pairs={{0,16},{8,24},{16,0},{24,8},{1,17},{9,25},{17,1},{25,9},{2,18},{10... | collective-permute-start | bytes 73736 | tf_op jit(solution)/shard_map/ppermute | solution.py:27
  12.2 8.4 %collective-permute-start.4 = (bf16[96,128]{1,0:T(8,128)(2,1)S(1)}, bf16[96,128]{1,0:T(8,128)(2,1)S(1)}, u32[]{:S(2)}, u32[]{:S(2)}) collective-permute-start(bf16[96,128]{1,0:T(8,128)(2,1)S(1)} %encode.1), channel_id=1, source_target_pairs={{0,8},{8,0},{16,24},{24,16},{1,9},{9,1},{17,25},{25,17},{2,10},{10... | collective-permute-start | bytes 73736 | tf_op jit(solution)/shard_map/ppermute | solution.py:27
  12.9 4.1 %collective-permute-start = (bf16[96,128]{1,0:T(8,128)(2,1)S(1)}, bf16[96,128]{1,0:T(8,128)(2,1)S(1)}, u32[]{:S(2)}, u32[]{:S(2)}) collective-permute-start(bf16[96,128]{1,0:T(8,128)(2,1)S(1)} %encode.1), channel_id=1, source_target_pairs={{0,2},{1,3},{2,0},{3,1},{4,6},{5,7},{6,4},{7,5},{8,10},{9,11},{10,... | collective-permute-start | bytes 73736 | tf_op jit(solution)/shard_map/ppermute | solution.py:27
  14.5 19.6 %collective-permute-start.17 = (bf16[192,1024]{1,0:T(8,128)(2,1)}, bf16[192,1024]{1,0:T(8,128)(2,1)S(1)}, u32[]{:S(2)}, u32[]{:S(2)}) collective-permute-start(bf16[192,1024]{1,0:T(8,128)(2,1)} %x_ref.1), channel_id=1, source_target_pairs={{0,2},{1,3},{2,0},{3,1},{4,6},{5,7},{6,4},{7,5},{8,10},{9,11},{10,... | collective-permute-start | bytes 1179656 | tf_op jit(solution)/shard_map/ppermute | solution.py:27
  16.9 13.0 %collective-permute-start.10 = (bf16[192,256]{1,0:T(8,128)(2,1)S(1)}, bf16[192,256]{1,0:T(8,128)(2,1)S(1)}, u32[]{:S(2)}, u32[]{:S(2)}) collective-permute-start(bf16[192,256]{1,0:T(8,128)(2,1)S(1)} %get-tuple-element.20), channel_id=1, source_target_pairs={{0,24},{8,16},{16,8},{24,0},{1,25},{9,17},{17,9},{25,1},{2,26},{10... | collective-permute-start | bytes 294920 | tf_op jit(solution)/shard_map/ppermute | solution.py:27
  20.6 9.3 %collective-permute-start.9 = (bf16[192,256]{1,0:T(8,128)(2,1)S(1)}, bf16[192,256]{1,0:T(8,128)(2,1)S(1)}, u32[]{:S(2)}, u32[]{:S(2)}) collective-permute-start(bf16[192,256]{1,0:T(8,128)(2,1)S(1)} %get-tuple-element.20), channel_id=1, source_target_pairs={{0,16},{8,24},{16,0},{24,8},{1,17},{9,25},{17,1},{25,9},{2,18},{10... | collective-permute-start | bytes 294920 | tf_op jit(solution)/shard_map/ppermute | solution.py:27
  20.7 7.6 %collective-permute-start.8 = (bf16[192,256]{1,0:T(8,128)(2,1)S(1)}, bf16[192,256]{1,0:T(8,128)(2,1)S(1)}, u32[]{:S(2)}, u32[]{:S(2)}) collective-permute-start(bf16[192,256]{1,0:T(8,128)(2,1)S(1)} %get-tuple-element.20), channel_id=1, source_target_pairs={{0,8},{8,0},{16,24},{24,16},{1,9},{9,1},{17,25},{25,17},{2,10},{10... | collective-permute-start | bytes 294920 | tf_op jit(solution)/shard_map/ppermute | solution.py:27
  21.5 5.5 %collective-permute-start.2 = (bf16[192,256]{1,0:T(8,128)(2,1)S(1)}, bf16[192,256]{1,0:T(8,128)(2,1)S(1)}, u32[]{:S(2)}, u32[]{:S(2)}) collective-permute-start(bf16[192,256]{1,0:T(8,128)(2,1)S(1)} %get-tuple-element.20), channel_id=1, source_target_pairs={{0,2},{1,3},{2,0},{3,1},{4,6},{5,7},{6,4},{7,5},{8,10},{9,11},{10,... | collective-permute-start | bytes 294920 | tf_op jit(solution)/shard_map/ppermute | solution.py:27
  26.9 1.2 %collective-permute-start.1 = (bf16[192,128]{1,0:T(8,128)(2,1)S(1)}, bf16[192,128]{1,0:T(8,128)(2,1)S(1)}, u32[]{:S(2)}, u32[]{:S(2)}) collective-permute-start(bf16[192,128]{1,0:T(8,128)(2,1)S(1)} %pad_maximum_fusion.7), channel_id=1, source_target_pairs={{0,1},{1,0},{2,3},{3,2},{4,5},{5,4},{6,7},{7,6},{8,9},{9,8},{10,11... | collective-permute-start | bytes 147464 | tf_op jit(solution)/shard_map/ppermute | solution.py:27
  28.2 1.8 %collective-permute-start.3 = (bf16[384,256]{1,0:T(8,128)(2,1)S(1)}, bf16[384,256]{1,0:T(8,128)(2,1)S(1)}, u32[]{:S(2)}, u32[]{:S(2)}) collective-permute-start(bf16[384,256]{1,0:T(8,128)(2,1)S(1)} %pad_maximum_fusion.4), channel_id=1, source_target_pairs={{0,1},{1,0},{2,3},{3,2},{4,5},{5,4},{6,7},{7,6},{8,9},{9,8},{10,11... | collective-permute-start | bytes 589832 | tf_op jit(solution)/shard_map/ppermute | solution.py:27
  28.4 5.7 %collective-permute-start.7 = (bf16[384,128]{1,0:T(8,128)(2,1)S(1)}, bf16[384,128]{1,0:T(8,128)(2,1)S(1)}, u32[]{:S(2)}, u32[]{:S(2)}) collective-permute-start(bf16[384,128]{1,0:T(8,128)(2,1)S(1)} %get-tuple-element.23), channel_id=1, source_target_pairs={{0,4},{4,0},{1,5},{5,1},{2,6},{6,2},{3,7},{7,3},{8,12},{12,8},{9,1... | collective-permute-start | bytes 294920 | tf_op jit(solution)/shard_map/ppermute | solution.py:27
  30.1 11.9 %collective-permute-start.11 = (bf16[768,256]{1,0:T(8,128)(2,1)S(1)}, bf16[768,256]{1,0:T(8,128)(2,1)S(1)}, u32[]{:S(2)}, u32[]{:S(2)}) collective-permute-start(bf16[768,256]{1,0:T(8,128)(2,1)S(1)} %get-tuple-element.17), channel_id=1, source_target_pairs={{0,4},{4,0},{1,5},{5,1},{2,6},{6,2},{3,7},{7,3},{8,12},{12,8},{9,1... | collective-permute-start | bytes 1179656 | tf_op jit(solution)/shard_map/ppermute | solution.py:27
  35.1 18.1 %collective-permute-start.18 = (bf16[384,1024]{1,0:T(8,128)(2,1)S(1)}, bf16[384,1024]{1,0:T(8,128)(2,1)S(1)}, u32[]{:S(2)}, u32[]{:S(2)}) collective-permute-start(bf16[384,1024]{1,0:T(8,128)(2,1)S(1)} %pad_maximum_fusion.1), channel_id=1, source_target_pairs={{0,1},{1,0},{2,3},{3,2},{4,5},{5,4},{6,7},{7,6},{8,9},{9,8},{10,11... | collective-permute-start | bytes 2359304 | tf_op jit(solution)/shard_map/ppermute | solution.py:27
  41.9 7.0 %copy-start.4 = (f32[64]{0:T(128)S(1)}, f32[64]{0:T(128)}, u32[]{:S(2)}) copy-start(f32[64]{0:T(128)} %param.9) | copy-start | bytes 772
  46.6 1.4 %collective-permute-start.14 = (f32[192,128]{1,0:T(8,128)S(1)}, f32[192,128]{1,0:T(8,128)S(1)}, u32[]{:S(2)}, u32[]{:S(2)}) collective-permute-start(f32[192,128]{1,0:T(8,128)S(1)} %get-tuple-element.11), channel_id=1, source_target_pairs={{0,1},{1,0},{2,3},{3,2},{4,5},{5,4},{6,7},{7,6},{8,9},{9,8},{10,11... | collective-permute-start | bytes 294920 | tf_op jit(solution)/shard_map/ppermute | solution.py:27
  48.0 4.9 %collective-permute-start.15 = (f32[192,128]{1,0:T(8,128)S(1)}, f32[192,128]{1,0:T(8,128)S(1)}, u32[]{:S(2)}, u32[]{:S(2)}) collective-permute-start(f32[192,128]{1,0:T(8,128)S(1)} %add.32), channel_id=1, source_target_pairs={{0,2},{1,3},{2,0},{3,1},{4,6},{5,7},{6,4},{7,5},{8,10},{9,11},{10,... | collective-permute-start | bytes 294920 | tf_op jit(solution)/shard_map/ppermute | solution.py:27
  53.1 1.7 %copy-start.2 = (bf16[1024,1024]{1,0:T(8,128)(2,1)S(1)}, bf16[1024,1024]{1,0:T(8,128)(2,1)}, u32[]{:S(2)}) copy-start(bf16[1024,1024]{1,0:T(8,128)(2,1)} %w1_ref.3) | copy-start | bytes 6291460
  53.1 7.6 %collective-permute-start.16 = (bf16[192,128]{1,0:T(8,128)(2,1)S(1)}, bf16[192,128]{1,0:T(8,128)(2,1)S(1)}, u32[]{:S(2)}, u32[]{:S(2)}) collective-permute-start(bf16[192,128]{1,0:T(8,128)(2,1)S(1)} %fusion.10.d_ref), channel_id=1, source_target_pairs={{0,1},{1,0},{2,3},{3,2},{4,5},{5,4},{6,7},{7,6},{8,9},{9,8},{10,11... | collective-permute-start | bytes 147464 | tf_op jit(solution)/shard_map/ppermute | solution.py:27
  60.7 1.9 %copy-start = (f32[768,1024]{1,0:T(8,128)S(1)}, f32[768,1024]{1,0:T(8,128)}, u32[]{:S(2)}) copy-start(f32[768,1024]{1,0:T(8,128)} %get-tuple-element.12.slope_ref) | copy-start | bytes 9437188
  64.7 21.8 %all-to-all-start = ((bf16[8,32,1088]{2,1,0:T(8,128)(2,1)}), bf16[8,32,1088]{2,1,0:T(8,128)(2,1)S(1)}, u32[]{:S(2)}, u32[]{:S(2)}) async-start(bf16[8,32,1088]{2,1,0:T(8,128)(2,1)} %bitcast.1), calls=%async_computation | async-start | bytes 1179648 | tf_op jit(solution)/shard_map/all_to_all | solution.py:290
  70.4 1.5 %collective-permute-start.12 = (f32[384,128]{1,0:T(8,128)S(1)}, f32[384,128]{1,0:T(8,128)S(1)}, u32[]{:S(2)}, u32[]{:S(2)}) collective-permute-start(f32[384,128]{1,0:T(8,128)S(1)} %slice.25), channel_id=1, source_target_pairs={{0,1},{1,0},{2,3},{3,2},{4,5},{5,4},{6,7},{7,6},{8,9},{9,8},{10,11... | collective-permute-start | bytes 589832 | tf_op jit(solution)/shard_map/ppermute | solution.py:27
  71.9 4.9 %collective-permute-start.13 = (f32[192,128]{1,0:T(8,128)S(1)}, f32[192,128]{1,0:T(8,128)S(1)}, u32[]{:S(2)}, u32[]{:S(2)}) collective-permute-start(f32[192,128]{1,0:T(8,128)S(1)} %slice.33), channel_id=1, source_target_pairs={{0,2},{1,3},{2,0},{3,1},{4,6},{5,7},{6,4},{7,5},{8,10},{9,11},{10,... | collective-permute-start | bytes 294920 | tf_op jit(solution)/shard_map/ppermute | solution.py:27

commit v2 on v0

v2 whole, which is shorter than its diff:
```python
import math

import jax
import jax.numpy as jnp
from jax import lax
from jax.experimental import pallas as pl
from jax.experimental.pallas import tpu as pltpu
from jax.sharding import PartitionSpec as P

probe_gain = 0.5
loss_gain = 0.02
F32 = jnp.float32
BF16 = jnp.bfloat16
VMEM_LIMIT = 48 * 1024 * 1024
VMEM_MOST = 60 * 1024 * 1024
VMEM = pl.BlockSpec(memory_space=pltpu.VMEM)
HBM = pl.BlockSpec(memory_space=pltpu.HBM)
ANY = pl.BlockSpec(memory_space=pl.ANY)


def dot_nn(left, right):
    return lax.dot_general(left, right, (((1,), (0,)), ((), ())), preferred_element_type=F32)


def dot_nt(left, right):
    return lax.dot_general(left, right, (((1,), (1,)), ((), ())), preferred_element_type=F32)


def swap(x, axis, mask):
    size = lax.axis_size(axis)
    return lax.ppermute(x, axis, [(i, i ^ mask) for i in range(size)])


def swap_both(x, deep_mask, tall_mask):
    deep, tall = lax.axis_size("enc"), lax.axis_size("kr")
    pairs_of = [(i, ((i // tall) ^ deep_mask) * tall + ((i % tall) ^ tall_mask)) for i in range(deep * tall)]
    return lax.ppermute(x, ("enc", "kr"), pairs_of)


def params(limit=VMEM_LIMIT):
    return pltpu.CompilerParams(vmem_limit_bytes=limit)


def encode_body(x_hbm, w1_hbm, w2t_hbm, inv_hbm, probe_hbm, solve_hbm, out_ref, x_ref, w1_ref, w2t_ref, inv_ref, sems):
    rows, width = x_ref.shape
    hid = w1_ref.shape[1]
    parts = 4
    block = hid // parts
    x_copy = pltpu.make_async_copy(x_hbm, x_ref, sems.at[0])
    w2_copy = pltpu.make_async_copy(w2t_hbm, w2t_ref, sems.at[1])
    probe_copy = pltpu.make_async_copy(probe_hbm, out_ref.at[pl.ds(0, rows), :], sems.at[2])
    solve_copy = pltpu.make_async_copy(solve_hbm, out_ref.at[pl.ds(rows, rows), :], sems.at[3])
    w1_copies = [
        pltpu.make_async_copy(w1_hbm.at[:, pl.ds(j * block, block)], w1_ref.at[:, pl.ds(j * block, block)], sems.at[4 + j])
        for j in range(parts)
    ]
    x_copy.start()
    w1_copies[0].start()
    w2_copy.start()
    for copy in w1_copies[1:]:
        copy.start()
    inv_copy = pltpu.make_async_copy(inv_hbm, inv_ref, sems.at[8])
    inv_copy.start()
    probe_copy.start()
    solve_copy.start()
    x_copy.wait()
    acc = None
    for j in range(parts):
        at = slice(j * block, (j + 1) * block)
        w1_copies[j].wait()
        pre = dot_nn(x_ref[...], w1_ref[:, at])
        hidden = (pre * jax.nn.sigmoid(pre)).astype(BF16)
        if j == 0:
            w2_copy.wait()
        part = dot_nt(hidden, w2t_ref[:, at])
        acc = part if acc is None else acc + part
    inv_copy.wait()
    scaled = (acc * inv_ref[...]).astype(BF16)
    out_ref[2 * rows :, :] = jnp.concatenate([scaled[: rows // 2], scaled[rows // 2 :]], axis=1)
    probe_copy.wait()
    solve_copy.wait()


def encode(inputs, w_first, w2t, inv_row, probes, solves):
    rows = inputs.shape[0]
    return pl.pallas_call(
        encode_body,
        in_specs=[HBM] * 6,
        out_specs=VMEM,
        out_shape=jax.ShapeDtypeStruct((2 * rows + rows // 2, probes.shape[1]), BF16),
        scratch_shapes=[
            pltpu.VMEM(inputs.shape, BF16),
            pltpu.VMEM(w_first.shape, BF16),
            pltpu.VMEM(w2t.shape, BF16),
            pltpu.VMEM(inv_row.shape, F32),
            pltpu.SemaphoreType.DMA((9,)),
        ],
        compiler_params=params(VMEM_MOST),
        name="encode",
    )(inputs, w_first, w2t, inv_row, probes, solves)


def block_parts(ref, own_rows):
    feat = ref.shape[1] // 2
    size = 2 * own_rows + own_rows // 2
    blocks = []
    for at in range(0, ref.shape[0], size):
        packed = ref[at + 2 * own_rows : at + size, :]
        u = jnp.concatenate([packed[:, :feat], packed[:, feat:]], axis=0)
        blocks.append((ref[at : at + own_rows, :], ref[at + own_rows : at + 2 * own_rows, :], u))
    return blocks


def gate_body(sizes, *refs):
    outs = refs[-1 - len(sizes) :]
    at = 0
    for size, out_ref in zip(sizes, outs):
        start = 0
        for ref in refs[at : at + size]:
            out_ref[start : start + ref.shape[0], :] = ref[...]
            start += ref.shape[0]
        at += size
    outs[-1][...] = refs[at][...]


def gate(groups, inputs, after):
    sizes = [len(group) for group in groups]
    blocks = [block for group in groups for block in group]
    shapes = [jax.ShapeDtypeStruct((sum(b.shape[0] for b in group), group[0].shape[1]), BF16) for group in groups]
    return pl.pallas_call(
        lambda *refs: gate_body(sizes, *refs),
        in_specs=[VMEM] * (len(blocks) + 1) + [ANY] * len(after),
        out_specs=(VMEM,) * (len(groups) + 1),
        out_shape=tuple(shapes) + (jax.ShapeDtypeStruct(inputs.shape, BF16),),
        compiler_params=params(),
        name="gate",
    )(*blocks, inputs, *after)


def rows_body(own_rows, count, *refs):
    row_refs, (rowa_ref, rsp_ref) = refs[:count], refs[-2:]
    blocks = [block for ref in row_refs for block in block_parts(ref, own_rows)]
    for b, (p, s, u) in enumerate(blocks):
        at = slice(b * own_rows, (b + 1) * own_rows)
        u32 = u.astype(F32)
        h = -0.5 * jnp.sum(u32 * u32, axis=1, keepdims=True)
        h1 = h.astype(BF16).astype(F32)
        h2 = (h - h1).astype(BF16).astype(F32)
        h3 = h - h1 - h2
        lane = lax.broadcasted_iota(jnp.int32, u.shape, 1)
        tail = jnp.where(lane == 0, h1, jnp.where(lane == 1, h2, jnp.where(lane == 2, h3, 0.0)))
        minus = jnp.full((own_rows, 2 * u.shape[1]), -0.5, BF16)
        rowa_ref[at, :] = jnp.concatenate([u, minus, tail.astype(BF16)], axis=1)
        rsp_ref[at, :] = jnp.concatenate([s, p], axis=1)


def group_rows(own_rows, row_blocks):
    count = len(row_blocks)
    shape = jax.ShapeDtypeStruct((lax.axis_size("kc") * own_rows, 2 * row_blocks[0].shape[1]), BF16)
    return pl.pallas_call(
        lambda *refs: rows_body(own_rows, count, *refs),
        in_specs=[VMEM] * count,
        out_specs=(VMEM, VMEM),
        out_shape=(shape, shape),
        compiler_params=params(),
        name="rows",
    )(*row_blocks)


def pair_body(own_rows, counts, first, last, rowa_ref, rsp_ref, *refs):
    col_refs, refs = refs[: len(counts)], refs[len(counts) :]
    if not first:
        v_in, m_in, s_in = refs[:3]
    if last:
        v_ref, gone_ref, keep_ref, send_ref = refs[-4:]
    else:
        v_ref, m_ref, s_ref = refs[-3:]
    probe = v_ref.shape[1]
    feat = probe // 2
    rows = rowa_ref.shape[0]
    blocks = [block for ref, n in zip(col_refs, counts) for block in block_parts(ref, own_rows)[:n]]
    group = 2
    v, m, sums = (None, None, None) if first else (v_in[...], m_in[...], s_in[...])
    for b in range(0, len(blocks), group):
        pieces = blocks[b : b + group]
        p = jnp.concatenate([q[0] for q in pieces], axis=0)
        s = jnp.concatenate([q[1] for q in pieces], axis=0)
        u = jnp.concatenate([q[2] for q in pieces], axis=0)
        u32 = u.astype(F32)
        sq = u32 * u32
        hi = sq.astype(BF16)
        lo = (sq - hi.astype(F32)).astype(BF16)
        lane = lax.broadcasted_iota(jnp.int32, u.shape, 1)
        ones = jnp.where(lane < 3, 1.0, 0.0).astype(BF16)
        kern = jnp.exp(dot_nt(rowa_ref[...], jnp.concatenate([u, hi, lo, ones], axis=1)))
        one = kern * dot_nt(rsp_ref[:, :probe], p)
        two = kern * dot_nt(rsp_ref[:, probe:], s)
        both = one + two
        lanes = both[:, :128]
        for at in range(128, both.shape[1], 128):
            lanes = lanes + both[:, at : at + 128]
        v_part = dot_nn(kern.astype(BF16), p)
        m_part = dot_nn(one.astype(BF16), u) + dot_nn(two.astype(BF16), u)
        v = v_part if v is None else v + v_part
        m = m_part if m is None else m + m_part
        sums = lanes if sums is None else sums + lanes
    if last:
        v = [v[b * own_rows : (b + 1) * own_rows] for b in range(rows // own_rows)]
        v_ref[...] = jnp.concatenate([v[0], v[1]], axis=0)
        gone_ref[...] = jnp.concatenate([v[2], v[3]], axis=0)
        t = jnp.sum(sums, axis=1, keepdims=True) * rowa_ref[:, :feat].astype(F32) - m
        t = [t[b * own_rows : (b + 1) * own_rows] for b in range(rows // own_rows)]
        keep_ref[...] = jnp.concatenate([t[0], t[1]], axis=1)
        send_ref[...] = jnp.concatenate([t[2], t[3]], axis=1)
    else:
        v_ref[...] = v
        m_ref[...] = m
        s_ref[...] = sums


def pairs(own_rows, rowa, rsp, col_blocks, counts, before, last):
    rows, cols = rowa.shape[0], sum(counts) * own_rows
    probe = col_blocks[0].shape[1]
    feat = probe // 2
    first = before is None
    operands = [rowa, rsp] + list(col_blocks) + list(before or ())
    whole = jax.ShapeDtypeStruct((rows, probe), F32)
    half = jax.ShapeDtypeStruct((rows // 2, probe), F32)
    quarter = jax.ShapeDtypeStruct((own_rows, probe), F32)
    thin = jax.ShapeDtypeStruct((rows, feat), F32)
    return pl.pallas_call(
        lambda *refs: pair_body(own_rows, counts, first, last, *refs),
        in_specs=[VMEM] * len(operands),
        out_specs=(VMEM,) * (4 if last else 3),
        out_shape=(half, half, quarter, quarter) if last else (whole, thin, jax.ShapeDtypeStruct((rows, 128), F32)),
        compiler_params=params(),
        cost_estimate=pl.CostEstimate(flops=1, bytes_accessed=2 * (rows + cols) * 384, transcendentals=0),
        name="pairs",
    )(*operands)


def selection(mine, width, share, order):
    tall, line = lax.axis_size("kr"), lax.axis_size("kc")
    at_row = lax.broadcasted_iota(jnp.int32, (mine, 1), 0)
    piece = at_row // share
    if order:
        owner_line = jnp.zeros_like(piece)
        for i, (deep_mask, tall_mask) in enumerate(order):
            target = (lax.axis_index("enc") ^ deep_mask) * tall + (lax.axis_index("kr") ^ tall_mask)
            owner_line = jnp.where(piece == i, target, owner_line)
        piece = owner_line
    owner = share * (line * piece + lax.axis_index("kc")) + at_row % share
    at_col = lax.broadcasted_iota(jnp.int32, (mine, width), 1)
    return jnp.where(at_col == owner, 1.0, 0.0).astype(BF16)


def prepare_body(share, order, xa_ref, xb_ref, w1_ref, *refs):
    slope_ref, xt_ref, ht_ref = refs[-3:]
    width, hid = w1_ref.shape
    sel = selection(xt_ref.shape[0], width, share, order)
    block = 256
    x = jnp.concatenate([xa_ref[...], xb_ref[...]], axis=0)
    xt_ref[...] = dot_nt(sel, x).astype(BF16)
    ht = None
    for j in range(hid // block):
        at = slice(j * block, (j + 1) * block)
        pre = dot_nn(x, w1_ref[:, at])
        sig = jax.nn.sigmoid(pre)
        hidden = (pre * sig).astype(BF16)
        slope_ref[:, at] = sig * (1.0 + pre * (1.0 - sig))
        part = dot_nt(sel[:, at], hidden)
        ht = part if ht is None else ht + part
    ht_ref[...] = ht.astype(BF16)


def prepare(xa, xb, w_first, share, order, after=()):
    rows = 2 * xa.shape[0]
    width, hid = w_first.shape
    thin = jax.ShapeDtypeStruct((width // lax.axis_size("kc"), rows), BF16)
    return pl.pallas_call(
        lambda *refs: prepare_body(share, order, *refs),
        in_specs=[VMEM] * 3 + [ANY] * len(after),
        out_specs=(VMEM,) * 3,
        out_shape=(jax.ShapeDtypeStruct((rows, hid), F32), thin, thin),
        compiler_params=params(),
        cost_estimate=pl.CostEstimate(flops=1, bytes_accessed=2**20, transcendentals=0),
        name="prepare",
    )(xa, xb, w_first, *after)


def finish_body(scale, term_ref, far_ref, inv_ref, *refs):
    feat = inv_ref.shape[1]
    far = far_ref[...]
    far = jnp.concatenate([far[:, feat:], far[:, :feat]], axis=1)
    inv = jnp.concatenate([inv_ref[...], inv_ref[...]], axis=1)
    refs[-1][...] = (scale * inv * (term_ref[...] + far)).astype(BF16)


def finish(scale, term, far, inv_row, after):
    return pl.pallas_call(
        lambda *refs: finish_body(scale, *refs),
        in_specs=[VMEM] * 3 + [ANY] * len(after),
        out_specs=VMEM,
        out_shape=jax.ShapeDtypeStruct(term.shape, BF16),
        compiler_params=params(),
        name="finish",
    )(term, far, inv_row, *after)


def grads_body(sizes, d_ref, e_ref, w2t_ref, slope_a, xt_a, ht_a, slope_b, xt_b, ht_b, *out_refs):
    feat, hid = w2t_ref.shape
    d, e = d_ref[...], e_ref[...]
    dfeat_a = jnp.concatenate([d[:, :feat], e[:, :feat]], axis=0)
    dfeat_b = jnp.concatenate([d[:, feat:], e[:, feat:]], axis=0)

    def store(at, part):
        start = 0
        for size, ref in zip(sizes, out_refs):
            ref[:, at] = part[start : start + size]
            start += size

    block = 256
    for j in range(hid // block):
        at = slice(j * block, (j + 1) * block)
        dpre_a = (dot_nn(dfeat_a, w2t_ref[:, at]) * slope_a[:, at]).astype(BF16)
        dpre_b = (dot_nn(dfeat_b, w2t_ref[:, at]) * slope_b[:, at]).astype(BF16)
        store(at, (dot_nn(xt_a[...], dpre_a) + dot_nn(xt_b[...], dpre_b)).astype(BF16))
    store(slice(hid, hid + feat), (dot_nn(ht_a[...], dfeat_a) + dot_nn(ht_b[...], dfeat_b)).astype(BF16))


def grads(d, e, w2t, group_a, group_b, sizes):
    feat, hid = w2t.shape
    return pl.pallas_call(
        lambda *refs: grads_body(sizes, *refs),
        in_specs=[VMEM] * 9,
        out_specs=(VMEM,) * len(sizes),
        out_shape=tuple(jax.ShapeDtypeStruct((size, hid + feat), BF16) for size in sizes),
        compiler_params=params(),
        name="grads",
    )(d, e, w2t, *group_a, *group_b)


def relay_body(count, got_ref, *refs):
    got = got_ref[...].astype(F32)
    start = 0
    for own_ref, out_ref in zip(refs[:count], refs[-count:]):
        size = own_ref.shape[0]
        out_ref[...] = (own_ref[...].astype(F32) + got[start : start + size]).astype(out_ref.dtype)
        start += size


def relay(got, own, kinds, after=()):
    return pl.pallas_call(
        lambda *refs: relay_body(len(own), *refs),
        in_specs=[VMEM] * (1 + len(own)) + [ANY] * len(after),
        out_specs=(VMEM,) * len(own),
        out_shape=tuple(jax.ShapeDtypeStruct(x.shape, kind) for x, kind in zip(own, kinds)),
        compiler_params=params(),
        name="relay",
    )(got, *own, *after)


def total_body(*refs):
    parts, (first_ref, second_ref) = refs[:-2], refs[-2:]
    total = parts[0][...].astype(F32)
    for ref in parts[1:]:
        total = total + ref[...].astype(F32)
    hid = first_ref.shape[1]
    first_ref[...] = total[:, :hid]
    second_ref[...] = total[:, hid:]


def total(parts, hid):
    share, width = parts[0].shape
    return pl.pallas_call(
        total_body,
        in_specs=[VMEM] * len(parts),
        out_specs=(VMEM, VMEM),
        out_shape=(jax.ShapeDtypeStruct((share, hid), F32), jax.ShapeDtypeStruct((share, width - hid), F32)),
        compiler_params=params(),
        name="total",
    )(*parts)


def hold_body(x_ref, *refs):
    refs[-1][...] = x_ref[...]


def hold(x, after):
    return pl.pallas_call(
        hold_body,
        in_specs=[VMEM] + [ANY] * len(after),
        out_specs=VMEM,
        out_shape=jax.ShapeDtypeStruct(x.shape, x.dtype),
        compiler_params=params(),
        name="hold",
    )(x, *after)


def local(inputs, w_first, w_second, inv_length, probes, solves):
    own_rows, width = inputs.shape
    hid, feat = w_second.shape
    probe_width = probes.shape[1]
    line, deep, tall = lax.axis_size("kc"), lax.axis_size("enc"), lax.axis_size("kr")
    lines = deep * tall
    share = width // (line * lines)
    order = [(2, 1), (3, 1), (1, 1), (0, 1), (2, 0), (3, 0), (1, 0), (0, 0)] if (deep, tall) == (4, 2) else None
    inv_row = inv_length[None, :]
    w2t = w_second.T

    own = encode(inputs, w_first, w2t, inv_row, probes, solves)
    x_core = swap(inputs, "kc", 1)
    group_a = prepare(inputs, x_core, w_first, share, order, (own,))
    far_row = swap(own, "kc", 2)
    tall_masks = range(1, tall)
    if order:
        z_two, z_one, y_own = swap(own, "enc", 2), swap(own, "enc", 1), swap(own, "kr", 1)
        z_both, row_both, held = gate(([z_one, z_two], [own, far_row]), inputs, (y_own, group_a[1]))
        core_both = swap(row_both, "kc", 1)
        calls = [
            ([row_both, y_own], [1, 1]),
            ([z_one, z_two], [1, 1]),
            ([swap(z_both, "kr", 1)], [2]),
            ([swap(z_two, "enc", 1), swap_both(own, 3, 1)], [1, 1]),
        ]
    else:
        columns = [own]
        mask = deep // 2
        while mask:
            columns = columns + [swap(block, "enc", mask) for block in columns]
            mask //= 2
        calls = [([block] + [swap(block, "kr", m) for m in tall_masks], [1] * tall) for block in columns]
        row_both, held = gate(([own, far_row],), inputs, ())
        core_both = swap(row_both, "kc", 1)
    rowa, rsp = group_rows(own_rows, [row_both, core_both])
    x_far = swap(held, "kc", 2)

    sofar = None
    for i, (blocks, counts) in enumerate(calls):
        sofar = pairs(own_rows, rowa, rsp, blocks, counts, sofar, i == len(calls) - 1)
    stay, gone, keep, send = sofar
    x_both = swap(hold(x_far, (send,)), "kc", 1)
    group_b = prepare(x_far, x_both, w_first, share, order, (send,))
    term = keep + swap(send, "kc", 1)
    lscale = loss_gain / math.sqrt(probe_width)
    dfeat = finish(-lscale, term, swap(term, "kc", 2), inv_row, (group_b[1],))
    other = swap(dfeat, "kc", 1)
    stay = stay + swap(hold(gone, (term,)), "kc", 1)
    sizes = [share * n for n in (4, 1, 1, 1, 1)] if order else [width // line]
    parts = grads(dfeat, other, w2t, group_a, group_b, sizes)
    far = swap(hold(stay[own_rows:], (parts[0],)), "kc", 2)
    if order:
        two, three, one, here = relay(swap(parts[0], "kr", 1), parts[1:], (BF16, BF16, BF16, F32), (far,))
        got = [here, swap(two, "enc", 2), swap(three, "enc", 3), swap(one, "enc", 1)]
    else:
        flat = lax.all_to_all(parts[0], ("enc", "kr"), 0, 0, tiled=True)
        got = list(flat.astype(F32).reshape(lines, share, hid + feat))
    grad_first, grad_second = total(got, hid)

    v = stay[:own_rows] + far
    products = (v * probe_gain).astype(BF16)
    return products, grad_first, grad_second


def solution(mesh):
    rows = P(("enc", "kr", "kc"), None)
    return jax.shard_map(
        local,
        mesh=mesh,
        in_specs=(rows, P(), P(), P(), rows, rows),
        out_specs=(rows, rows, rows),
        check_vma=False,
    )
```

time: 473 us -> 61.2 us (0.13)
  waiting for transfers between devices: 299 us -> 21.3 us
  blocking collectives: 124 us -> 0 us
  starting transfers between devices: 0.16 us -> 20.3 us
  Pallas kernels: 0 us -> 17.8 us
  matrix products: 16.9 us -> 0 us
  local copies, waits for them, and re-layouts: 15.1 us -> 0.03 us
  between operations: 14.5 us -> 0.86 us
    unnamed x6 -> x0, waiting for transfers between devices: 153 us -> none
    reduce_scatter x2 -> x0, waiting for transfers between devices: 146 us -> none  [the longest x1 135 us: local(): lax.psum_scatter(second_term, ('enc', 'kr', 'kc'), scatter_dimension=0, t...]
    all_gather x6 -> x0, blocking collectives: 118 us -> none  [the longest x1 33.5 us: local(): lax.all_gather(solves, ('enc', 'kr'), axis=0, tiled=True)]
    ppermute x0 -> x20, waiting for transfers between devices: none -> 21.3 us  [the longest x19 21.3 us: swap(): return lax.ppermute(x, axis, [(i, i ^ mask) for i in range(size)])]
    ppermute x0 -> x20, starting transfers between devices: none -> 20.3 us  [the longest x19 17.3 us: swap(): return lax.ppermute(x, axis, [(i, i ^ mask) for i in range(size)])]
    pallas_call x0 -> x16, Pallas kernels: none -> 17.8 us  [the longest x4 5.49 us: pairs(): pl.pallas_call(lambda *refs: pair_body(own_rows, counts, first, last, *re...]
    dot_general x16 -> x0, matrix products: 16.9 us -> none  [the longest x2 6.31 us: contract_outer(): lax.dot_general(left, right, (((0,), (0,)), ((), ())), preferred_element_...]
    unnamed x24 -> x8, local copies, waits for them, and re-layouts: 12 us -> 0.02 us
  transfers between devices with their start and end apart: 4 -> 20, of which waited for: 4 -> 9; matrix products, arithmetic and copies ran while one was open for 3% -> 1% of each run, Pallas kernels for 0% -> 26%
where the time goes in v2:
time: 61.2 us; the launch traced here: 61 us
  waiting for transfers between devices  21.3 us (35%)
  starting transfers between devices  20.3 us (33%)
  Pallas kernels  17.8 us (29%)
  between operations  0.86 us (1%)
  other arithmetic  0.67 us (1%)
    ppermute x19, waiting for transfers between devices, swap(): return lax.ppermute(x, axis, [(i, i ^ mask) for i in range(size)])  21.3 us
    ppermute x19, starting transfers between devices, swap(): return lax.ppermute(x, axis, [(i, i ^ mask) for i in range(size)])  17.3 us
    pallas_call x4, Pallas kernels, pairs(): pl.pallas_call(lambda *refs: pair_body(own_rows, counts, first, last, *re...  5.49 us
    pallas_call x2, Pallas kernels, prepare(): pl.pallas_call(lambda *refs: prepare_body(share, order, *refs), in_specs=...  4.76 us
    pallas_call x1, Pallas kernels, encode(): pl.pallas_call(encode_body, in_specs=[HBM] * 6, out_specs=VMEM, out_shape...  3.73 us
    ppermute x1, starting transfers between devices, swap_both(): return lax.ppermute(x, ('enc', 'kr'), pairs_of)  3 us
    pallas_call x1, Pallas kernels, grads(): pl.pallas_call(lambda *refs: grads_body(sizes, *refs), in_specs=[VMEM] *...  1.43 us
  transfers between devices with their start and end apart: 20, of which 9 were waited for; matrix products, arithmetic and copies ran while one was open for 1% of the time, Pallas kernels for 26%

profile of v2, /device:TPU:0, one launch (start us, length us, event | category | flops | bytes accessed | tf_op | source)
XLA Modules:
  0.0 61.0 jit_solution(13181763476988363465)
XLA Ops:
  0.6 0.0 copy-start.1
  0.6 0.0 copy-start
  0.7 0.5 collective-permute-start.4
  1.2 3.7 %encode.1.refs_3_.refs_2_ = bf16[480,128]{1,0:T(8,128)(2,1)} custom-call(bf16[192,1024]{1,0:T(8,128)(2,1)} %refs_4_.1, bf16[1024,1024]{1,0:T(8,128)(2,1)} %refs_2_.3, bf16[64,1024]{1,0:T(8,128)(2,1)} %bitcast.2, f32[1,64]{1,0:T(1,128)} %bitcast.4, bf16[192,128]{1,0:T(8,128)(2,1)} %probe_hbm.1, bf16[192,128]{1,0:T(8,128)(2,1)} %solve_hbm.1), custom_call_target="tpu_custom_call" | custom-call | tf_op jit(solution)/shard_map/encode/pallas_call | solution.py:86
  4.9 3.6 %collective-permute-start.1 = (bf16[480,128]{1,0:T(8,128)(2,1)}, bf16[480,128]{1,0:T(8,128)(2,1)S(1)}, u32[]{:S(2)}, u32[]{:S(2)}) collective-permute-start(bf16[480,128]{1,0:T(8,128)(2,1)} %encode.1.refs_3_.refs_2_), channel_id=1, source_target_pairs={{0,16},{8,24},{16,0},{24,8},{1,17},{9,25},{17,1},{25,9},{2,18},{10... | collective-permute-start | bytes 368648 | tf_op jit(solution)/shard_map/ppermute | solution.py:31
  8.5 1.6 %collective-permute-start = (bf16[480,128]{1,0:T(8,128)(2,1)}, bf16[480,128]{1,0:T(8,128)(2,1)S(1)}, u32[]{:S(2)}, u32[]{:S(2)}) collective-permute-start(bf16[480,128]{1,0:T(8,128)(2,1)} %encode.1.refs_3_.refs_2_), channel_id=1, source_target_pairs={{0,8},{8,0},{16,24},{24,16},{1,9},{9,1},{17,25},{25,17},{2,10},{10... | collective-permute-start | bytes 368648 | tf_op jit(solution)/shard_map/ppermute | solution.py:31
  10.1 1.5 %collective-permute-start.3 = (bf16[480,128]{1,0:T(8,128)(2,1)}, bf16[480,128]{1,0:T(8,128)(2,1)S(1)}, u32[]{:S(2)}, u32[]{:S(2)}) collective-permute-start(bf16[480,128]{1,0:T(8,128)(2,1)} %encode.1.refs_3_.refs_2_), channel_id=1, source_target_pairs={{0,4},{4,0},{1,5},{5,1},{2,6},{6,2},{3,7},{7,3},{8,12},{12,8},{9,1... | collective-permute-start | bytes 368648 | tf_op jit(solution)/shard_map/ppermute | solution.py:31
  11.6 1.5 %collective-permute-start.2 = (bf16[480,128]{1,0:T(8,128)(2,1)}, bf16[480,128]{1,0:T(8,128)(2,1)S(1)}, u32[]{:S(2)}, u32[]{:S(2)}) collective-permute-start(bf16[480,128]{1,0:T(8,128)(2,1)} %encode.1.refs_3_.refs_2_), channel_id=1, source_target_pairs={{0,2},{1,3},{2,0},{3,1},{4,6},{5,7},{6,4},{7,5},{8,10},{9,11},{10,... | collective-permute-start | bytes 368648 | tf_op jit(solution)/shard_map/ppermute | solution.py:31
  13.1 0.0 collective-permute-done.4.refs_1_
  13.1 0.0 copy-done.1
  13.1 0.0 copy-done
  13.1 2.4 %prepare.2 = (f32[384,1024]{1,0:T(8,128)S(1)}, bf16[256,384]{1,0:T(8,128)(2,1)S(1)}, bf16[256,384]{1,0:T(8,128)(2,1)S(1)}) custom-call(bf16[192,1024]{1,0:T(8,128)(2,1)S(1)} %copy-done.1, bf16[192,1024]{1,0:T(8,128)(2,1)S(1)} %collective-permute-done.4.refs_1_, bf16[1024,1024]{1,0:T(8,128)(2,1)S(1)} %copy-done, bf16[480,128]{1,0:T(8,128)(2,1)} %encode.1.refs_3_.refs_2_), custom_call_target="tpu_custom_call" | custom-call | flops 1 | bytes 1048576 | tf_op jit(solution)/shard_map/prepare/pallas_call | solution.py:280
  15.5 0.0 collective-permute-done.1.refs_1_.refs_3_
  15.5 0.0 collective-permute-done.refs_0_.refs_2_
  15.5 0.0 collective-permute-done.3.refs_5_.refs_3_
  15.5 1.2 %collective-permute-done.2.refs_3_ = bf16[480,128]{1,0:T(8,128)(2,1)S(1)} collective-permute-done((bf16[480,128]{1,0:T(8,128)(2,1)}, bf16[480,128]{1,0:T(8,128)(2,1)S(1)}, u32[]{:S(2)}, u32[]{:S(2)}) %collective-permute-start.2) | collective-permute-done | bytes 122912 | tf_op jit(solution)/shard_map/ppermute | solution.py:31
  16.7 1.0 %gate.1 = (bf16[960,128]{1,0:T(8,128)(2,1)S(1)}, bf16[960,128]{1,0:T(8,128)(2,1)S(1)}, bf16[192,1024]{1,0:T(8,128)(2,1)S(1)}) custom-call(bf16[480,128]{1,0:T(8,128)(2,1)S(1)} %collective-permute-done.refs_0_.refs_2_, bf16[480,128]{1,0:T(8,128)(2,1)S(1)} %collective-permute-done.1.refs_1_.refs_3_, bf16[480,128]{1,0:T(8,128)(2,1)} %encode.1.refs_3_.refs_2_, ...), custom_call_target="tpu_custom_call" | custom-call | tf_op jit(solution)/shard_map/gate/pallas_call | solution.py:130
  17.7 1.6 %collective-permute-start.12 = (bf16[192,1024]{1,0:T(8,128)(2,1)S(1)}, bf16[192,1024]{1,0:T(8,128)(2,1)S(1)}, u32[]{:S(2)}, u32[]{:S(2)}) collective-permute-start(bf16[192,1024]{1,0:T(8,128)(2,1)S(1)} %get-tuple-element.56), channel_id=1, source_target_pairs={{0,2},{1,3},{2,0},{3,1},{4,6},{5,7},{6,4},{7,5},{8,10},{9,11},{10,... | collective-permute-start | bytes 1179656 | tf_op jit(solution)/shard_map/ppermute | solution.py:31
  19.2 0.0 collective-permute-start.5
  19.2 0.5 collective-permute-start.8
  19.7 3.0 %collective-permute-start.7 = (bf16[480,128]{1,0:T(8,128)(2,1)}, bf16[480,128]{1,0:T(8,128)(2,1)S(1)}, u32[]{:S(2)}, u32[]{:S(2)}) collective-permute-start(bf16[480,128]{1,0:T(8,128)(2,1)} %encode.1.refs_3_.refs_2_), channel_id=1, source_target_pairs={{0,28},{4,24},{8,20},{12,16},{16,12},{20,8},{24,4},{28,0},{1,29},{... | collective-permute-start | bytes 368648 | tf_op jit(solution)/shard_map/ppermute | solution.py:37
  22.7 0.0 collective-permute-start.6
  22.7 0.0 collective-permute-done.5.refs_1_
  22.7 0.5 rows.1
  23.3 1.3 %pairs.4 = (f32[768,128]{1,0:T(8,128)S(1)}, f32[768,64]{1,0:T(8,128)S(1)}, f32[768,128]{1,0:T(8,128)S(1)}) custom-call(bf16[768,256]{1,0:T(8,128)(2,1)S(1)} %get-tuple-element.40.refs_0_, bf16[768,256]{1,0:T(8,128)(2,1)S(1)} %get-tuple-element.41.refs_1_, bf16[960,128]{1,0:T(8,128)(2,1)S(1)} %get-tuple-element.39.refs_0_.refs_2_, ...), custom_call_target="tpu_custom_call" | custom-call | flops 1 | bytes 884736 | tf_op jit(solution)/shard_map/pairs/pallas_call | solution.py:231
  24.6 1.4 %pairs.5 = (f32[768,128]{1,0:T(8,128)S(1)}, f32[768,64]{1,0:T(8,128)S(1)}, f32[768,128]{1,0:T(8,128)S(1)}) custom-call(bf16[768,256]{1,0:T(8,128)(2,1)S(1)} %get-tuple-element.40.refs_0_, bf16[768,256]{1,0:T(8,128)(2,1)S(1)} %get-tuple-element.41.refs_1_, bf16[480,128]{1,0:T(8,128)(2,1)S(1)} %collective-permute-done.refs_0_.refs_2_, ...), custom_call_target="tpu_custom_call" | custom-call | flops 1 | bytes 884736 | tf_op jit(solution)/shard_map/pairs/pallas_call | solution.py:231
  26.0 4.2 %collective-permute-done.8.refs_2_ = bf16[960,128]{1,0:T(8,128)(2,1)S(1)} collective-permute-done((bf16[960,128]{1,0:T(8,128)(2,1)S(1)}, bf16[960,128]{1,0:T(8,128)(2,1)S(1)}, u32[]{:S(2)}, u32[]{:S(2)}) %collective-permute-start.8) | collective-permute-done | bytes 245792 | tf_op jit(solution)/shard_map/ppermute | solution.py:31
  30.2 1.4 %pairs.6 = (f32[768,128]{1,0:T(8,128)S(1)}, f32[768,64]{1,0:T(8,128)S(1)}, f32[768,128]{1,0:T(8,128)S(1)}) custom-call(bf16[768,256]{1,0:T(8,128)(2,1)S(1)} %get-tuple-element.40.refs_0_, bf16[768,256]{1,0:T(8,128)(2,1)S(1)} %get-tuple-element.41.refs_1_, bf16[960,128]{1,0:T(8,128)(2,1)S(1)} %collective-permute-done.8.refs_2_, ...), custom_call_target="tpu_custom_call" | custom-call | flops 1 | bytes 884736 | tf_op jit(solution)/shard_map/pairs/pallas_call | solution.py:231
  31.6 0.0 collective-permute-done.7.refs_3_
  31.6 0.0 collective-permute-done.6.refs_2_
  31.6 1.4 %pairs.7 = (f32[384,128]{1,0:T(8,128)S(1)}, f32[384,128]{1,0:T(8,128)S(1)}, f32[192,128]{1,0:T(8,128)S(1)}, f32[192,128]{1,0:T(8,128)S(1)}) custom-call(bf16[768,256]{1,0:T(8,128)(2,1)S(1)} %get-tuple-element.40.refs_0_, bf16[768,256]{1,0:T(8,128)(2,1)S(1)} %get-tuple-element.41.refs_1_, bf16[480,128]{1,0:T(8,128)(2,1)S(1)} %collective-permute-done.6.refs_2_, ...), custom_call_target="tpu_custom_call" | custom-call | flops 1 | bytes 884736 | tf_op jit(solution)/shard_map/pairs/pallas_call | solution.py:231
  33.0 0.0 collective-permute-done.12.x_ref.refs_0_
  33.1 0.1 collective-permute-start.13
  33.2 0.5 collective-permute-start.9
  33.7 1.4 %collective-permute-done.9 = f32[192,128]{1,0:T(8,128)S(1)} collective-permute-done((f32[192,128]{1,0:T(8,128)S(1)}, f32[192,128]{1,0:T(8,128)S(1)}, u32[]{:S(2)}, u32[]{:S(2)}) %collective-permute-start.9) | collective-permute-done | bytes 98336 | tf_op jit(solution)/shard_map/ppermute | solution.py:31
  35.0 0.0 copy-start.3
  35.0 0.0 copy-start.2
  35.0 0.6 collective-permute-start.11
  35.7 0.0 collective-permute-done.13.refs_1_
  35.7 2.4 %prepare.3 = (f32[384,1024]{1,0:T(8,128)S(1)}, bf16[256,384]{1,0:T(8,128)(2,1)S(1)}, bf16[256,384]{1,0:T(8,128)(2,1)S(1)}) custom-call(bf16[192,1024]{1,0:T(8,128)(2,1)S(1)} %collective-permute-done.12.x_ref.refs_0_, bf16[192,1024]{1,0:T(8,128)(2,1)S(1)} %collective-permute-done.13.refs_1_, bf16[1024,1024]{1,0:T(8,128)(2,1)S(1)} %copy-done, ...), custom_call_target="tpu_custom_call" | custom-call | flops 1 | bytes 1048576 | tf_op jit(solution)/shard_map/prepare/pallas_call | solution.py:280
  38.0 1.9 %collective-permute-done.11.refs_1_ = f32[192,128]{1,0:T(8,128)S(1)} collective-permute-done((f32[192,128]{1,0:T(8,128)S(1)}, f32[192,128]{1,0:T(8,128)S(1)}, u32[]{:S(2)}, u32[]{:S(2)}) %collective-permute-start.11) | collective-permute-done | bytes 98336 | tf_op jit(solution)/shard_map/ppermute | solution.py:31
  40.0 0.0 copy-done.3
  40.0 0.1 finish.1.refs_0_
  40.1 0.1 collective-permute-start.14
  40.2 0.6 collective-permute-start.10
  40.7 0.6 %collective-permute-done.14.refs_1_ = bf16[192,128]{1,0:T(8,128)(2,1)S(1)} collective-permute-done((bf16[192,128]{1,0:T(8,128)(2,1)S(1)}, bf16[192,128]{1,0:T(8,128)(2,1)S(1)}, u32[]{:S(2)}, u32[]{:S(2)}) %collective-permute-start.14) | collective-permute-done | bytes 49184 | tf_op jit(solution)/shard_map/ppermute | solution.py:31
  41.3 0.0 copy-done.2
  41.4 1.4 %grads.1 = (bf16[128,1088]{1,0:T(8,128)(2,1)S(1)}, bf16[32,1088]{1,0:T(8,128)(2,1)S(1)}, bf16[32,1088]{1,0:T(8,128)(2,1)S(1)}, bf16[32,1088]{1,0:T(8,128)(2,1)S(1)}, bf16[32,1088]{1,0:T(8,128)(2,1)S(1)}) custom-call(bf16[192,128]{1,0:T(8,128)(2,1)S(1)} %finish.1.refs_0_, bf16[192,128]{1,0:T(8,128)(2,1)S(1)} %collective-permute-done.14.refs_1_, ...), custom_call_target="tpu_custom_call" | custom-call | tf_op jit(solution)/shard_map/grads/pallas_call | solution.py:333
  42.8 0.6 collective-permute-start.16
  43.4 0.0 collective-permute-done.10
  43.4 0.6 collective-permute-start.15
  44.0 4.1 %collective-permute-done.15.refs_5_ = f32[192,128]{1,0:T(8,128)S(1)} collective-permute-done((f32[192,128]{1,0:T(8,128)S(1)}, f32[192,128]{1,0:T(8,128)S(1)}, u32[]{:S(2)}, u32[]{:S(2)}) %collective-permute-start.15) | collective-permute-done | bytes 98336 | tf_op jit(solution)/shard_map/ppermute | solution.py:31
  48.1 3.8 %collective-permute-done.16.refs_0_ = bf16[128,1088]{1,0:T(8,128)(2,1)S(1)} collective-permute-done((bf16[128,1088]{1,0:T(8,128)(2,1)S(1)}, bf16[128,1088]{1,0:T(8,128)(2,1)S(1)}, u32[]{:S(2)}, u32[]{:S(2)}) %collective-permute-start.16) | collective-permute-done | bytes 278560 | tf_op jit(solution)/shard_map/ppermute | solution.py:31
  51.9 0.1 relay.1
  52.0 0.4 collective-permute-start.17
  52.4 2.5 %collective-permute-start.18 = (bf16[32,1088]{1,0:T(8,128)(2,1)S(1)}, bf16[32,1088]{1,0:T(8,128)(2,1)S(1)}, u32[]{:S(2)}, u32[]{:S(2)}) collective-permute-start(bf16[32,1088]{1,0:T(8,128)(2,1)S(1)} %get-tuple-element.69), channel_id=1, source_target_pairs={{0,24},{8,16},{16,8},{24,0},{1,25},{9,17},{17,9},{25,1},{2,26},{10... | collective-permute-start | bytes 208904 | tf_op jit(solution)/shard_map/ppermute | solution.py:31
  54.9 0.7 %collective-permute-start.19 = (bf16[32,1088]{1,0:T(8,128)(2,1)S(1)}, bf16[32,1088]{1,0:T(8,128)(2,1)S(1)}, u32[]{:S(2)}, u32[]{:S(2)}) collective-permute-start(bf16[32,1088]{1,0:T(8,128)(2,1)S(1)} %get-tuple-element.70), channel_id=1, source_target_pairs={{0,8},{8,0},{16,24},{24,16},{1,9},{9,1},{17,25},{25,17},{2,10},{10... | collective-permute-start | bytes 208904 | tf_op jit(solution)/shard_map/ppermute | solution.py:31
  55.6 0.6 %fusion.1 = bf16[192,128]{1,0:T(8,128)(2,1)} fusion(f32[192,128]{1,0:T(8,128)S(1)} %collective-permute-done.15.refs_5_, f32[384,128]{1,0:T(8,128)S(1)} %add.10), kind=kLoop, calls=%fused_computation.2 | loop fusion | flops 73728 | bytes 245760 | tf_op jit(solution)/shard_map/convert_element_type | solution.py:461
  56.2 3.6 %collective-permute-done.17.refs_1_ = bf16[32,1088]{1,0:T(8,128)(2,1)S(1)} collective-permute-done((bf16[32,1088]{1,0:T(8,128)(2,1)S(1)}, bf16[32,1088]{1,0:T(8,128)(2,1)S(1)}, u32[]{:S(2)}, u32[]{:S(2)}) %collective-permute-start.17) | collective-permute-done | bytes 69664 | tf_op jit(solution)/shard_map/ppermute | solution.py:31
  59.8 0.0 collective-permute-done.18.refs_2_
  59.8 0.5 collective-permute-done.19.refs_3_
  60.3 0.7 %total.1 = (f32[32,1024]{1,0:T(8,128)}, f32[32,64]{1,0:T(8,128)}) custom-call(f32[32,1088]{1,0:T(8,128)S(1)} %get-tuple-element.67.refs_0_, bf16[32,1088]{1,0:T(8,128)(2,1)S(1)} %collective-permute-done.17.refs_1_, bf16[32,1088]{1,0:T(8,128)(2,1)S(1)} %collective-permute-done.18.refs_2_, bf16[32,1088]{1,0:T(8,128)(2,1)S(1)} %collective-permute-done.19.refs_3_), custom_call_target="tpu_custom_call" | custom-call | tf_op jit(solution)/shard_map/total/pallas_call | solution.py:375
  (6 shorter events, 0.1 us)
Async XLA Ops:
  0.6 12.5 %copy-start.1 = (bf16[192,1024]{1,0:T(8,128)(2,1)S(1)}, bf16[192,1024]{1,0:T(8,128)(2,1)}, u32[]{:S(2)}) copy-start(bf16[192,1024]{1,0:T(8,128)(2,1)} %refs_4_.1) | copy-start | bytes 1179652
  0.6 12.5 %copy-start = (bf16[1024,1024]{1,0:T(8,128)(2,1)S(1)}, bf16[1024,1024]{1,0:T(8,128)(2,1)}, u32[]{:S(2)}) copy-start(bf16[1024,1024]{1,0:T(8,128)(2,1)} %refs_2_.3) | copy-start | bytes 6291460
  0.7 12.5 %collective-permute-start.4 = (bf16[192,1024]{1,0:T(8,128)(2,1)}, bf16[192,1024]{1,0:T(8,128)(2,1)S(1)}, u32[]{:S(2)}, u32[]{:S(2)}) collective-permute-start(bf16[192,1024]{1,0:T(8,128)(2,1)} %refs_4_.1), channel_id=1, source_target_pairs={{0,1},{1,0},{2,3},{3,2},{4,5},{5,4},{6,7},{7,6},{8,9},{9,8},{10,11... | collective-permute-start | bytes 1179656 | tf_op jit(solution)/shard_map/ppermute | solution.py:31
  4.9 10.6 %collective-permute-start.1 = (bf16[480,128]{1,0:T(8,128)(2,1)}, bf16[480,128]{1,0:T(8,128)(2,1)S(1)}, u32[]{:S(2)}, u32[]{:S(2)}) collective-permute-start(bf16[480,128]{1,0:T(8,128)(2,1)} %encode.1.refs_3_.refs_2_), channel_id=1, source_target_pairs={{0,16},{8,24},{16,0},{24,8},{1,17},{9,25},{17,1},{25,9},{2,18},{10... | collective-permute-start | bytes 368648 | tf_op jit(solution)/shard_map/ppermute | solution.py:31
  8.5 7.0 %collective-permute-start = (bf16[480,128]{1,0:T(8,128)(2,1)}, bf16[480,128]{1,0:T(8,128)(2,1)S(1)}, u32[]{:S(2)}, u32[]{:S(2)}) collective-permute-start(bf16[480,128]{1,0:T(8,128)(2,1)} %encode.1.refs_3_.refs_2_), channel_id=1, source_target_pairs={{0,8},{8,0},{16,24},{24,16},{1,9},{9,1},{17,25},{25,17},{2,10},{10... | collective-permute-start | bytes 368648 | tf_op jit(solution)/shard_map/ppermute | solution.py:31
  10.1 5.4 %collective-permute-start.3 = (bf16[480,128]{1,0:T(8,128)(2,1)}, bf16[480,128]{1,0:T(8,128)(2,1)S(1)}, u32[]{:S(2)}, u32[]{:S(2)}) collective-permute-start(bf16[480,128]{1,0:T(8,128)(2,1)} %encode.1.refs_3_.refs_2_), channel_id=1, source_target_pairs={{0,4},{4,0},{1,5},{5,1},{2,6},{6,2},{3,7},{7,3},{8,12},{12,8},{9,1... | collective-permute-start | bytes 368648 | tf_op jit(solution)/shard_map/ppermute | solution.py:31
  11.6 5.1 %collective-permute-start.2 = (bf16[480,128]{1,0:T(8,128)(2,1)}, bf16[480,128]{1,0:T(8,128)(2,1)S(1)}, u32[]{:S(2)}, u32[]{:S(2)}) collective-permute-start(bf16[480,128]{1,0:T(8,128)(2,1)} %encode.1.refs_3_.refs_2_), channel_id=1, source_target_pairs={{0,2},{1,3},{2,0},{3,1},{4,6},{5,7},{6,4},{7,5},{8,10},{9,11},{10,... | collective-permute-start | bytes 368648 | tf_op jit(solution)/shard_map/ppermute | solution.py:31
  17.7 15.4 %collective-permute-start.12 = (bf16[192,1024]{1,0:T(8,128)(2,1)S(1)}, bf16[192,1024]{1,0:T(8,128)(2,1)S(1)}, u32[]{:S(2)}, u32[]{:S(2)}) collective-permute-start(bf16[192,1024]{1,0:T(8,128)(2,1)S(1)} %get-tuple-element.56), channel_id=1, source_target_pairs={{0,2},{1,3},{2,0},{3,1},{4,6},{5,7},{6,4},{7,5},{8,10},{9,11},{10,... | collective-permute-start | bytes 1179656 | tf_op jit(solution)/shard_map/ppermute | solution.py:31
  19.2 3.5 %collective-permute-start.5 = (bf16[960,128]{1,0:T(8,128)(2,1)S(1)}, bf16[960,128]{1,0:T(8,128)(2,1)S(1)}, u32[]{:S(2)}, u32[]{:S(2)}) collective-permute-start(bf16[960,128]{1,0:T(8,128)(2,1)S(1)} %get-tuple-element.39.refs_0_.refs_2_), channel_id=1, source_target_pairs={{0,1},{1,0},{2,3},{3,2},{4,5},{5,4},{6,7},{7,6},{8,9},{9,8},{10,11... | collective-permute-start | bytes 737288 | tf_op jit(solution)/shard_map/ppermute | solution.py:31
  19.2 11.0 %collective-permute-start.8 = (bf16[960,128]{1,0:T(8,128)(2,1)S(1)}, bf16[960,128]{1,0:T(8,128)(2,1)S(1)}, u32[]{:S(2)}, u32[]{:S(2)}) collective-permute-start(bf16[960,128]{1,0:T(8,128)(2,1)S(1)} %get-tuple-element.42), channel_id=1, source_target_pairs={{0,4},{4,0},{1,5},{5,1},{2,6},{6,2},{3,7},{7,3},{8,12},{12,8},{9,1... | collective-permute-start | bytes 737288 | tf_op jit(solution)/shard_map/ppermute | solution.py:31
  19.7 11.9 %collective-permute-start.7 = (bf16[480,128]{1,0:T(8,128)(2,1)}, bf16[480,128]{1,0:T(8,128)(2,1)S(1)}, u32[]{:S(2)}, u32[]{:S(2)}) collective-permute-start(bf16[480,128]{1,0:T(8,128)(2,1)} %encode.1.refs_3_.refs_2_), channel_id=1, source_target_pairs={{0,28},{4,24},{8,20},{12,16},{16,12},{20,8},{24,4},{28,0},{1,29},{... | collective-permute-start | bytes 368648 | tf_op jit(solution)/shard_map/ppermute | solution.py:37
  22.7 8.9 %collective-permute-start.6 = (bf16[480,128]{1,0:T(8,128)(2,1)S(1)}, bf16[480,128]{1,0:T(8,128)(2,1)S(1)}, u32[]{:S(2)}, u32[]{:S(2)}) collective-permute-start(bf16[480,128]{1,0:T(8,128)(2,1)S(1)} %collective-permute-done.1.refs_1_.refs_3_), channel_id=1, source_target_pairs={{0,8},{8,0},{16,24},{24,16},{1,9},{9,1},{17,25},{25,17},{2,10},{10... | collective-permute-start | bytes 368648 | tf_op jit(solution)/shard_map/ppermute | solution.py:31
  33.1 2.6 %collective-permute-start.13 = (bf16[192,1024]{1,0:T(8,128)(2,1)S(1)}, bf16[192,1024]{1,0:T(8,128)(2,1)S(1)}, u32[]{:S(2)}, u32[]{:S(2)}) collective-permute-start(bf16[192,1024]{1,0:T(8,128)(2,1)S(1)} %hold.4), channel_id=1, source_target_pairs={{0,1},{1,0},{2,3},{3,2},{4,5},{5,4},{6,7},{7,6},{8,9},{9,8},{10,11... | collective-permute-start | bytes 1179656 | tf_op jit(solution)/shard_map/ppermute | solution.py:31
  33.2 1.9 %collective-permute-start.9 = (f32[192,128]{1,0:T(8,128)S(1)}, f32[192,128]{1,0:T(8,128)S(1)}, u32[]{:S(2)}, u32[]{:S(2)}) collective-permute-start(f32[192,128]{1,0:T(8,128)S(1)} %get-tuple-element.55.refs_0_.refs_3_), channel_id=1, source_target_pairs={{0,1},{1,0},{2,3},{3,2},{4,5},{5,4},{6,7},{7,6},{8,9},{9,8},{10,11... | collective-permute-start | bytes 294920 | tf_op jit(solution)/shard_map/ppermute | solution.py:31
  35.0 4.9 %copy-start.3 = (f32[64]{0:T(128)S(1)}, f32[64]{0:T(128)}, u32[]{:S(2)}) copy-start(f32[64]{0:T(128)} %param.9) | copy-start | bytes 772
  35.0 6.3 %copy-start.2 = (bf16[1024,64]{0,1:T(8,128)(2,1)S(1)}, bf16[1024,64]{0,1:T(8,128)(2,1)}, u32[]{:S(2)}) copy-start(bf16[1024,64]{0,1:T(8,128)(2,1)} %param.8) | copy-start | bytes 393220
  35.0 4.9 %collective-permute-start.11 = (f32[192,128]{1,0:T(8,128)S(1)}, f32[192,128]{1,0:T(8,128)S(1)}, u32[]{:S(2)}, u32[]{:S(2)}) collective-permute-start(f32[192,128]{1,0:T(8,128)S(1)} %add.9.refs_0_), channel_id=1, source_target_pairs={{0,2},{1,3},{2,0},{3,1},{4,6},{5,7},{6,4},{7,5},{8,10},{9,11},{10,... | collective-permute-start | bytes 294920 | tf_op jit(solution)/shard_map/ppermute | solution.py:31
  40.1 1.3 %collective-permute-start.14 = (bf16[192,128]{1,0:T(8,128)(2,1)S(1)}, bf16[192,128]{1,0:T(8,128)(2,1)S(1)}, u32[]{:S(2)}, u32[]{:S(2)}) collective-permute-start(bf16[192,128]{1,0:T(8,128)(2,1)S(1)} %finish.1.refs_0_), channel_id=1, source_target_pairs={{0,1},{1,0},{2,3},{3,2},{4,5},{5,4},{6,7},{7,6},{8,9},{9,8},{10,11... | collective-permute-start | bytes 147464 | tf_op jit(solution)/shard_map/ppermute | solution.py:31
  40.2 3.2 %collective-permute-start.10 = (f32[384,128]{1,0:T(8,128)S(1)}, f32[384,128]{1,0:T(8,128)S(1)}, u32[]{:S(2)}, u32[]{:S(2)}) collective-permute-start(f32[384,128]{1,0:T(8,128)S(1)} %hold.3), channel_id=1, source_target_pairs={{0,1},{1,0},{2,3},{3,2},{4,5},{5,4},{6,7},{7,6},{8,9},{9,8},{10,11... | collective-permute-start | bytes 589832 | tf_op jit(solution)/shard_map/ppermute | solution.py:31
  42.8 9.1 %collective-permute-start.16 = (bf16[128,1088]{1,0:T(8,128)(2,1)S(1)}, bf16[128,1088]{1,0:T(8,128)(2,1)S(1)}, u32[]{:S(2)}, u32[]{:S(2)}) collective-permute-start(bf16[128,1088]{1,0:T(8,128)(2,1)S(1)} %get-tuple-element.62.refs_0_), channel_id=1, source_target_pairs={{0,4},{4,0},{1,5},{5,1},{2,6},{6,2},{3,7},{7,3},{8,12},{12,8},{9,1... | collective-permute-start | bytes 835592 | tf_op jit(solution)/shard_map/ppermute | solution.py:31
  43.4 4.7 %collective-permute-start.15 = (f32[192,128]{1,0:T(8,128)S(1)}, f32[192,128]{1,0:T(8,128)S(1)}, u32[]{:S(2)}, u32[]{:S(2)}) collective-permute-start(f32[192,128]{1,0:T(8,128)S(1)} %hold.5), channel_id=1, source_target_pairs={{0,2},{1,3},{2,0},{3,1},{4,6},{5,7},{6,4},{7,5},{8,10},{9,11},{10,... | collective-permute-start | bytes 294920 | tf_op jit(solution)/shard_map/ppermute | solution.py:31
  52.0 7.8 %collective-permute-start.17 = (bf16[32,1088]{1,0:T(8,128)(2,1)S(1)}, bf16[32,1088]{1,0:T(8,128)(2,1)S(1)}, u32[]{:S(2)}, u32[]{:S(2)}) collective-permute-start(bf16[32,1088]{1,0:T(8,128)(2,1)S(1)} %get-tuple-element.68), channel_id=1, source_target_pairs={{0,16},{8,24},{16,0},{24,8},{1,17},{9,25},{17,1},{25,9},{2,18},{10... | collective-permute-start | bytes 208904 | tf_op jit(solution)/shard_map/ppermute | solution.py:31
  52.4 7.4 %collective-permute-start.18 = (bf16[32,1088]{1,0:T(8,128)(2,1)S(1)}, bf16[32,1088]{1,0:T(8,128)(2,1)S(1)}, u32[]{:S(2)}, u32[]{:S(2)}) collective-permute-start(bf16[32,1088]{1,0:T(8,128)(2,1)S(1)} %get-tuple-element.69), channel_id=1, source_target_pairs={{0,24},{8,16},{16,8},{24,0},{1,25},{9,17},{17,9},{25,1},{2,26},{10... | collective-permute-start | bytes 208904 | tf_op jit(solution)/shard_map/ppermute | solution.py:31
  54.9 5.4 %collective-permute-start.19 = (bf16[32,1088]{1,0:T(8,128)(2,1)S(1)}, bf16[32,1088]{1,0:T(8,128)(2,1)S(1)}, u32[]{:S(2)}, u32[]{:S(2)}) collective-permute-start(bf16[32,1088]{1,0:T(8,128)(2,1)S(1)} %get-tuple-element.70), channel_id=1, source_target_pairs={{0,8},{8,0},{16,24},{24,16},{1,9},{9,1},{17,25},{25,17},{2,10},{10... | collective-permute-start | bytes 208904 | tf_op jit(solution)/shard_map/ppermute | solution.py:31

commit v3 on v2

--- a/solution.py
+++ b/solution.py
@@ -112,7 +112,7 @@
 
 
 def gate_body(sizes, *refs):
-    outs = refs[-1 - len(sizes) :]
+    outs = refs[-len(sizes) :]
     at = 0
     for size, out_ref in zip(sizes, outs):
         start = 0
@@ -120,21 +120,20 @@
             out_ref[start : start + ref.shape[0], :] = ref[...]
             start += ref.shape[0]
         at += size
-    outs[-1][...] = refs[at][...]
-
-
-def gate(groups, inputs, after):
+
+
+def gate(groups, after=()):
     sizes = [len(group) for group in groups]
     blocks = [block for group in groups for block in group]
     shapes = [jax.ShapeDtypeStruct((sum(b.shape[0] for b in group), group[0].shape[1]), BF16) for group in groups]
     return pl.pallas_call(
         lambda *refs: gate_body(sizes, *refs),
-        in_specs=[VMEM] * (len(blocks) + 1) + [ANY] * len(after),
-        out_specs=(VMEM,) * (len(groups) + 1),
-        out_shape=tuple(shapes) + (jax.ShapeDtypeStruct(inputs.shape, BF16),),
+        in_specs=[VMEM] * len(blocks) + [ANY] * len(after),
+        out_specs=(VMEM,) * len(groups),
+        out_shape=tuple(shapes),
         compiler_params=params(),
         name="gate",
-    )(*blocks, inputs, *after)
+    )(*blocks, *after)
 
 
 def rows_body(own_rows, count, *refs):
@@ -273,7 +272,7 @@
     ht_ref[...] = ht.astype(BF16)
 
 
-def prepare(xa, xb, w_first, share, order, after=()):
+def prepare(xa, xb, w_first, share, order, after):
     rows = 2 * xa.shape[0]
     width, hid = w_first.shape
     thin = jax.ShapeDtypeStruct((width // lax.axis_size("kc"), rows), BF16)
@@ -404,7 +403,7 @@
     line, deep, tall = lax.axis_size("kc"), lax.axis_size("enc"), lax.axis_size("kr")
     lines = deep * tall
     share = width // (line * lines)
-    order = [(2, 1), (3, 1), (1, 1), (0, 1), (2, 0), (3, 0), (1, 0), (0, 0)] if (deep, tall) == (4, 2) else None
+    order = [(2, 1), (3, 1), (1, 1), (2, 0), (3, 0), (1, 0), (0, 1), (0, 0)] if (deep, tall) == (4, 2) else None
     inv_row = inv_length[None, :]
     w2t = w_second.T
 
@@ -415,13 +414,13 @@
     tall_masks = range(1, tall)
     if order:
         z_two, z_one, y_own = swap(own, "enc", 2), swap(own, "enc", 1), swap(own, "kr", 1)
-        z_both, row_both, held = gate(([z_one, z_two], [own, far_row]), inputs, (y_own, group_a[1]))
+        z_both, row_both = gate(([z_one, z_two], [own, far_row]), (y_own, group_a[1]))
         core_both = swap(row_both, "kc", 1)
         calls = [
             ([row_both, y_own], [1, 1]),
             ([z_one, z_two], [1, 1]),
             ([swap(z_both, "kr", 1)], [2]),
-            ([swap(z_two, "enc", 1), swap_both(own, 3, 1)], [1, 1]),
+            ([swap(z_two, "enc", 1), swap(y_own, "enc", 3)], [1, 1]),
         ]
     else:
         columns = [own]
@@ -430,28 +429,28 @@
             columns = columns + [swap(block, "enc", mask) for block in columns]
             mask //= 2
         calls = [([block] + [swap(block, "kr", m) for m in tall_masks], [1] * tall) for block in columns]
-        row_both, held = gate(([own, far_row],), inputs, ())
+        (row_both,) = gate(([own, far_row],))
         core_both = swap(row_both, "kc", 1)
     rowa, rsp = group_rows(own_rows, [row_both, core_both])
-    x_far = swap(held, "kc", 2)
+    x_far = swap(hold(inputs, (core_both,)), "kc", 2)
 
     sofar = None
     for i, (blocks, counts) in enumerate(calls):
         sofar = pairs(own_rows, rowa, rsp, blocks, counts, sofar, i == len(calls) - 1)
     stay, gone, keep, send = sofar
-    x_both = swap(hold(x_far, (send,)), "kc", 1)
+    term = keep + swap(send, "kc", 1)
+    x_both = swap(hold(x_far, (term,)), "kc", 1)
     group_b = prepare(x_far, x_both, w_first, share, order, (send,))
-    term = keep + swap(send, "kc", 1)
     lscale = loss_gain / math.sqrt(probe_width)
     dfeat = finish(-lscale, term, swap(term, "kc", 2), inv_row, (group_b[1],))
     other = swap(dfeat, "kc", 1)
     stay = stay + swap(hold(gone, (term,)), "kc", 1)
-    sizes = [share * n for n in (4, 1, 1, 1, 1)] if order else [width // line]
+    sizes = [share * n for n in (3, 1, 1, 1, 1, 1)] if order else [width // line]
     parts = grads(dfeat, other, w2t, group_a, group_b, sizes)
     far = swap(hold(stay[own_rows:], (parts[0],)), "kc", 2)
     if order:
-        two, three, one, here = relay(swap(parts[0], "kr", 1), parts[1:], (BF16, BF16, BF16, F32), (far,))
-        got = [here, swap(two, "enc", 2), swap(three, "enc", 3), swap(one, "enc", 1)]
+        two, three, one = relay(swap(parts[0], "kr", 1), parts[1:4], (BF16,) * 3, (far,))
+        got = [parts[5], swap(two, "enc", 2), swap(three, "enc", 3), swap(one, "enc", 1), swap(parts[4], "kr", 1)]
     else:
         flat = lax.all_to_all(parts[0], ("enc", "kr"), 0, 0, tiled=True)
         got = list(flat.astype(F32).reshape(lines, share, hid + feat))

time: 61.2 us -> 58 us (0.948)
  waiting for transfers between devices: 21.3 us -> 17.3 us
  local copies, waits for them, and re-layouts: 0.03 us -> 0.95 us
  Pallas kernels: 17.8 us -> 16.9 us
  starting transfers between devices: 20.3 us -> 21.2 us
    ppermute x19 -> x21, waiting for transfers between devices: 21.3 us -> 17.3 us  [swap(): return lax.ppermute(x, axis, [(i, i ^ mask) for i in range(size)])]
    ppermute x19 -> x21, starting transfers between devices: 17.3 us -> 21.2 us  [swap(): return lax.ppermute(x, axis, [(i, i ^ mask) for i in range(size)])]
    ppermute x1 -> x0, starting transfers between devices: 3 us -> none  [swap_both(): return lax.ppermute(x, ('enc', 'kr'), pairs_of)]
    pallas_call x1, Pallas kernels: 0.96 us -> 0.03 us  [gate(): pl.pallas_call(lambda *refs: gate_body(sizes, *refs), in_specs=[VMEM] * l...]
    unnamed x8 -> x12, local copies, waits for them, and re-layouts: 0.02 us -> 0.94 us
  transfers between devices with their start and end apart: 20 -> 21, of which waited for: 9 -> 13; matrix products, arithmetic and copies ran while one was open for 1% -> 1% of each run, Pallas kernels for 26% -> 28%
where the time goes in v3:
time: 58 us; the launch traced here: 57.8 us
  starting transfers between devices  21.2 us (37%)
  waiting for transfers between devices  17.3 us (30%)
  Pallas kernels  16.9 us (29%)
  local copies, waits for them, and re-layouts  0.95 us (2%)
  between operations  0.87 us (2%)
  other arithmetic  0.67 us (1%)
    ppermute x21, starting transfers between devices, swap(): return lax.ppermute(x, axis, [(i, i ^ mask) for i in range(size)])  21.2 us
    ppermute x21, waiting for transfers between devices, swap(): return lax.ppermute(x, axis, [(i, i ^ mask) for i in range(size)])  17.3 us
    pallas_call x4, Pallas kernels, pairs(): pl.pallas_call(lambda *refs: pair_body(own_rows, counts, first, last, *re...  5.48 us
    pallas_call x2, Pallas kernels, prepare(): pl.pallas_call(lambda *refs: prepare_body(share, order, *refs), in_specs=...  4.76 us
    pallas_call x1, Pallas kernels, encode(): pl.pallas_call(encode_body, in_specs=[HBM] * 6, out_specs=VMEM, out_shape...  3.73 us
    pallas_call x1, Pallas kernels, grads(): pl.pallas_call(lambda *refs: grads_body(sizes, *refs), in_specs=[VMEM] *...  1.41 us
  transfers between devices with their start and end apart: 21, of which 13 were waited for; matrix products, arithmetic and copies ran while one was open for 1% of the time, Pallas kernels for 28%

profile of v3, /device:TPU:0, one launch (start us, length us, event | category | flops | bytes accessed | tf_op | source)
XLA Modules:
  0.0 57.8 jit_solution(4781667137195342109)
XLA Ops:
  0.6 0.0 copy-start.1
  0.6 0.0 copy-start
  0.7 0.5 collective-permute-start.4
  1.2 3.7 %encode.1.refs_3_.refs_2_ = bf16[480,128]{1,0:T(8,128)(2,1)} custom-call(bf16[192,1024]{1,0:T(8,128)(2,1)} %x_ref.1, bf16[1024,1024]{1,0:T(8,128)(2,1)} %refs_2_.3, bf16[64,1024]{1,0:T(8,128)(2,1)} %bitcast.2, f32[1,64]{1,0:T(1,128)} %bitcast.4, bf16[192,128]{1,0:T(8,128)(2,1)} %probe_hbm.1, bf16[192,128]{1,0:T(8,128)(2,1)} %solve_hbm.1), custom_call_target="tpu_custom_call" | custom-call | tf_op jit(solution)/shard_map/encode/pallas_call | solution.py:86
  4.9 3.6 %collective-permute-start.1 = (bf16[480,128]{1,0:T(8,128)(2,1)}, bf16[480,128]{1,0:T(8,128)(2,1)S(1)}, u32[]{:S(2)}, u32[]{:S(2)}) collective-permute-start(bf16[480,128]{1,0:T(8,128)(2,1)} %encode.1.refs_3_.refs_2_), channel_id=1, source_target_pairs={{0,16},{8,24},{16,0},{24,8},{1,17},{9,25},{17,1},{25,9},{2,18},{10... | collective-permute-start | bytes 368648 | tf_op jit(solution)/shard_map/ppermute | solution.py:31
  8.5 1.5 %collective-permute-start.3 = (bf16[480,128]{1,0:T(8,128)(2,1)}, bf16[480,128]{1,0:T(8,128)(2,1)S(1)}, u32[]{:S(2)}, u32[]{:S(2)}) collective-permute-start(bf16[480,128]{1,0:T(8,128)(2,1)} %encode.1.refs_3_.refs_2_), channel_id=1, source_target_pairs={{0,4},{4,0},{1,5},{5,1},{2,6},{6,2},{3,7},{7,3},{8,12},{12,8},{9,1... | collective-permute-start | bytes 368648 | tf_op jit(solution)/shard_map/ppermute | solution.py:31
  10.0 1.6 %collective-permute-start = (bf16[480,128]{1,0:T(8,128)(2,1)}, bf16[480,128]{1,0:T(8,128)(2,1)S(1)}, u32[]{:S(2)}, u32[]{:S(2)}) collective-permute-start(bf16[480,128]{1,0:T(8,128)(2,1)} %encode.1.refs_3_.refs_2_), channel_id=1, source_target_pairs={{0,8},{8,0},{16,24},{24,16},{1,9},{9,1},{17,25},{25,17},{2,10},{10... | collective-permute-start | bytes 368648 | tf_op jit(solution)/shard_map/ppermute | solution.py:31
  11.6 1.5 %collective-permute-start.2 = (bf16[480,128]{1,0:T(8,128)(2,1)}, bf16[480,128]{1,0:T(8,128)(2,1)S(1)}, u32[]{:S(2)}, u32[]{:S(2)}) collective-permute-start(bf16[480,128]{1,0:T(8,128)(2,1)} %encode.1.refs_3_.refs_2_), channel_id=1, source_target_pairs={{0,2},{1,3},{2,0},{3,1},{4,6},{5,7},{6,4},{7,5},{8,10},{9,11},{10,... | collective-permute-start | bytes 368648 | tf_op jit(solution)/shard_map/ppermute | solution.py:31
  13.1 0.0 collective-permute-done.4.refs_1_
  13.1 0.0 copy-done.1
  13.1 0.0 copy-done
  13.1 0.0 copy-start.2
  13.1 0.9 %copy-done.2 = bf16[480,128]{1,0:T(8,128)(2,1)S(1)} copy-done((bf16[480,128]{1,0:T(8,128)(2,1)S(1)}, bf16[480,128]{1,0:T(8,128)(2,1)}, u32[]{:S(2)}) %copy-start.2) | copy-done | bytes 122904
  14.0 2.4 %prepare.2 = (f32[384,1024]{1,0:T(8,128)S(1)}, bf16[256,384]{1,0:T(8,128)(2,1)S(1)}, bf16[256,384]{1,0:T(8,128)(2,1)S(1)}) custom-call(bf16[192,1024]{1,0:T(8,128)(2,1)S(1)} %copy-done.1, bf16[192,1024]{1,0:T(8,128)(2,1)S(1)} %collective-permute-done.4.refs_1_, bf16[1024,1024]{1,0:T(8,128)(2,1)S(1)} %copy-done, bf16[480,128]{1,0:T(8,128)(2,1)S(1)} %copy-done.2), custom_call_target="tpu_custom_call" | custom-call | flops 1 | bytes 1048576 | tf_op jit(solution)/shard_map/prepare/pallas_call | solution.py:279
  16.4 0.0 collective-permute-done.1.refs_1_.refs_3_
  16.4 0.0 collective-permute-done.3.refs_4_.refs_3_
  16.4 0.3 collective-permute-done.refs_0_.refs_2_
  16.7 0.0 collective-permute-done.2.refs_3_
  16.8 0.1 collective-permute-start.5
  16.9 1.5 %collective-permute-done.5.refs_1_.refs_0_ = bf16[960,128]{1,0:T(8,128)(2,1)S(1)} collective-permute-done((bf16[960,128]{1,0:T(8,128)(2,1)S(1)}, bf16[960,128]{1,0:T(8,128)(2,1)S(1)}, u32[]{:S(2)}, u32[]{:S(2)}) %collective-permute-start.5) | collective-permute-done | bytes 245792 | tf_op jit(solution)/shard_map/ppermute | solution.py:31
  18.4 1.6 %collective-permute-start.12 = (bf16[192,1024]{1,0:T(8,128)(2,1)S(1)}, bf16[192,1024]{1,0:T(8,128)(2,1)S(1)}, u32[]{:S(2)}, u32[]{:S(2)}) collective-permute-start(bf16[192,1024]{1,0:T(8,128)(2,1)S(1)} %hold.5), channel_id=1, source_target_pairs={{0,2},{1,3},{2,0},{3,1},{4,6},{5,7},{6,4},{7,5},{8,10},{9,11},{10,... | collective-permute-start | bytes 1179656 | tf_op jit(solution)/shard_map/ppermute | solution.py:31
  20.0 0.5 collective-permute-start.8
  20.5 1.2 %collective-permute-start.6 = (bf16[480,128]{1,0:T(8,128)(2,1)S(1)}, bf16[480,128]{1,0:T(8,128)(2,1)S(1)}, u32[]{:S(2)}, u32[]{:S(2)}) collective-permute-start(bf16[480,128]{1,0:T(8,128)(2,1)S(1)} %collective-permute-done.1.refs_1_.refs_3_), channel_id=1, source_target_pairs={{0,8},{8,0},{16,24},{24,16},{1,9},{9,1},{17,25},{25,17},{2,10},{10... | collective-permute-start | bytes 368648 | tf_op jit(solution)/shard_map/ppermute | solution.py:31
  21.7 1.8 %collective-permute-start.7 = (bf16[480,128]{1,0:T(8,128)(2,1)S(1)}, bf16[480,128]{1,0:T(8,128)(2,1)S(1)}, u32[]{:S(2)}, u32[]{:S(2)}) collective-permute-start(bf16[480,128]{1,0:T(8,128)(2,1)S(1)} %collective-permute-done.3.refs_4_.refs_3_), channel_id=1, source_target_pairs={{0,24},{8,16},{16,8},{24,0},{1,25},{9,17},{17,9},{25,1},{2,26},{10... | collective-permute-start | bytes 368648 | tf_op jit(solution)/shard_map/ppermute | solution.py:31
  23.5 0.5 rows.1
  24.0 1.3 %pairs.4 = (f32[768,128]{1,0:T(8,128)S(1)}, f32[768,64]{1,0:T(8,128)S(1)}, f32[768,128]{1,0:T(8,128)S(1)}) custom-call(bf16[768,256]{1,0:T(8,128)(2,1)S(1)} %get-tuple-element.39.refs_0_, bf16[768,256]{1,0:T(8,128)(2,1)S(1)} %get-tuple-element.40.refs_1_, bf16[960,128]{1,0:T(8,128)(2,1)S(1)} %get-tuple-element.38.refs_0_.refs_2_, ...), custom_call_target="tpu_custom_call" | custom-call | flops 1 | bytes 884736 | tf_op jit(solution)/shard_map/pairs/pallas_call | solution.py:230
  25.4 1.4 %pairs.5 = (f32[768,128]{1,0:T(8,128)S(1)}, f32[768,64]{1,0:T(8,128)S(1)}, f32[768,128]{1,0:T(8,128)S(1)}) custom-call(bf16[768,256]{1,0:T(8,128)(2,1)S(1)} %get-tuple-element.39.refs_0_, bf16[768,256]{1,0:T(8,128)(2,1)S(1)} %get-tuple-element.40.refs_1_, bf16[480,128]{1,0:T(8,128)(2,1)S(1)} %collective-permute-done.refs_0_.refs_2_, ...), custom_call_target="tpu_custom_call" | custom-call | flops 1 | bytes 884736 | tf_op jit(solution)/shard_map/pairs/pallas_call | solution.py:230
  26.7 1.0 %collective-permute-done.8.refs_2_ = bf16[960,128]{1,0:T(8,128)(2,1)S(1)} collective-permute-done((bf16[960,128]{1,0:T(8,128)(2,1)S(1)}, bf16[960,128]{1,0:T(8,128)(2,1)S(1)}, u32[]{:S(2)}, u32[]{:S(2)}) %collective-permute-start.8) | collective-permute-done | bytes 245792 | tf_op jit(solution)/shard_map/ppermute | solution.py:31
  27.7 1.4 %pairs.6 = (f32[768,128]{1,0:T(8,128)S(1)}, f32[768,64]{1,0:T(8,128)S(1)}, f32[768,128]{1,0:T(8,128)S(1)}) custom-call(bf16[768,256]{1,0:T(8,128)(2,1)S(1)} %get-tuple-element.39.refs_0_, bf16[768,256]{1,0:T(8,128)(2,1)S(1)} %get-tuple-element.40.refs_1_, bf16[960,128]{1,0:T(8,128)(2,1)S(1)} %collective-permute-done.8.refs_2_, ...), custom_call_target="tpu_custom_call" | custom-call | flops 1 | bytes 884736 | tf_op jit(solution)/shard_map/pairs/pallas_call | solution.py:230
  29.1 0.0 collective-permute-done.6.refs_2_
  29.1 0.2 collective-permute-done.7.refs_3_
  29.3 1.4 %pairs.7 = (f32[384,128]{1,0:T(8,128)S(1)}, f32[384,128]{1,0:T(8,128)S(1)}, f32[192,128]{1,0:T(8,128)S(1)}, f32[192,128]{1,0:T(8,128)S(1)}) custom-call(bf16[768,256]{1,0:T(8,128)(2,1)S(1)} %get-tuple-element.39.refs_0_, bf16[768,256]{1,0:T(8,128)(2,1)S(1)} %get-tuple-element.40.refs_1_, bf16[480,128]{1,0:T(8,128)(2,1)S(1)} %collective-permute-done.6.refs_2_, ...), custom_call_target="tpu_custom_call" | custom-call | flops 1 | bytes 884736 | tf_op jit(solution)/shard_map/pairs/pallas_call | solution.py:230
  30.7 0.1 collective-permute-start.9
  30.8 1.3 %collective-permute-done.9 = f32[192,128]{1,0:T(8,128)S(1)} collective-permute-done((f32[192,128]{1,0:T(8,128)S(1)}, f32[192,128]{1,0:T(8,128)S(1)}, u32[]{:S(2)}, u32[]{:S(2)}) %collective-permute-start.9) | collective-permute-done | bytes 98336 | tf_op jit(solution)/shard_map/ppermute | solution.py:31
  32.1 0.0 collective-permute-done.12.x_ref.refs_0_
  32.1 0.2 collective-permute-start.13
  32.4 0.6 collective-permute-start.11
  32.9 0.0 copy-start.5
  32.9 0.0 copy-start.4
  32.9 0.1 collective-permute-start.10
  33.1 0.8 %collective-permute-done.13.refs_1_ = bf16[192,1024]{1,0:T(8,128)(2,1)S(1)} collective-permute-done((bf16[192,1024]{1,0:T(8,128)(2,1)S(1)}, bf16[192,1024]{1,0:T(8,128)(2,1)S(1)}, u32[]{:S(2)}, u32[]{:S(2)}) %collective-permute-start.13) | collective-permute-done | bytes 393248 | tf_op jit(solution)/shard_map/ppermute | solution.py:31
  33.9 2.4 %prepare.3 = (f32[384,1024]{1,0:T(8,128)S(1)}, bf16[256,384]{1,0:T(8,128)(2,1)S(1)}, bf16[256,384]{1,0:T(8,128)(2,1)S(1)}) custom-call(bf16[192,1024]{1,0:T(8,128)(2,1)S(1)} %collective-permute-done.12.x_ref.refs_0_, bf16[192,1024]{1,0:T(8,128)(2,1)S(1)} %collective-permute-done.13.refs_1_, bf16[1024,1024]{1,0:T(8,128)(2,1)S(1)} %copy-done, ...), custom_call_target="tpu_custom_call" | custom-call | flops 1 | bytes 1048576 | tf_op jit(solution)/shard_map/prepare/pallas_call | solution.py:279
  36.3 1.1 %collective-permute-done.11.refs_1_ = f32[192,128]{1,0:T(8,128)S(1)} collective-permute-done((f32[192,128]{1,0:T(8,128)S(1)}, f32[192,128]{1,0:T(8,128)S(1)}, u32[]{:S(2)}, u32[]{:S(2)}) %collective-permute-start.11) | collective-permute-done | bytes 98336 | tf_op jit(solution)/shard_map/ppermute | solution.py:31
  37.4 0.0 copy-done.5
  37.4 0.1 finish.1.refs_0_
  37.5 0.1 collective-permute-start.14
  37.6 1.2 %collective-permute-done.14.refs_1_ = bf16[192,128]{1,0:T(8,128)(2,1)S(1)} collective-permute-done((bf16[192,128]{1,0:T(8,128)(2,1)S(1)}, bf16[192,128]{1,0:T(8,128)(2,1)S(1)}, u32[]{:S(2)}, u32[]{:S(2)}) %collective-permute-start.14) | collective-permute-done | bytes 49184 | tf_op jit(solution)/shard_map/ppermute | solution.py:31
  38.8 1.4 %grads.1 = (bf16[96,1088]{1,0:T(8,128)(2,1)S(1)}, bf16[32,1088]{1,0:T(8,128)(2,1)S(1)}, bf16[32,1088]{1,0:T(8,128)(2,1)S(1)}, bf16[32,1088]{1,0:T(8,128)(2,1)S(1...) custom-call(bf16[192,128]{1,0:T(8,128)(2,1)S(1)} %finish.1.refs_0_, ...), custom_call_target="tpu_custom_call" | custom-call | tf_op jit(solution)/shard_map/grads/pallas_call | solution.py:332
  40.2 1.0 %collective-permute-start.16 = (bf16[96,1088]{1,0:T(8,128)(2,1)S(1)}, bf16[96,1088]{1,0:T(8,128)(2,1)S(1)}, u32[]{:S(2)}, u32[]{:S(2)}) collective-permute-start(bf16[96,1088]{1,0:T(8,128)(2,1)S(1)} %get-tuple-element.60.refs_0_), channel_id=1, source_target_pairs={{0,4},{4,0},{1,5},{5,1},{2,6},{6,2},{3,7},{7,3},{8,12},{12,8},{9,1... | collective-permute-start | bytes 626696 | tf_op jit(solution)/shard_map/ppermute | solution.py:31
  41.3 0.0 collective-permute-done.10
  41.3 0.6 %collective-permute-start.15 = (f32[192,128]{1,0:T(8,128)S(1)}, f32[192,128]{1,0:T(8,128)S(1)}, u32[]{:S(2)}, u32[]{:S(2)}) collective-permute-start(f32[192,128]{1,0:T(8,128)S(1)} %hold.7), channel_id=1, source_target_pairs={{0,2},{1,3},{2,0},{3,1},{4,6},{5,7},{6,4},{7,5},{8,10},{9,11},{10,... | collective-permute-start | bytes 294920 | tf_op jit(solution)/shard_map/ppermute | solution.py:31
  41.9 1.1 %collective-permute-start.20 = (bf16[32,1088]{1,0:T(8,128)(2,1)S(1)}, bf16[32,1088]{1,0:T(8,128)(2,1)S(1)}, u32[]{:S(2)}, u32[]{:S(2)}) collective-permute-start(bf16[32,1088]{1,0:T(8,128)(2,1)S(1)} %get-tuple-element.68), channel_id=1, source_target_pairs={{0,4},{4,0},{1,5},{5,1},{2,6},{6,2},{3,7},{7,3},{8,12},{12,8},{9,1... | collective-permute-start | bytes 208904 | tf_op jit(solution)/shard_map/ppermute | solution.py:31
  43.0 3.0 %collective-permute-done.15.refs_4_ = f32[192,128]{1,0:T(8,128)S(1)} collective-permute-done((f32[192,128]{1,0:T(8,128)S(1)}, f32[192,128]{1,0:T(8,128)S(1)}, u32[]{:S(2)}, u32[]{:S(2)}) %collective-permute-start.15) | collective-permute-done | bytes 98336 | tf_op jit(solution)/shard_map/ppermute | solution.py:31
  46.0 2.5 %collective-permute-done.16.refs_0_ = bf16[96,1088]{1,0:T(8,128)(2,1)S(1)} collective-permute-done((bf16[96,1088]{1,0:T(8,128)(2,1)S(1)}, bf16[96,1088]{1,0:T(8,128)(2,1)S(1)}, u32[]{:S(2)}, u32[]{:S(2)}) %collective-permute-start.16) | collective-permute-done | bytes 208928 | tf_op jit(solution)/shard_map/ppermute | solution.py:31
  48.6 0.1 relay.1
  48.6 2.0 %collective-permute-start.17 = (bf16[32,1088]{1,0:T(8,128)(2,1)S(1)}, bf16[32,1088]{1,0:T(8,128)(2,1)S(1)}, u32[]{:S(2)}, u32[]{:S(2)}) collective-permute-start(bf16[32,1088]{1,0:T(8,128)(2,1)S(1)} %get-tuple-element.65), channel_id=1, source_target_pairs={{0,16},{8,24},{16,0},{24,8},{1,17},{9,25},{17,1},{25,9},{2,18},{10... | collective-permute-start | bytes 208904 | tf_op jit(solution)/shard_map/ppermute | solution.py:31
  50.6 1.2 %collective-permute-start.18 = (bf16[32,1088]{1,0:T(8,128)(2,1)S(1)}, bf16[32,1088]{1,0:T(8,128)(2,1)S(1)}, u32[]{:S(2)}, u32[]{:S(2)}) collective-permute-start(bf16[32,1088]{1,0:T(8,128)(2,1)S(1)} %get-tuple-element.66), channel_id=1, source_target_pairs={{0,24},{8,16},{16,8},{24,0},{1,25},{9,17},{17,9},{25,1},{2,26},{10... | collective-permute-start | bytes 208904 | tf_op jit(solution)/shard_map/ppermute | solution.py:31
  51.8 0.4 collective-permute-start.19
  52.2 0.6 %fusion.1 = bf16[192,128]{1,0:T(8,128)(2,1)} fusion(f32[192,128]{1,0:T(8,128)S(1)} %collective-permute-done.15.refs_4_, f32[384,128]{1,0:T(8,128)S(1)} %add.10), kind=kLoop, calls=%fused_computation.2 | loop fusion | flops 73728 | bytes 245760 | tf_op jit(solution)/shard_map/convert_element_type | solution.py:460
  52.8 0.0 collective-permute-done.20.refs_4_
  52.8 2.7 %collective-permute-done.17.refs_1_ = bf16[32,1088]{1,0:T(8,128)(2,1)S(1)} collective-permute-done((bf16[32,1088]{1,0:T(8,128)(2,1)S(1)}, bf16[32,1088]{1,0:T(8,128)(2,1)S(1)}, u32[]{:S(2)}, u32[]{:S(2)}) %collective-permute-start.17) | collective-permute-done | bytes 69664 | tf_op jit(solution)/shard_map/ppermute | solution.py:31
  55.5 1.4 %collective-permute-done.18.refs_2_ = bf16[32,1088]{1,0:T(8,128)(2,1)S(1)} collective-permute-done((bf16[32,1088]{1,0:T(8,128)(2,1)S(1)}, bf16[32,1088]{1,0:T(8,128)(2,1)S(1)}, u32[]{:S(2)}, u32[]{:S(2)}) %collective-permute-start.18) | collective-permute-done | bytes 69664 | tf_op jit(solution)/shard_map/ppermute | solution.py:31
  56.9 0.2 collective-permute-done.19.refs_3_
  57.1 0.7 %total.1 = (f32[32,1024]{1,0:T(8,128)}, f32[32,64]{1,0:T(8,128)}) custom-call(bf16[32,1088]{1,0:T(8,128)(2,1)S(1)} %get-tuple-element.61.refs_0_, bf16[32,1088]{1,0:T(8,128)(2,1)S(1)} %collective-permute-done.17.refs_1_, bf16[32,1088]{1,0:T(8,128)(2,1)S(1)} %collective-permute-done.18.refs_2_, bf16[32,1088]{1,0:T(8,128)(2,1)S(1)} %collective-permute-done.19.refs_3_, ...), custom_call_target="tpu_custom_call" | custom-call | tf_op jit(solution)/shard_map/total/pallas_call | solution.py:374
  (11 shorter events, 0.2 us)
Async XLA Ops:
  0.6 12.5 %copy-start.1 = (bf16[192,1024]{1,0:T(8,128)(2,1)S(1)}, bf16[192,1024]{1,0:T(8,128)(2,1)}, u32[]{:S(2)}) copy-start(bf16[192,1024]{1,0:T(8,128)(2,1)} %x_ref.1) | copy-start | bytes 1179652
  0.6 12.5 %copy-start = (bf16[1024,1024]{1,0:T(8,128)(2,1)S(1)}, bf16[1024,1024]{1,0:T(8,128)(2,1)}, u32[]{:S(2)}) copy-start(bf16[1024,1024]{1,0:T(8,128)(2,1)} %refs_2_.3) | copy-start | bytes 6291460
  0.7 12.5 %collective-permute-start.4 = (bf16[192,1024]{1,0:T(8,128)(2,1)}, bf16[192,1024]{1,0:T(8,128)(2,1)S(1)}, u32[]{:S(2)}, u32[]{:S(2)}) collective-permute-start(bf16[192,1024]{1,0:T(8,128)(2,1)} %x_ref.1), channel_id=1, source_target_pairs={{0,1},{1,0},{2,3},{3,2},{4,5},{5,4},{6,7},{7,6},{8,9},{9,8},{10,11... | collective-permute-start | bytes 1179656 | tf_op jit(solution)/shard_map/ppermute | solution.py:31
  4.9 11.5 %collective-permute-start.1 = (bf16[480,128]{1,0:T(8,128)(2,1)}, bf16[480,128]{1,0:T(8,128)(2,1)S(1)}, u32[]{:S(2)}, u32[]{:S(2)}) collective-permute-start(bf16[480,128]{1,0:T(8,128)(2,1)} %encode.1.refs_3_.refs_2_), channel_id=1, source_target_pairs={{0,16},{8,24},{16,0},{24,8},{1,17},{9,25},{17,1},{25,9},{2,18},{10... | collective-permute-start | bytes 368648 | tf_op jit(solution)/shard_map/ppermute | solution.py:31
  8.5 7.9 %collective-permute-start.3 = (bf16[480,128]{1,0:T(8,128)(2,1)}, bf16[480,128]{1,0:T(8,128)(2,1)S(1)}, u32[]{:S(2)}, u32[]{:S(2)}) collective-permute-start(bf16[480,128]{1,0:T(8,128)(2,1)} %encode.1.refs_3_.refs_2_), channel_id=1, source_target_pairs={{0,4},{4,0},{1,5},{5,1},{2,6},{6,2},{3,7},{7,3},{8,12},{12,8},{9,1... | collective-permute-start | bytes 368648 | tf_op jit(solution)/shard_map/ppermute | solution.py:31
  10.0 6.7 %collective-permute-start = (bf16[480,128]{1,0:T(8,128)(2,1)}, bf16[480,128]{1,0:T(8,128)(2,1)S(1)}, u32[]{:S(2)}, u32[]{:S(2)}) collective-permute-start(bf16[480,128]{1,0:T(8,128)(2,1)} %encode.1.refs_3_.refs_2_), channel_id=1, source_target_pairs={{0,8},{8,0},{16,24},{24,16},{1,9},{9,1},{17,25},{25,17},{2,10},{10... | collective-permute-start | bytes 368648 | tf_op jit(solution)/shard_map/ppermute | solution.py:31
  11.6 5.1 %collective-permute-start.2 = (bf16[480,128]{1,0:T(8,128)(2,1)}, bf16[480,128]{1,0:T(8,128)(2,1)S(1)}, u32[]{:S(2)}, u32[]{:S(2)}) collective-permute-start(bf16[480,128]{1,0:T(8,128)(2,1)} %encode.1.refs_3_.refs_2_), channel_id=1, source_target_pairs={{0,2},{1,3},{2,0},{3,1},{4,6},{5,7},{6,4},{7,5},{8,10},{9,11},{10,... | collective-permute-start | bytes 368648 | tf_op jit(solution)/shard_map/ppermute | solution.py:31
  13.1 0.9 %copy-start.2 = (bf16[480,128]{1,0:T(8,128)(2,1)S(1)}, bf16[480,128]{1,0:T(8,128)(2,1)}, u32[]{:S(2)}) copy-start(bf16[480,128]{1,0:T(8,128)(2,1)} %encode.1.refs_3_.refs_2_) | copy-start | bytes 368644
  14.0 2.7 %copy-start.3 = (bf16[480,128]{1,0:T(8,128)(2,1)S(1)}, bf16[480,128]{1,0:T(8,128)(2,1)}, u32[]{:S(2)}) copy-start(bf16[480,128]{1,0:T(8,128)(2,1)} %encode.1.refs_3_.refs_2_) | copy-start | bytes 368644
  16.8 1.6 %collective-permute-start.5 = (bf16[960,128]{1,0:T(8,128)(2,1)S(1)}, bf16[960,128]{1,0:T(8,128)(2,1)S(1)}, u32[]{:S(2)}, u32[]{:S(2)}) collective-permute-start(bf16[960,128]{1,0:T(8,128)(2,1)S(1)} %get-tuple-element.38.refs_0_.refs_2_), channel_id=1, source_target_pairs={{0,1},{1,0},{2,3},{3,2},{4,5},{5,4},{6,7},{7,6},{8,9},{9,8},{10,11... | collective-permute-start | bytes 737288 | tf_op jit(solution)/shard_map/ppermute | solution.py:31
  18.4 13.7 %collective-permute-start.12 = (bf16[192,1024]{1,0:T(8,128)(2,1)S(1)}, bf16[192,1024]{1,0:T(8,128)(2,1)S(1)}, u32[]{:S(2)}, u32[]{:S(2)}) collective-permute-start(bf16[192,1024]{1,0:T(8,128)(2,1)S(1)} %hold.5), channel_id=1, source_target_pairs={{0,2},{1,3},{2,0},{3,1},{4,6},{5,7},{6,4},{7,5},{8,10},{9,11},{10,... | collective-permute-start | bytes 1179656 | tf_op jit(solution)/shard_map/ppermute | solution.py:31
  20.0 7.7 %collective-permute-start.8 = (bf16[960,128]{1,0:T(8,128)(2,1)S(1)}, bf16[960,128]{1,0:T(8,128)(2,1)S(1)}, u32[]{:S(2)}, u32[]{:S(2)}) collective-permute-start(bf16[960,128]{1,0:T(8,128)(2,1)S(1)} %get-tuple-element.41), channel_id=1, source_target_pairs={{0,4},{4,0},{1,5},{5,1},{2,6},{6,2},{3,7},{7,3},{8,12},{12,8},{9,1... | collective-permute-start | bytes 737288 | tf_op jit(solution)/shard_map/ppermute | solution.py:31
  20.5 8.6 %collective-permute-start.6 = (bf16[480,128]{1,0:T(8,128)(2,1)S(1)}, bf16[480,128]{1,0:T(8,128)(2,1)S(1)}, u32[]{:S(2)}, u32[]{:S(2)}) collective-permute-start(bf16[480,128]{1,0:T(8,128)(2,1)S(1)} %collective-permute-done.1.refs_1_.refs_3_), channel_id=1, source_target_pairs={{0,8},{8,0},{16,24},{24,16},{1,9},{9,1},{17,25},{25,17},{2,10},{10... | collective-permute-start | bytes 368648 | tf_op jit(solution)/shard_map/ppermute | solution.py:31
  21.7 7.6 %collective-permute-start.7 = (bf16[480,128]{1,0:T(8,128)(2,1)S(1)}, bf16[480,128]{1,0:T(8,128)(2,1)S(1)}, u32[]{:S(2)}, u32[]{:S(2)}) collective-permute-start(bf16[480,128]{1,0:T(8,128)(2,1)S(1)} %collective-permute-done.3.refs_4_.refs_3_), channel_id=1, source_target_pairs={{0,24},{8,16},{16,8},{24,0},{1,25},{9,17},{17,9},{25,1},{2,26},{10... | collective-permute-start | bytes 368648 | tf_op jit(solution)/shard_map/ppermute | solution.py:31
  30.7 1.4 %collective-permute-start.9 = (f32[192,128]{1,0:T(8,128)S(1)}, f32[192,128]{1,0:T(8,128)S(1)}, u32[]{:S(2)}, u32[]{:S(2)}) collective-permute-start(f32[192,128]{1,0:T(8,128)S(1)} %get-tuple-element.54.refs_3_), channel_id=1, source_target_pairs={{0,1},{1,0},{2,3},{3,2},{4,5},{5,4},{6,7},{7,6},{8,9},{9,8},{10,11... | collective-permute-start | bytes 294920 | tf_op jit(solution)/shard_map/ppermute | solution.py:31
  32.1 1.8 %collective-permute-start.13 = (bf16[192,1024]{1,0:T(8,128)(2,1)S(1)}, bf16[192,1024]{1,0:T(8,128)(2,1)S(1)}, u32[]{:S(2)}, u32[]{:S(2)}) collective-permute-start(bf16[192,1024]{1,0:T(8,128)(2,1)S(1)} %hold.6), channel_id=1, source_target_pairs={{0,1},{1,0},{2,3},{3,2},{4,5},{5,4},{6,7},{7,6},{8,9},{9,8},{10,11... | collective-permute-start | bytes 1179656 | tf_op jit(solution)/shard_map/ppermute | solution.py:31
  32.4 5.1 %collective-permute-start.11 = (f32[192,128]{1,0:T(8,128)S(1)}, f32[192,128]{1,0:T(8,128)S(1)}, u32[]{:S(2)}, u32[]{:S(2)}) collective-permute-start(f32[192,128]{1,0:T(8,128)S(1)} %add.9.refs_0_), channel_id=1, source_target_pairs={{0,2},{1,3},{2,0},{3,1},{4,6},{5,7},{6,4},{7,5},{8,10},{9,11},{10,... | collective-permute-start | bytes 294920 | tf_op jit(solution)/shard_map/ppermute | solution.py:31
  32.9 4.5 %copy-start.5 = (f32[64]{0:T(128)S(1)}, f32[64]{0:T(128)}, u32[]{:S(2)}) copy-start(f32[64]{0:T(128)} %param.9) | copy-start | bytes 772
  32.9 5.9 %copy-start.4 = (bf16[1024,64]{0,1:T(8,128)(2,1)S(1)}, bf16[1024,64]{0,1:T(8,128)(2,1)}, u32[]{:S(2)}) copy-start(bf16[1024,64]{0,1:T(8,128)(2,1)} %param.8) | copy-start | bytes 393220
  32.9 8.3 %collective-permute-start.10 = (f32[384,128]{1,0:T(8,128)S(1)}, f32[384,128]{1,0:T(8,128)S(1)}, u32[]{:S(2)}, u32[]{:S(2)}) collective-permute-start(f32[384,128]{1,0:T(8,128)S(1)} %hold.4), channel_id=1, source_target_pairs={{0,1},{1,0},{2,3},{3,2},{4,5},{5,4},{6,7},{7,6},{8,9},{9,8},{10,11... | collective-permute-start | bytes 589832 | tf_op jit(solution)/shard_map/ppermute | solution.py:31
  37.5 1.3 %collective-permute-start.14 = (bf16[192,128]{1,0:T(8,128)(2,1)S(1)}, bf16[192,128]{1,0:T(8,128)(2,1)S(1)}, u32[]{:S(2)}, u32[]{:S(2)}) collective-permute-start(bf16[192,128]{1,0:T(8,128)(2,1)S(1)} %finish.1.refs_0_), channel_id=1, source_target_pairs={{0,1},{1,0},{2,3},{3,2},{4,5},{5,4},{6,7},{7,6},{8,9},{9,8},{10,11... | collective-permute-start | bytes 147464 | tf_op jit(solution)/shard_map/ppermute | solution.py:31
  40.2 8.3 %collective-permute-start.16 = (bf16[96,1088]{1,0:T(8,128)(2,1)S(1)}, bf16[96,1088]{1,0:T(8,128)(2,1)S(1)}, u32[]{:S(2)}, u32[]{:S(2)}) collective-permute-start(bf16[96,1088]{1,0:T(8,128)(2,1)S(1)} %get-tuple-element.60.refs_0_), channel_id=1, source_target_pairs={{0,4},{4,0},{1,5},{5,1},{2,6},{6,2},{3,7},{7,3},{8,12},{12,8},{9,1... | collective-permute-start | bytes 626696 | tf_op jit(solution)/shard_map/ppermute | solution.py:31
  41.3 4.7 %collective-permute-start.15 = (f32[192,128]{1,0:T(8,128)S(1)}, f32[192,128]{1,0:T(8,128)S(1)}, u32[]{:S(2)}, u32[]{:S(2)}) collective-permute-start(f32[192,128]{1,0:T(8,128)S(1)} %hold.7), channel_id=1, source_target_pairs={{0,2},{1,3},{2,0},{3,1},{4,6},{5,7},{6,4},{7,5},{8,10},{9,11},{10,... | collective-permute-start | bytes 294920 | tf_op jit(solution)/shard_map/ppermute | solution.py:31
  41.9 10.9 %collective-permute-start.20 = (bf16[32,1088]{1,0:T(8,128)(2,1)S(1)}, bf16[32,1088]{1,0:T(8,128)(2,1)S(1)}, u32[]{:S(2)}, u32[]{:S(2)}) collective-permute-start(bf16[32,1088]{1,0:T(8,128)(2,1)S(1)} %get-tuple-element.68), channel_id=1, source_target_pairs={{0,4},{4,0},{1,5},{5,1},{2,6},{6,2},{3,7},{7,3},{8,12},{12,8},{9,1... | collective-permute-start | bytes 208904 | tf_op jit(solution)/shard_map/ppermute | solution.py:31
  48.6 6.9 %collective-permute-start.17 = (bf16[32,1088]{1,0:T(8,128)(2,1)S(1)}, bf16[32,1088]{1,0:T(8,128)(2,1)S(1)}, u32[]{:S(2)}, u32[]{:S(2)}) collective-permute-start(bf16[32,1088]{1,0:T(8,128)(2,1)S(1)} %get-tuple-element.65), channel_id=1, source_target_pairs={{0,16},{8,24},{16,0},{24,8},{1,17},{9,25},{17,1},{25,9},{2,18},{10... | collective-permute-start | bytes 208904 | tf_op jit(solution)/shard_map/ppermute | solution.py:31
  50.6 6.3 %collective-permute-start.18 = (bf16[32,1088]{1,0:T(8,128)(2,1)S(1)}, bf16[32,1088]{1,0:T(8,128)(2,1)S(1)}, u32[]{:S(2)}, u32[]{:S(2)}) collective-permute-start(bf16[32,1088]{1,0:T(8,128)(2,1)S(1)} %get-tuple-element.66), channel_id=1, source_target_pairs={{0,24},{8,16},{16,8},{24,0},{1,25},{9,17},{17,9},{25,1},{2,26},{10... | collective-permute-start | bytes 208904 | tf_op jit(solution)/shard_map/ppermute | solution.py:31
  51.8 5.3 %collective-permute-start.19 = (bf16[32,1088]{1,0:T(8,128)(2,1)S(1)}, bf16[32,1088]{1,0:T(8,128)(2,1)S(1)}, u32[]{:S(2)}, u32[]{:S(2)}) collective-permute-start(bf16[32,1088]{1,0:T(8,128)(2,1)S(1)} %get-tuple-element.67), channel_id=1, source_target_pairs={{0,8},{8,0},{16,24},{24,16},{1,9},{9,1},{17,25},{25,17},{2,10},{10... | collective-permute-start | bytes 208904 | tf_op jit(solution)/shard_map/ppermute | solution.py:31

commit v4 on v3

--- a/solution.py
+++ b/solution.py
@@ -12,7 +12,7 @@
 F32 = jnp.float32
 BF16 = jnp.bfloat16
 VMEM_LIMIT = 48 * 1024 * 1024
-VMEM_MOST = 60 * 1024 * 1024
+VMEM_MOST = 58 * 1024 * 1024
 VMEM = pl.BlockSpec(memory_space=pltpu.VMEM)
 HBM = pl.BlockSpec(memory_space=pltpu.HBM)
 ANY = pl.BlockSpec(memory_space=pl.ANY)
@@ -44,7 +44,7 @@
 def encode_body(x_hbm, w1_hbm, w2t_hbm, inv_hbm, probe_hbm, solve_hbm, out_ref, x_ref, w1_ref, w2t_ref, inv_ref, sems):
     rows, width = x_ref.shape
     hid = w1_ref.shape[1]
-    parts = 4
+    parts = 2
     block = hid // parts
     x_copy = pltpu.make_async_copy(x_hbm, x_ref, sems.at[0])
     w2_copy = pltpu.make_async_copy(w2t_hbm, w2t_ref, sems.at[1])
@@ -171,7 +171,7 @@
     if not first:
         v_in, m_in, s_in = refs[:3]
     if last:
-        v_ref, gone_ref, keep_ref, send_ref = refs[-4:]
+        v_ref, gone_ref, term_ref = refs[-3:]
     else:
         v_ref, m_ref, s_ref = refs[-3:]
     probe = v_ref.shape[1]
@@ -209,8 +209,8 @@
         gone_ref[...] = jnp.concatenate([v[2], v[3]], axis=0)
         t = jnp.sum(sums, axis=1, keepdims=True) * rowa_ref[:, :feat].astype(F32) - m
         t = [t[b * own_rows : (b + 1) * own_rows] for b in range(rows // own_rows)]
-        keep_ref[...] = jnp.concatenate([t[0], t[1]], axis=1)
-        send_ref[...] = jnp.concatenate([t[2], t[3]], axis=1)
+        term_ref[:own_rows, :] = jnp.concatenate([t[0], t[1]], axis=1)
+        term_ref[own_rows:, :] = jnp.concatenate([t[2], t[3]], axis=1)
     else:
         v_ref[...] = v
         m_ref[...] = m
@@ -225,13 +225,12 @@
     operands = [rowa, rsp] + list(col_blocks) + list(before or ())
     whole = jax.ShapeDtypeStruct((rows, probe), F32)
     half = jax.ShapeDtypeStruct((rows // 2, probe), F32)
-    quarter = jax.ShapeDtypeStruct((own_rows, probe), F32)
     thin = jax.ShapeDtypeStruct((rows, feat), F32)
     return pl.pallas_call(
         lambda *refs: pair_body(own_rows, counts, first, last, *refs),
         in_specs=[VMEM] * len(operands),
-        out_specs=(VMEM,) * (4 if last else 3),
-        out_shape=(half, half, quarter, quarter) if last else (whole, thin, jax.ShapeDtypeStruct((rows, 128), F32)),
+        out_specs=(VMEM,) * 3,
+        out_shape=(half, half, half) if last else (whole, thin, jax.ShapeDtypeStruct((rows, 128), F32)),
         compiler_params=params(),
         cost_estimate=pl.CostEstimate(flops=1, bytes_accessed=2 * (rows + cols) * 384, transcendentals=0),
         name="pairs",
@@ -287,12 +286,29 @@
     )(xa, xb, w_first, *after)
 
 
+def merge_body(term_ref, got_ref, sum_ref, out_ref):
+    rows = term_ref.shape[0] // 2
+    feat = term_ref.shape[1] // 2
+    for at, theirs in ((0, rows), (rows, 0)):
+        both = term_ref[at : at + rows, :] + got_ref[theirs : theirs + rows, :]
+        sum_ref[at : at + rows, :] = both
+        out_ref[at : at + rows, :] = jnp.concatenate([both[:, feat:], both[:, :feat]], axis=1).astype(BF16)
+
+
+def merge(term, got):
+    return pl.pallas_call(
+        merge_body,
+        in_specs=[VMEM] * 2,
+        out_specs=(VMEM, VMEM),
+        out_shape=(jax.ShapeDtypeStruct(got.shape, F32), jax.ShapeDtypeStruct(got.shape, BF16)),
+        compiler_params=params(),
+        name="merge",
+    )(term, got)
+
+
 def finish_body(scale, term_ref, far_ref, inv_ref, *refs):
-    feat = inv_ref.shape[1]
-    far = far_ref[...]
-    far = jnp.concatenate([far[:, feat:], far[:, :feat]], axis=1)
     inv = jnp.concatenate([inv_ref[...], inv_ref[...]], axis=1)
-    refs[-1][...] = (scale * inv * (term_ref[...] + far)).astype(BF16)
+    refs[-1][...] = (scale * inv * (term_ref[...] + far_ref[...].astype(F32))).astype(BF16)
 
 
 def finish(scale, term, far, inv_row, after):
@@ -306,37 +322,57 @@
     )(term, far, inv_row, *after)
 
 
-def grads_body(sizes, d_ref, e_ref, w2t_ref, slope_a, xt_a, ht_a, slope_b, xt_b, ht_b, *out_refs):
+def grads_body(pieces, share, d_ref, w2t_ref, slope_a, xt_a, ht_a, slope_b, xt_b, ht_b, *out_refs):
     feat, hid = w2t_ref.shape
-    d, e = d_ref[...], e_ref[...]
+    half = d_ref.shape[0] // 2
+    d, e = d_ref[:half, :], d_ref[half:, :]
     dfeat_a = jnp.concatenate([d[:, :feat], e[:, :feat]], axis=0)
     dfeat_b = jnp.concatenate([d[:, feat:], e[:, feat:]], axis=0)
+    size = dense_rows(share, hid, feat)
 
     def store(at, part):
-        start = 0
-        for size, ref in zip(sizes, out_refs):
-            ref[:, at] = part[start : start + size]
-            start += size
-
-    block = 256
-    for j in range(hid // block):
-        at = slice(j * block, (j + 1) * block)
-        dpre_a = (dot_nn(dfeat_a, w2t_ref[:, at]) * slope_a[:, at]).astype(BF16)
-        dpre_b = (dot_nn(dfeat_b, w2t_ref[:, at]) * slope_b[:, at]).astype(BF16)
+        if pieces is None:
+            out_refs[0][:, at : at + part.shape[1]] = part
+            return
+        row = 0
+        for count, ref in zip(pieces, out_refs):
+            for n in range(count):
+                block = part[row : row + share]
+                to = n * size + at * share // 128
+                if at < hid:
+                    for lane in range(0, part.shape[1], 128):
+                        ref[to : to + share, :] = block[:, lane : lane + 128]
+                        to += share
+                else:
+                    half = share // 2
+                    ref[to : to + half, :] = jnp.concatenate([block[:half], block[half:]], axis=1)
+                row += share
+
+    width = 256
+    for at in range(0, hid, width):
+        cols = slice(at, at + width)
+        dpre_a = (dot_nn(dfeat_a, w2t_ref[:, cols]) * slope_a[:, cols]).astype(BF16)
+        dpre_b = (dot_nn(dfeat_b, w2t_ref[:, cols]) * slope_b[:, cols]).astype(BF16)
         store(at, (dot_nn(xt_a[...], dpre_a) + dot_nn(xt_b[...], dpre_b)).astype(BF16))
-    store(slice(hid, hid + feat), (dot_nn(ht_a[...], dfeat_a) + dot_nn(ht_b[...], dfeat_b)).astype(BF16))
-
-
-def grads(d, e, w2t, group_a, group_b, sizes):
+    store(hid, (dot_nn(ht_a[...], dfeat_a) + dot_nn(ht_b[...], dfeat_b)).astype(BF16))
+
+
+def dense_rows(share, hid, feat):
+    return share * (hid + feat) // 128
+
+
+def grads(dfeat, w2t, group_a, group_b, pieces, share):
     feat, hid = w2t.shape
-    return pl.pallas_call(
-        lambda *refs: grads_body(sizes, *refs),
-        in_specs=[VMEM] * 9,
-        out_specs=(VMEM,) * len(sizes),
-        out_shape=tuple(jax.ShapeDtypeStruct((size, hid + feat), BF16) for size in sizes),
+    size = dense_rows(share, hid, feat)
+    shapes = [(group_a[1].shape[0], hid + feat)] if pieces is None else [(count * size, 128) for count in pieces]
+    return pl.pallas_call(
+        lambda *refs: grads_body(pieces, share, *refs),
+        in_specs=[VMEM] * 8,
+        out_specs=(VMEM,) * len(shapes),
+        out_shape=tuple(jax.ShapeDtypeStruct(shape, BF16) for shape in shapes),
         compiler_params=params(),
         name="grads",
-    )(d, e, w2t, *group_a, *group_b)
+    )(dfeat, w2t, *group_a, *group_b)
 
 
 def relay_body(count, got_ref, *refs):
@@ -359,23 +395,31 @@
     )(got, *own, *after)
 
 
-def total_body(*refs):
+def total_body(dense, *refs):
     parts, (first_ref, second_ref) = refs[:-2], refs[-2:]
     total = parts[0][...].astype(F32)
     for ref in parts[1:]:
         total = total + ref[...].astype(F32)
-    hid = first_ref.shape[1]
-    first_ref[...] = total[:, :hid]
-    second_ref[...] = total[:, hid:]
-
-
-def total(parts, hid):
-    share, width = parts[0].shape
-    return pl.pallas_call(
-        total_body,
+    share, hid = first_ref.shape
+    feat = second_ref.shape[1]
+    if not dense:
+        first_ref[...] = total[:, :hid]
+        second_ref[...] = total[:, hid:]
+        return
+    row = 0
+    for at in range(0, hid, 128):
+        first_ref[:, at : at + 128] = total[row : row + share]
+        row += share
+    second_ref[: share // 2, :] = total[row:, :feat]
+    second_ref[share // 2 :, :] = total[row:, feat:]
+
+
+def total(parts, share, hid, feat, dense):
+    return pl.pallas_call(
+        lambda *refs: total_body(dense, *refs),
         in_specs=[VMEM] * len(parts),
         out_specs=(VMEM, VMEM),
-        out_shape=(jax.ShapeDtypeStruct((share, hid), F32), jax.ShapeDtypeStruct((share, width - hid), F32)),
+        out_shape=(jax.ShapeDtypeStruct((share, hid), F32), jax.ShapeDtypeStruct((share, feat), F32)),
         compiler_params=params(),
         name="total",
     )(*parts)
@@ -403,7 +447,7 @@
     line, deep, tall = lax.axis_size("kc"), lax.axis_size("enc"), lax.axis_size("kr")
     lines = deep * tall
     share = width // (line * lines)
-    order = [(2, 1), (3, 1), (1, 1), (2, 0), (3, 0), (1, 0), (0, 1), (0, 0)] if (deep, tall) == (4, 2) else None
+    order = [(2, 1), (3, 1), (1, 1), (0, 1), (2, 0), (3, 0), (1, 0), (0, 0)] if (deep, tall) == (4, 2) else None
     inv_row = inv_length[None, :]
     w2t = w_second.T
 
@@ -414,7 +458,8 @@
     tall_masks = range(1, tall)
     if order:
         z_two, z_one, y_own = swap(own, "enc", 2), swap(own, "enc", 1), swap(own, "kr", 1)
-        z_both, row_both = gate(([z_one, z_two], [own, far_row]), (y_own, group_a[1]))
+        (z_both,) = gate(([z_one, z_two],), (y_own, group_a[1]))
+        (row_both,) = gate(([own, far_row],), (z_both,))
         core_both = swap(row_both, "kc", 1)
         calls = [
             ([row_both, y_own], [1, 1]),
@@ -432,29 +477,28 @@
         (row_both,) = gate(([own, far_row],))
         core_both = swap(row_both, "kc", 1)
     rowa, rsp = group_rows(own_rows, [row_both, core_both])
-    x_far = swap(hold(inputs, (core_both,)), "kc", 2)
+    x_far = swap(inputs, "kc", 2)
 
     sofar = None
     for i, (blocks, counts) in enumerate(calls):
         sofar = pairs(own_rows, rowa, rsp, blocks, counts, sofar, i == len(calls) - 1)
-    stay, gone, keep, send = sofar
-    term = keep + swap(send, "kc", 1)
+    stay, gone, term = sofar
+    term, moved = merge(term, swap(term, "kc", 1))
     x_both = swap(hold(x_far, (term,)), "kc", 1)
-    group_b = prepare(x_far, x_both, w_first, share, order, (send,))
+    group_b = prepare(x_far, x_both, w_first, share, order, (term,))
     lscale = loss_gain / math.sqrt(probe_width)
-    dfeat = finish(-lscale, term, swap(term, "kc", 2), inv_row, (group_b[1],))
-    other = swap(dfeat, "kc", 1)
+    dfeat = finish(-lscale, term, swap(moved, "kc", 2), inv_row, (group_b[1],))
     stay = stay + swap(hold(gone, (term,)), "kc", 1)
-    sizes = [share * n for n in (3, 1, 1, 1, 1, 1)] if order else [width // line]
-    parts = grads(dfeat, other, w2t, group_a, group_b, sizes)
+    parts = grads(dfeat, w2t, group_a, group_b, (2, 1, 1, 1, 1, 1, 1) if order else None, share)
     far = swap(hold(stay[own_rows:], (parts[0],)), "kc", 2)
     if order:
-        two, three, one = relay(swap(parts[0], "kr", 1), parts[1:4], (BF16,) * 3, (far,))
-        got = [parts[5], swap(two, "enc", 2), swap(three, "enc", 3), swap(one, "enc", 1), swap(parts[4], "kr", 1)]
+        two, three = relay(swap(parts[0], "kr", 1), parts[3:5], (BF16, BF16))
+        (one,) = relay(swap(parts[1], "kr", 1), parts[5:6], (BF16,), (two, far))
+        got = [parts[6], swap(two, "enc", 2), swap(three, "enc", 3), swap(one, "enc", 1), swap(parts[2], "kr", 1)]
     else:
         flat = lax.all_to_all(parts[0], ("enc", "kr"), 0, 0, tiled=True)
         got = list(flat.astype(F32).reshape(lines, share, hid + feat))
-    grad_first, grad_second = total(got, hid)
+    grad_first, grad_second = total(got, share, hid, feat, order is not None)
 
     v = stay[:own_rows] + far
     products = (v * probe_gain).astype(BF16)

time: 58 us -> 54 us (0.931)
  waiting for transfers between devices: 17.3 us -> 11.2 us
  starting transfers between devices: 21.2 us -> 23.3 us
    ppermute x21, waiting for transfers between devices: 17.3 us -> 11.2 us  [swap(): return lax.ppermute(x, axis, [(i, i ^ mask) for i in range(size)])]
    ppermute x21, starting transfers between devices: 21.2 us -> 23.3 us  [swap(): return lax.ppermute(x, axis, [(i, i ^ mask) for i in range(size)])]
    pallas_call x2 -> x3, Pallas kernels: 2.11 us -> 2.29 us  [the longest x1 1.49 us: grads(): pl.pallas_call(lambda *refs: grads_body(pieces, share, *refs), in_specs=[...]
  transfers between devices with their start and end apart: 21 -> 21, of which waited for: 13 -> 8; matrix products, arithmetic and copies ran while one was open for 1% -> 1% of each run, Pallas kernels for 28% -> 30%
where the time goes in v4:
time: 54 us; the launch traced here: 53.8 us
  starting transfers between devices  23.3 us (43%)
  Pallas kernels  16.8 us (31%)
  waiting for transfers between devices  11.2 us (21%)
  local copies, waits for them, and re-layouts  0.95 us (2%)
  between operations  0.87 us (2%)
  other arithmetic  0.66 us (1%)
    ppermute x21, starting transfers between devices, swap(): return lax.ppermute(x, axis, [(i, i ^ mask) for i in range(size)])  23.3 us
    ppermute x21, waiting for transfers between devices, swap(): return lax.ppermute(x, axis, [(i, i ^ mask) for i in range(size)])  11.2 us
    pallas_call x4, Pallas kernels, pairs(): pl.pallas_call(lambda *refs: pair_body(own_rows, counts, first, last, *re...  5.48 us
    pallas_call x2, Pallas kernels, prepare(): pl.pallas_call(lambda *refs: prepare_body(share, order, *refs), in_specs=...  4.76 us
    pallas_call x1, Pallas kernels, encode(): pl.pallas_call(encode_body, in_specs=[HBM] * 6, out_specs=VMEM, out_shape...  3.52 us
    pallas_call x1, Pallas kernels, grads(): pl.pallas_call(lambda *refs: grads_body(pieces, share, *refs), in_specs=[...  1.49 us
  transfers between devices with their start and end apart: 21, of which 8 were waited for; matrix products, arithmetic and copies ran while one was open for 1% of the time, Pallas kernels for 30%

profile of v4, /device:TPU:0, one launch (start us, length us, event | category | flops | bytes accessed | tf_op | source)
XLA Modules:
  0.0 53.8 jit_solution(17606122521574803637)
XLA Ops:
  0.6 0.0 copy-start.1
  0.6 0.0 copy-start
  0.7 0.5 collective-permute-start.4
  1.2 3.5 %encode.1.refs_3_.refs_0_ = bf16[480,128]{1,0:T(8,128)(2,1)} custom-call(bf16[192,1024]{1,0:T(8,128)(2,1)} %refs_0_.1, bf16[1024,1024]{1,0:T(8,128)(2,1)} %refs_2_.3, bf16[64,1024]{1,0:T(8,128)(2,1)} %bitcast.2, f32[1,64]{1,0:T(1,128)} %bitcast.4, bf16[192,128]{1,0:T(8,128)(2,1)} %probe_hbm.1, bf16[192,128]{1,0:T(8,128)(2,1)} %solve_hbm.1), custom_call_target="tpu_custom_call" | custom-call | tf_op jit(solution)/shard_map/encode/pallas_call | solution.py:86
  4.7 3.6 %collective-permute-start.2 = (bf16[480,128]{1,0:T(8,128)(2,1)}, bf16[480,128]{1,0:T(8,128)(2,1)S(1)}, u32[]{:S(2)}, u32[]{:S(2)}) collective-permute-start(bf16[480,128]{1,0:T(8,128)(2,1)} %encode.1.refs_3_.refs_0_), channel_id=1, source_target_pairs={{0,16},{8,24},{16,0},{24,8},{1,17},{9,25},{17,1},{25,9},{2,18},{10... | collective-permute-start | bytes 368648 | tf_op jit(solution)/shard_map/ppermute | solution.py:31
  8.3 1.5 %collective-permute-start.3 = (bf16[480,128]{1,0:T(8,128)(2,1)}, bf16[480,128]{1,0:T(8,128)(2,1)S(1)}, u32[]{:S(2)}, u32[]{:S(2)}) collective-permute-start(bf16[480,128]{1,0:T(8,128)(2,1)} %encode.1.refs_3_.refs_0_), channel_id=1, source_target_pairs={{0,4},{4,0},{1,5},{5,1},{2,6},{6,2},{3,7},{7,3},{8,12},{12,8},{9,1... | collective-permute-start | bytes 368648 | tf_op jit(solution)/shard_map/ppermute | solution.py:31
  9.8 1.6 %collective-permute-start.1 = (bf16[480,128]{1,0:T(8,128)(2,1)}, bf16[480,128]{1,0:T(8,128)(2,1)S(1)}, u32[]{:S(2)}, u32[]{:S(2)}) collective-permute-start(bf16[480,128]{1,0:T(8,128)(2,1)} %encode.1.refs_3_.refs_0_), channel_id=1, source_target_pairs={{0,8},{8,0},{16,24},{24,16},{1,9},{9,1},{17,25},{25,17},{2,10},{10... | collective-permute-start | bytes 368648 | tf_op jit(solution)/shard_map/ppermute | solution.py:31
  11.4 1.5 %collective-permute-start = (bf16[480,128]{1,0:T(8,128)(2,1)}, bf16[480,128]{1,0:T(8,128)(2,1)S(1)}, u32[]{:S(2)}, u32[]{:S(2)}) collective-permute-start(bf16[480,128]{1,0:T(8,128)(2,1)} %encode.1.refs_3_.refs_0_), channel_id=1, source_target_pairs={{0,2},{1,3},{2,0},{3,1},{4,6},{5,7},{6,4},{7,5},{8,10},{9,11},{10,... | collective-permute-start | bytes 368648 | tf_op jit(solution)/shard_map/ppermute | solution.py:31
  12.9 0.0 collective-permute-done.4.refs_1_
  12.9 0.0 copy-done.1
  12.9 0.0 copy-done
  12.9 0.0 copy-start.2
  12.9 0.9 %copy-done.2 = bf16[480,128]{1,0:T(8,128)(2,1)S(1)} copy-done((bf16[480,128]{1,0:T(8,128)(2,1)S(1)}, bf16[480,128]{1,0:T(8,128)(2,1)}, u32[]{:S(2)}) %copy-start.2) | copy-done | bytes 122904
  13.8 2.4 %prepare.2 = (f32[384,1024]{1,0:T(8,128)S(1)}, bf16[256,384]{1,0:T(8,128)(2,1)S(1)}, bf16[256,384]{1,0:T(8,128)(2,1)S(1)}) custom-call(bf16[192,1024]{1,0:T(8,128)(2,1)S(1)} %copy-done.1, bf16[192,1024]{1,0:T(8,128)(2,1)S(1)} %collective-permute-done.4.refs_1_, bf16[1024,1024]{1,0:T(8,128)(2,1)S(1)} %copy-done, bf16[480,128]{1,0:T(8,128)(2,1)S(1)} %copy-done.2), custom_call_target="tpu_custom_call" | custom-call | flops 1 | bytes 1048576 | tf_op jit(solution)/shard_map/prepare/pallas_call | solution.py:278
  16.2 0.0 collective-permute-done.2.refs_1_.refs_3_
  16.2 0.0 collective-permute-done.3.refs_2_.refs_3_
  16.2 0.3 collective-permute-done.1.refs_0_.refs_2_
  16.5 0.0 collective-permute-done.refs_1_
  16.6 0.0 copy-done.3
  16.6 0.1 collective-permute-start.5
  16.7 0.6 %collective-permute-start.8 = (bf16[960,128]{1,0:T(8,128)(2,1)S(1)}, bf16[960,128]{1,0:T(8,128)(2,1)S(1)}, u32[]{:S(2)}, u32[]{:S(2)}) collective-permute-start(bf16[960,128]{1,0:T(8,128)(2,1)S(1)} %gate.2.refs_2_), channel_id=1, source_target_pairs={{0,4},{4,0},{1,5},{5,1},{2,6},{6,2},{3,7},{7,3},{8,12},{12,8},{9,1... | collective-permute-start | bytes 737288 | tf_op jit(solution)/shard_map/ppermute | solution.py:31
  17.3 1.5 %collective-permute-start.12 = (bf16[192,1024]{1,0:T(8,128)(2,1)S(1)}, bf16[192,1024]{1,0:T(8,128)(2,1)S(1)}, u32[]{:S(2)}, u32[]{:S(2)}) collective-permute-start(bf16[192,1024]{1,0:T(8,128)(2,1)S(1)} %copy-done.1), channel_id=1, source_target_pairs={{0,2},{1,3},{2,0},{3,1},{4,6},{5,7},{6,4},{7,5},{8,10},{9,11},{10,... | collective-permute-start | bytes 1179656 | tf_op jit(solution)/shard_map/ppermute | solution.py:31
  18.8 1.2 %collective-permute-start.6 = (bf16[480,128]{1,0:T(8,128)(2,1)S(1)}, bf16[480,128]{1,0:T(8,128)(2,1)S(1)}, u32[]{:S(2)}, u32[]{:S(2)}) collective-permute-start(bf16[480,128]{1,0:T(8,128)(2,1)S(1)} %collective-permute-done.2.refs_1_.refs_3_), channel_id=1, source_target_pairs={{0,8},{8,0},{16,24},{24,16},{1,9},{9,1},{17,25},{25,17},{2,10},{10... | collective-permute-start | bytes 368648 | tf_op jit(solution)/shard_map/ppermute | solution.py:31
  20.0 1.8 %collective-permute-start.7 = (bf16[480,128]{1,0:T(8,128)(2,1)S(1)}, bf16[480,128]{1,0:T(8,128)(2,1)S(1)}, u32[]{:S(2)}, u32[]{:S(2)}) collective-permute-start(bf16[480,128]{1,0:T(8,128)(2,1)S(1)} %collective-permute-done.3.refs_2_.refs_3_), channel_id=1, source_target_pairs={{0,24},{8,16},{16,8},{24,0},{1,25},{9,17},{17,9},{25,1},{2,26},{10... | collective-permute-start | bytes 368648 | tf_op jit(solution)/shard_map/ppermute | solution.py:31
  21.8 0.0 collective-permute-done.5.refs_1_
  21.8 0.5 rows.1
  22.3 1.3 %pairs.4 = (f32[768,128]{1,0:T(8,128)S(1)}, f32[768,64]{1,0:T(8,128)S(1)}, f32[768,128]{1,0:T(8,128)S(1)}) custom-call(bf16[768,256]{1,0:T(8,128)(2,1)S(1)} %get-tuple-element.37.refs_0_, bf16[768,256]{1,0:T(8,128)(2,1)S(1)} %get-tuple-element.38.refs_1_, bf16[960,128]{1,0:T(8,128)(2,1)S(1)} %gate.3.refs_0_.refs_2_, ...), custom_call_target="tpu_custom_call" | custom-call | flops 1 | bytes 884736 | tf_op jit(solution)/shard_map/pairs/pallas_call | solution.py:229
  23.6 1.4 %pairs.5 = (f32[768,128]{1,0:T(8,128)S(1)}, f32[768,64]{1,0:T(8,128)S(1)}, f32[768,128]{1,0:T(8,128)S(1)}) custom-call(bf16[768,256]{1,0:T(8,128)(2,1)S(1)} %get-tuple-element.37.refs_0_, bf16[768,256]{1,0:T(8,128)(2,1)S(1)} %get-tuple-element.38.refs_1_, bf16[480,128]{1,0:T(8,128)(2,1)S(1)} %collective-permute-done.1.refs_0_.refs_2_, ...), custom_call_target="tpu_custom_call" | custom-call | flops 1 | bytes 884736 | tf_op jit(solution)/shard_map/pairs/pallas_call | solution.py:229
  25.0 0.0 collective-permute-done.8.refs_2_
  25.0 1.4 %pairs.6 = (f32[768,128]{1,0:T(8,128)S(1)}, f32[768,64]{1,0:T(8,128)S(1)}, f32[768,128]{1,0:T(8,128)S(1)}) custom-call(bf16[768,256]{1,0:T(8,128)(2,1)S(1)} %get-tuple-element.37.refs_0_, bf16[768,256]{1,0:T(8,128)(2,1)S(1)} %get-tuple-element.38.refs_1_, bf16[960,128]{1,0:T(8,128)(2,1)S(1)} %collective-permute-done.8.refs_2_, ...), custom_call_target="tpu_custom_call" | custom-call | flops 1 | bytes 884736 | tf_op jit(solution)/shard_map/pairs/pallas_call | solution.py:229
  26.4 0.0 collective-permute-done.6.refs_2_
  26.4 1.4 %collective-permute-done.7.refs_3_ = bf16[480,128]{1,0:T(8,128)(2,1)S(1)} collective-permute-done((bf16[480,128]{1,0:T(8,128)(2,1)S(1)}, bf16[480,128]{1,0:T(8,128)(2,1)S(1)}, u32[]{:S(2)}, u32[]{:S(2)}) %collective-permute-start.7) | collective-permute-done | bytes 122912 | tf_op jit(solution)/shard_map/ppermute | solution.py:31
  27.9 1.4 %pairs.7 = (f32[384,128]{1,0:T(8,128)S(1)}, f32[384,128]{1,0:T(8,128)S(1)}, f32[384,128]{1,0:T(8,128)S(1)}) custom-call(bf16[768,256]{1,0:T(8,128)(2,1)S(1)} %get-tuple-element.37.refs_0_, bf16[768,256]{1,0:T(8,128)(2,1)S(1)} %get-tuple-element.38.refs_1_, bf16[480,128]{1,0:T(8,128)(2,1)S(1)} %collective-permute-done.6.refs_2_, ...), custom_call_target="tpu_custom_call" | custom-call | flops 1 | bytes 884736 | tf_op jit(solution)/shard_map/pairs/pallas_call | solution.py:229
  29.3 0.1 collective-permute-start.9
  29.4 1.4 %collective-permute-done.9.got_ref = f32[384,128]{1,0:T(8,128)S(1)} collective-permute-done((f32[384,128]{1,0:T(8,128)S(1)}, f32[384,128]{1,0:T(8,128)S(1)}, u32[]{:S(2)}, u32[]{:S(2)}) %collective-permute-start.9) | collective-permute-done | bytes 196640 | tf_op jit(solution)/shard_map/ppermute | solution.py:31
  30.8 0.1 merge.1
  30.9 0.0 collective-permute-done.12.x_ref.refs_0_
  30.9 0.2 collective-permute-start.13
  31.2 0.0 copy-start.5
  31.2 0.4 collective-permute-start.10
  31.6 0.5 collective-permute-start.11
  32.2 0.6 %collective-permute-done.13.refs_1_ = bf16[192,1024]{1,0:T(8,128)(2,1)S(1)} collective-permute-done((bf16[192,1024]{1,0:T(8,128)(2,1)S(1)}, bf16[192,1024]{1,0:T(8,128)(2,1)S(1)}, u32[]{:S(2)}, u32[]{:S(2)}) %collective-permute-start.13) | collective-permute-done | bytes 393248 | tf_op jit(solution)/shard_map/ppermute | solution.py:31
  32.7 2.4 %prepare.3 = (f32[384,1024]{1,0:T(8,128)S(1)}, bf16[256,384]{1,0:T(8,128)(2,1)S(1)}, bf16[256,384]{1,0:T(8,128)(2,1)S(1)}) custom-call(bf16[192,1024]{1,0:T(8,128)(2,1)S(1)} %collective-permute-done.12.x_ref.refs_0_, bf16[192,1024]{1,0:T(8,128)(2,1)S(1)} %collective-permute-done.13.refs_1_, bf16[1024,1024]{1,0:T(8,128)(2,1)S(1)} %copy-done, ...), custom_call_target="tpu_custom_call" | custom-call | flops 1 | bytes 1048576 | tf_op jit(solution)/shard_map/prepare/pallas_call | solution.py:278
  35.1 1.3 %collective-permute-done.11.refs_1_ = bf16[384,128]{1,0:T(8,128)(2,1)S(1)} collective-permute-done((bf16[384,128]{1,0:T(8,128)(2,1)S(1)}, bf16[384,128]{1,0:T(8,128)(2,1)S(1)}, u32[]{:S(2)}, u32[]{:S(2)}) %collective-permute-start.11) | collective-permute-done | bytes 98336 | tf_op jit(solution)/shard_map/ppermute | solution.py:31
  36.5 0.0 copy-done.5
  36.5 0.1 finish.1.refs_0_
  36.6 1.5 %grads.1 = (bf16[544,128]{1,0:T(8,128)(2,1)S(1)}, bf16[272,128]{1,0:T(8,128)(2,1)S(1)}, bf16[272,128]{1,0:T(8,128)(2,1)S(1)}, bf16[272,128]{1,0:T(8,128)(2,1)S(1...) custom-call(bf16[384,128]{1,0:T(8,128)(2,1)S(1)} %finish.1.refs_0_, ...), custom_call_target="tpu_custom_call" | custom-call | tf_op jit(solution)/shard_map/grads/pallas_call | solution.py:368
  38.0 1.1 %collective-permute-start.15 = (bf16[544,128]{1,0:T(8,128)(2,1)S(1)}, bf16[544,128]{1,0:T(8,128)(2,1)S(1)}, u32[]{:S(2)}, u32[]{:S(2)}) collective-permute-start(bf16[544,128]{1,0:T(8,128)(2,1)S(1)} %get-tuple-element.58.refs_0_), channel_id=1, source_target_pairs={{0,4},{4,0},{1,5},{5,1},{2,6},{6,2},{3,7},{7,3},{8,12},{12,8},{9,1... | collective-permute-start | bytes 417800 | tf_op jit(solution)/shard_map/ppermute | solution.py:31
  39.1 0.0 collective-permute-done.10
  39.2 0.6 %collective-permute-start.14 = (f32[192,128]{1,0:T(8,128)S(1)}, f32[192,128]{1,0:T(8,128)S(1)}, u32[]{:S(2)}, u32[]{:S(2)}) collective-permute-start(f32[192,128]{1,0:T(8,128)S(1)} %hold.5), channel_id=1, source_target_pairs={{0,2},{1,3},{2,0},{3,1},{4,6},{5,7},{6,4},{7,5},{8,10},{9,11},{10,... | collective-permute-start | bytes 294920 | tf_op jit(solution)/shard_map/ppermute | solution.py:31
  39.8 1.0 %collective-permute-start.18 = (bf16[272,128]{1,0:T(8,128)(2,1)S(1)}, bf16[272,128]{1,0:T(8,128)(2,1)S(1)}, u32[]{:S(2)}, u32[]{:S(2)}) collective-permute-start(bf16[272,128]{1,0:T(8,128)(2,1)S(1)} %get-tuple-element.64), channel_id=1, source_target_pairs={{0,4},{4,0},{1,5},{5,1},{2,6},{6,2},{3,7},{7,3},{8,12},{12,8},{9,1... | collective-permute-start | bytes 208904 | tf_op jit(solution)/shard_map/ppermute | solution.py:31
  40.8 1.0 %collective-permute-start.20 = (bf16[272,128]{1,0:T(8,128)(2,1)S(1)}, bf16[272,128]{1,0:T(8,128)(2,1)S(1)}, u32[]{:S(2)}, u32[]{:S(2)}) collective-permute-start(bf16[272,128]{1,0:T(8,128)(2,1)S(1)} %get-tuple-element.66), channel_id=1, source_target_pairs={{0,4},{4,0},{1,5},{5,1},{2,6},{6,2},{3,7},{7,3},{8,12},{12,8},{9,1... | collective-permute-start | bytes 208904 | tf_op jit(solution)/shard_map/ppermute | solution.py:31
  41.8 2.7 %collective-permute-done.15.refs_0_ = bf16[544,128]{1,0:T(8,128)(2,1)S(1)} collective-permute-done((bf16[544,128]{1,0:T(8,128)(2,1)S(1)}, bf16[544,128]{1,0:T(8,128)(2,1)S(1)}, u32[]{:S(2)}, u32[]{:S(2)}) %collective-permute-start.15) | collective-permute-done | bytes 139296 | tf_op jit(solution)/shard_map/ppermute | solution.py:31
  44.5 2.0 %collective-permute-start.16 = (bf16[272,128]{1,0:T(8,128)(2,1)S(1)}, bf16[272,128]{1,0:T(8,128)(2,1)S(1)}, u32[]{:S(2)}, u32[]{:S(2)}) collective-permute-start(bf16[272,128]{1,0:T(8,128)(2,1)S(1)} %get-tuple-element.62.refs_2_), channel_id=1, source_target_pairs={{0,16},{8,24},{16,0},{24,8},{1,17},{9,25},{17,1},{25,9},{2,18},{10... | collective-permute-start | bytes 208904 | tf_op jit(solution)/shard_map/ppermute | solution.py:31
  46.5 0.0 collective-permute-done.18.refs_0_
  46.5 0.0 collective-permute-done.14.refs_3_
  46.5 0.4 collective-permute-start.19
  47.0 2.1 %collective-permute-start.17 = (bf16[272,128]{1,0:T(8,128)(2,1)S(1)}, bf16[272,128]{1,0:T(8,128)(2,1)S(1)}, u32[]{:S(2)}, u32[]{:S(2)}) collective-permute-start(bf16[272,128]{1,0:T(8,128)(2,1)S(1)} %get-tuple-element.63), channel_id=1, source_target_pairs={{0,24},{8,16},{16,8},{24,0},{1,25},{9,17},{17,9},{25,1},{2,26},{10... | collective-permute-start | bytes 208904 | tf_op jit(solution)/shard_map/ppermute | solution.py:31
  49.1 0.6 %fusion.1 = bf16[192,128]{1,0:T(8,128)(2,1)} fusion(f32[192,128]{1,0:T(8,128)S(1)} %collective-permute-done.14.refs_3_, f32[384,128]{1,0:T(8,128)S(1)} %add.6), kind=kLoop, calls=%fused_computation.2 | loop fusion | flops 73728 | bytes 245760 | tf_op jit(solution)/shard_map/convert_element_type | solution.py:504
  49.7 0.0 collective-permute-done.20.refs_4_
  49.7 1.6 %collective-permute-done.19.refs_3_ = bf16[272,128]{1,0:T(8,128)(2,1)S(1)} collective-permute-done((bf16[272,128]{1,0:T(8,128)(2,1)S(1)}, bf16[272,128]{1,0:T(8,128)(2,1)S(1)}, u32[]{:S(2)}, u32[]{:S(2)}) %collective-permute-start.19) | collective-permute-done | bytes 69664 | tf_op jit(solution)/shard_map/ppermute | solution.py:31
  51.3 0.0 collective-permute-done.16.refs_1_
  51.3 1.8 %collective-permute-done.17.refs_2_ = bf16[272,128]{1,0:T(8,128)(2,1)S(1)} collective-permute-done((bf16[272,128]{1,0:T(8,128)(2,1)S(1)}, bf16[272,128]{1,0:T(8,128)(2,1)S(1)}, u32[]{:S(2)}, u32[]{:S(2)}) %collective-permute-start.17) | collective-permute-done | bytes 69664 | tf_op jit(solution)/shard_map/ppermute | solution.py:31
  53.1 0.7 %total.1 = (f32[32,1024]{1,0:T(8,128)}, f32[32,64]{1,0:T(8,128)}) custom-call(bf16[272,128]{1,0:T(8,128)(2,1)S(1)} %get-tuple-element.59.refs_0_, bf16[272,128]{1,0:T(8,128)(2,1)S(1)} %collective-permute-done.16.refs_1_, bf16[272,128]{1,0:T(8,128)(2,1)S(1)} %collective-permute-done.17.refs_2_, bf16[272,128]{1,0:T(8,128)(2,1)S(1)} %collective-permute-done.19.refs_3_, ...), custom_call_target="tpu_custom_call" | custom-call | tf_op jit(solution)/shard_map/total/pallas_call | solution.py:418
  (12 shorter events, 0.2 us)
Async XLA Ops:
  0.6 12.3 %copy-start.1 = (bf16[192,1024]{1,0:T(8,128)(2,1)S(1)}, bf16[192,1024]{1,0:T(8,128)(2,1)}, u32[]{:S(2)}) copy-start(bf16[192,1024]{1,0:T(8,128)(2,1)} %refs_0_.1) | copy-start | bytes 1179652
  0.6 12.3 %copy-start = (bf16[1024,1024]{1,0:T(8,128)(2,1)S(1)}, bf16[1024,1024]{1,0:T(8,128)(2,1)}, u32[]{:S(2)}) copy-start(bf16[1024,1024]{1,0:T(8,128)(2,1)} %refs_2_.3) | copy-start | bytes 6291460
  0.7 12.2 %collective-permute-start.4 = (bf16[192,1024]{1,0:T(8,128)(2,1)}, bf16[192,1024]{1,0:T(8,128)(2,1)S(1)}, u32[]{:S(2)}, u32[]{:S(2)}) collective-permute-start(bf16[192,1024]{1,0:T(8,128)(2,1)} %refs_0_.1), channel_id=1, source_target_pairs={{0,1},{1,0},{2,3},{3,2},{4,5},{5,4},{6,7},{7,6},{8,9},{9,8},{10,11... | collective-permute-start | bytes 1179656 | tf_op jit(solution)/shard_map/ppermute | solution.py:31
  4.7 11.5 %collective-permute-start.2 = (bf16[480,128]{1,0:T(8,128)(2,1)}, bf16[480,128]{1,0:T(8,128)(2,1)S(1)}, u32[]{:S(2)}, u32[]{:S(2)}) collective-permute-start(bf16[480,128]{1,0:T(8,128)(2,1)} %encode.1.refs_3_.refs_0_), channel_id=1, source_target_pairs={{0,16},{8,24},{16,0},{24,8},{1,17},{9,25},{17,1},{25,9},{2,18},{10... | collective-permute-start | bytes 368648 | tf_op jit(solution)/shard_map/ppermute | solution.py:31
  8.3 7.9 %collective-permute-start.3 = (bf16[480,128]{1,0:T(8,128)(2,1)}, bf16[480,128]{1,0:T(8,128)(2,1)S(1)}, u32[]{:S(2)}, u32[]{:S(2)}) collective-permute-start(bf16[480,128]{1,0:T(8,128)(2,1)} %encode.1.refs_3_.refs_0_), channel_id=1, source_target_pairs={{0,4},{4,0},{1,5},{5,1},{2,6},{6,2},{3,7},{7,3},{8,12},{12,8},{9,1... | collective-permute-start | bytes 368648 | tf_op jit(solution)/shard_map/ppermute | solution.py:31
  9.8 6.7 %collective-permute-start.1 = (bf16[480,128]{1,0:T(8,128)(2,1)}, bf16[480,128]{1,0:T(8,128)(2,1)S(1)}, u32[]{:S(2)}, u32[]{:S(2)}) collective-permute-start(bf16[480,128]{1,0:T(8,128)(2,1)} %encode.1.refs_3_.refs_0_), channel_id=1, source_target_pairs={{0,8},{8,0},{16,24},{24,16},{1,9},{9,1},{17,25},{25,17},{2,10},{10... | collective-permute-start | bytes 368648 | tf_op jit(solution)/shard_map/ppermute | solution.py:31
  11.4 5.1 %collective-permute-start = (bf16[480,128]{1,0:T(8,128)(2,1)}, bf16[480,128]{1,0:T(8,128)(2,1)S(1)}, u32[]{:S(2)}, u32[]{:S(2)}) collective-permute-start(bf16[480,128]{1,0:T(8,128)(2,1)} %encode.1.refs_3_.refs_0_), channel_id=1, source_target_pairs={{0,2},{1,3},{2,0},{3,1},{4,6},{5,7},{6,4},{7,5},{8,10},{9,11},{10,... | collective-permute-start | bytes 368648 | tf_op jit(solution)/shard_map/ppermute | solution.py:31
  12.9 0.9 %copy-start.2 = (bf16[480,128]{1,0:T(8,128)(2,1)S(1)}, bf16[480,128]{1,0:T(8,128)(2,1)}, u32[]{:S(2)}) copy-start(bf16[480,128]{1,0:T(8,128)(2,1)} %encode.1.refs_3_.refs_0_) | copy-start | bytes 368644
  13.8 2.7 %copy-start.3 = (bf16[480,128]{1,0:T(8,128)(2,1)S(1)}, bf16[480,128]{1,0:T(8,128)(2,1)}, u32[]{:S(2)}) copy-start(bf16[480,128]{1,0:T(8,128)(2,1)} %encode.1.refs_3_.refs_0_) | copy-start | bytes 368644
  16.6 5.2 %collective-permute-start.5 = (bf16[960,128]{1,0:T(8,128)(2,1)S(1)}, bf16[960,128]{1,0:T(8,128)(2,1)S(1)}, u32[]{:S(2)}, u32[]{:S(2)}) collective-permute-start(bf16[960,128]{1,0:T(8,128)(2,1)S(1)} %gate.3.refs_0_.refs_2_), channel_id=1, source_target_pairs={{0,1},{1,0},{2,3},{3,2},{4,5},{5,4},{6,7},{7,6},{8,9},{9,8},{10,11... | collective-permute-start | bytes 737288 | tf_op jit(solution)/shard_map/ppermute | solution.py:31
  16.7 8.4 %collective-permute-start.8 = (bf16[960,128]{1,0:T(8,128)(2,1)S(1)}, bf16[960,128]{1,0:T(8,128)(2,1)S(1)}, u32[]{:S(2)}, u32[]{:S(2)}) collective-permute-start(bf16[960,128]{1,0:T(8,128)(2,1)S(1)} %gate.2.refs_2_), channel_id=1, source_target_pairs={{0,4},{4,0},{1,5},{5,1},{2,6},{6,2},{3,7},{7,3},{8,12},{12,8},{9,1... | collective-permute-start | bytes 737288 | tf_op jit(solution)/shard_map/ppermute | solution.py:31
  17.3 13.6 %collective-permute-start.12 = (bf16[192,1024]{1,0:T(8,128)(2,1)S(1)}, bf16[192,1024]{1,0:T(8,128)(2,1)S(1)}, u32[]{:S(2)}, u32[]{:S(2)}) collective-permute-start(bf16[192,1024]{1,0:T(8,128)(2,1)S(1)} %copy-done.1), channel_id=1, source_target_pairs={{0,2},{1,3},{2,0},{3,1},{4,6},{5,7},{6,4},{7,5},{8,10},{9,11},{10,... | collective-permute-start | bytes 1179656 | tf_op jit(solution)/shard_map/ppermute | solution.py:31
  18.8 7.6 %collective-permute-start.6 = (bf16[480,128]{1,0:T(8,128)(2,1)S(1)}, bf16[480,128]{1,0:T(8,128)(2,1)S(1)}, u32[]{:S(2)}, u32[]{:S(2)}) collective-permute-start(bf16[480,128]{1,0:T(8,128)(2,1)S(1)} %collective-permute-done.2.refs_1_.refs_3_), channel_id=1, source_target_pairs={{0,8},{8,0},{16,24},{24,16},{1,9},{9,1},{17,25},{25,17},{2,10},{10... | collective-permute-start | bytes 368648 | tf_op jit(solution)/shard_map/ppermute | solution.py:31
  20.0 7.9 %collective-permute-start.7 = (bf16[480,128]{1,0:T(8,128)(2,1)S(1)}, bf16[480,128]{1,0:T(8,128)(2,1)S(1)}, u32[]{:S(2)}, u32[]{:S(2)}) collective-permute-start(bf16[480,128]{1,0:T(8,128)(2,1)S(1)} %collective-permute-done.3.refs_2_.refs_3_), channel_id=1, source_target_pairs={{0,24},{8,16},{16,8},{24,0},{1,25},{9,17},{17,9},{25,1},{2,26},{10... | collective-permute-start | bytes 368648 | tf_op jit(solution)/shard_map/ppermute | solution.py:31
  29.3 1.5 %collective-permute-start.9 = (f32[384,128]{1,0:T(8,128)S(1)}, f32[384,128]{1,0:T(8,128)S(1)}, u32[]{:S(2)}, u32[]{:S(2)}) collective-permute-start(f32[384,128]{1,0:T(8,128)S(1)} %get-tuple-element.50.term_ref), channel_id=1, source_target_pairs={{0,1},{1,0},{2,3},{3,2},{4,5},{5,4},{6,7},{7,6},{8,9},{9,8},{10,11... | collective-permute-start | bytes 589832 | tf_op jit(solution)/shard_map/ppermute | solution.py:31
  30.9 1.8 %collective-permute-start.13 = (bf16[192,1024]{1,0:T(8,128)(2,1)S(1)}, bf16[192,1024]{1,0:T(8,128)(2,1)S(1)}, u32[]{:S(2)}, u32[]{:S(2)}) collective-permute-start(bf16[192,1024]{1,0:T(8,128)(2,1)S(1)} %hold.4), channel_id=1, source_target_pairs={{0,1},{1,0},{2,3},{3,2},{4,5},{5,4},{6,7},{7,6},{8,9},{9,8},{10,11... | collective-permute-start | bytes 1179656 | tf_op jit(solution)/shard_map/ppermute | solution.py:31
  31.2 5.3 %copy-start.5 = (f32[64]{0:T(128)S(1)}, f32[64]{0:T(128)}, u32[]{:S(2)}) copy-start(f32[64]{0:T(128)} %param.9) | copy-start | bytes 772
  31.2 7.9 %collective-permute-start.10 = (f32[384,128]{1,0:T(8,128)S(1)}, f32[384,128]{1,0:T(8,128)S(1)}, u32[]{:S(2)}, u32[]{:S(2)}) collective-permute-start(f32[384,128]{1,0:T(8,128)S(1)} %hold.3), channel_id=1, source_target_pairs={{0,1},{1,0},{2,3},{3,2},{4,5},{5,4},{6,7},{7,6},{8,9},{9,8},{10,11... | collective-permute-start | bytes 589832 | tf_op jit(solution)/shard_map/ppermute | solution.py:31
  31.6 4.9 %copy-start.4 = (bf16[1024,64]{0,1:T(8,128)(2,1)S(1)}, bf16[1024,64]{0,1:T(8,128)(2,1)}, u32[]{:S(2)}) copy-start(bf16[1024,64]{0,1:T(8,128)(2,1)} %param.8) | copy-start | bytes 393220
  31.6 4.8 %collective-permute-start.11 = (bf16[384,128]{1,0:T(8,128)(2,1)S(1)}, bf16[384,128]{1,0:T(8,128)(2,1)S(1)}, u32[]{:S(2)}, u32[]{:S(2)}) collective-permute-start(bf16[384,128]{1,0:T(8,128)(2,1)S(1)} %get-tuple-element.52), channel_id=1, source_target_pairs={{0,2},{1,3},{2,0},{3,1},{4,6},{5,7},{6,4},{7,5},{8,10},{9,11},{10,... | collective-permute-start | bytes 294920 | tf_op jit(solution)/shard_map/ppermute | solution.py:31
  38.0 6.4 %collective-permute-start.15 = (bf16[544,128]{1,0:T(8,128)(2,1)S(1)}, bf16[544,128]{1,0:T(8,128)(2,1)S(1)}, u32[]{:S(2)}, u32[]{:S(2)}) collective-permute-start(bf16[544,128]{1,0:T(8,128)(2,1)S(1)} %get-tuple-element.58.refs_0_), channel_id=1, source_target_pairs={{0,4},{4,0},{1,5},{5,1},{2,6},{6,2},{3,7},{7,3},{8,12},{12,8},{9,1... | collective-permute-start | bytes 417800 | tf_op jit(solution)/shard_map/ppermute | solution.py:31
  39.2 7.4 %collective-permute-start.14 = (f32[192,128]{1,0:T(8,128)S(1)}, f32[192,128]{1,0:T(8,128)S(1)}, u32[]{:S(2)}, u32[]{:S(2)}) collective-permute-start(f32[192,128]{1,0:T(8,128)S(1)} %hold.5), channel_id=1, source_target_pairs={{0,2},{1,3},{2,0},{3,1},{4,6},{5,7},{6,4},{7,5},{8,10},{9,11},{10,... | collective-permute-start | bytes 294920 | tf_op jit(solution)/shard_map/ppermute | solution.py:31
  39.8 6.8 %collective-permute-start.18 = (bf16[272,128]{1,0:T(8,128)(2,1)S(1)}, bf16[272,128]{1,0:T(8,128)(2,1)S(1)}, u32[]{:S(2)}, u32[]{:S(2)}) collective-permute-start(bf16[272,128]{1,0:T(8,128)(2,1)S(1)} %get-tuple-element.64), channel_id=1, source_target_pairs={{0,4},{4,0},{1,5},{5,1},{2,6},{6,2},{3,7},{7,3},{8,12},{12,8},{9,1... | collective-permute-start | bytes 208904 | tf_op jit(solution)/shard_map/ppermute | solution.py:31
  40.8 8.9 %collective-permute-start.20 = (bf16[272,128]{1,0:T(8,128)(2,1)S(1)}, bf16[272,128]{1,0:T(8,128)(2,1)S(1)}, u32[]{:S(2)}, u32[]{:S(2)}) collective-permute-start(bf16[272,128]{1,0:T(8,128)(2,1)S(1)} %get-tuple-element.66), channel_id=1, source_target_pairs={{0,4},{4,0},{1,5},{5,1},{2,6},{6,2},{3,7},{7,3},{8,12},{12,8},{9,1... | collective-permute-start | bytes 208904 | tf_op jit(solution)/shard_map/ppermute | solution.py:31
  44.5 6.8 %collective-permute-start.16 = (bf16[272,128]{1,0:T(8,128)(2,1)S(1)}, bf16[272,128]{1,0:T(8,128)(2,1)S(1)}, u32[]{:S(2)}, u32[]{:S(2)}) collective-permute-start(bf16[272,128]{1,0:T(8,128)(2,1)S(1)} %get-tuple-element.62.refs_2_), channel_id=1, source_target_pairs={{0,16},{8,24},{16,0},{24,8},{1,17},{9,25},{17,1},{25,9},{2,18},{10... | collective-permute-start | bytes 208904 | tf_op jit(solution)/shard_map/ppermute | solution.py:31
  46.5 4.8 %collective-permute-start.19 = (bf16[272,128]{1,0:T(8,128)(2,1)S(1)}, bf16[272,128]{1,0:T(8,128)(2,1)S(1)}, u32[]{:S(2)}, u32[]{:S(2)}) collective-permute-start(bf16[272,128]{1,0:T(8,128)(2,1)S(1)} %relay.3), channel_id=1, source_target_pairs={{0,8},{8,0},{16,24},{24,16},{1,9},{9,1},{17,25},{25,17},{2,10},{10... | collective-permute-start | bytes 208904 | tf_op jit(solution)/shard_map/ppermute | solution.py:31
  47.0 6.1 %collective-permute-start.17 = (bf16[272,128]{1,0:T(8,128)(2,1)S(1)}, bf16[272,128]{1,0:T(8,128)(2,1)S(1)}, u32[]{:S(2)}, u32[]{:S(2)}) collective-permute-start(bf16[272,128]{1,0:T(8,128)(2,1)S(1)} %get-tuple-element.63), channel_id=1, source_target_pairs={{0,24},{8,16},{16,8},{24,0},{1,25},{9,17},{17,9},{25,1},{2,26},{10... | collective-permute-start | bytes 208904 | tf_op jit(solution)/shard_map/ppermute | solution.py:31

commit v5 on v4

--- a/solution.py
+++ b/solution.py
@@ -286,7 +286,8 @@
     )(xa, xb, w_first, *after)
 
 
-def merge_body(term_ref, got_ref, sum_ref, out_ref):
+def merge_body(term_ref, got_ref, x_ref, sum_ref, out_ref, passed_ref):
+    passed_ref[...] = x_ref[...]
     rows = term_ref.shape[0] // 2
     feat = term_ref.shape[1] // 2
     for at, theirs in ((0, rows), (rows, 0)):
@@ -295,37 +296,24 @@
         out_ref[at : at + rows, :] = jnp.concatenate([both[:, feat:], both[:, :feat]], axis=1).astype(BF16)
 
 
-def merge(term, got):
+def merge(term, got, x):
+    shapes = ((got.shape, F32), (got.shape, BF16), (x.shape, BF16))
     return pl.pallas_call(
         merge_body,
-        in_specs=[VMEM] * 2,
-        out_specs=(VMEM, VMEM),
-        out_shape=(jax.ShapeDtypeStruct(got.shape, F32), jax.ShapeDtypeStruct(got.shape, BF16)),
+        in_specs=[VMEM] * 3,
+        out_specs=(VMEM,) * 3,
+        out_shape=tuple(jax.ShapeDtypeStruct(*shape) for shape in shapes),
         compiler_params=params(),
         name="merge",
-    )(term, got)
-
-
-def finish_body(scale, term_ref, far_ref, inv_ref, *refs):
+    )(term, got, x)
+
+
+def grads_body(pieces, share, scale, term_ref, far_ref, inv_ref, w2t_ref, slope_a, xt_a, ht_a, slope_b, xt_b, ht_b, *out_refs):
+    feat, hid = w2t_ref.shape
+    half = term_ref.shape[0] // 2
     inv = jnp.concatenate([inv_ref[...], inv_ref[...]], axis=1)
-    refs[-1][...] = (scale * inv * (term_ref[...] + far_ref[...].astype(F32))).astype(BF16)
-
-
-def finish(scale, term, far, inv_row, after):
-    return pl.pallas_call(
-        lambda *refs: finish_body(scale, *refs),
-        in_specs=[VMEM] * 3 + [ANY] * len(after),
-        out_specs=VMEM,
-        out_shape=jax.ShapeDtypeStruct(term.shape, BF16),
-        compiler_params=params(),
-        name="finish",
-    )(term, far, inv_row, *after)
-
-
-def grads_body(pieces, share, d_ref, w2t_ref, slope_a, xt_a, ht_a, slope_b, xt_b, ht_b, *out_refs):
-    feat, hid = w2t_ref.shape
-    half = d_ref.shape[0] // 2
-    d, e = d_ref[:half, :], d_ref[half:, :]
+    dfeat = (scale * inv * (term_ref[...] + far_ref[...].astype(F32))).astype(BF16)
+    d, e = dfeat[:half, :], dfeat[half:, :]
     dfeat_a = jnp.concatenate([d[:, :feat], e[:, :feat]], axis=0)
     dfeat_b = jnp.concatenate([d[:, feat:], e[:, feat:]], axis=0)
     size = dense_rows(share, hid, feat)
@@ -361,18 +349,18 @@
     return share * (hid + feat) // 128
 
 
-def grads(dfeat, w2t, group_a, group_b, pieces, share):
+def grads(scale, term, far, inv_row, w2t, group_a, group_b, pieces, share):
     feat, hid = w2t.shape
     size = dense_rows(share, hid, feat)
     shapes = [(group_a[1].shape[0], hid + feat)] if pieces is None else [(count * size, 128) for count in pieces]
     return pl.pallas_call(
-        lambda *refs: grads_body(pieces, share, *refs),
-        in_specs=[VMEM] * 8,
+        lambda *refs: grads_body(pieces, share, scale, *refs),
+        in_specs=[VMEM] * 10,
         out_specs=(VMEM,) * len(shapes),
         out_shape=tuple(jax.ShapeDtypeStruct(shape, BF16) for shape in shapes),
         compiler_params=params(),
         name="grads",
-    )(dfeat, w2t, *group_a, *group_b)
+    )(term, far, inv_row, w2t, *group_a, *group_b)
 
 
 def relay_body(count, got_ref, *refs):
@@ -457,8 +445,8 @@
     far_row = swap(own, "kc", 2)
     tall_masks = range(1, tall)
     if order:
-        z_two, z_one, y_own = swap(own, "enc", 2), swap(own, "enc", 1), swap(own, "kr", 1)
-        (z_both,) = gate(([z_one, z_two],), (y_own, group_a[1]))
+        z_one, z_two, y_own = swap(own, "enc", 1), swap(own, "enc", 2), swap(own, "kr", 1)
+        (z_both,) = gate(([z_one, z_two],), (y_own, far_row, group_a[1]))
         (row_both,) = gate(([own, far_row],), (z_both,))
         core_both = swap(row_both, "kc", 1)
         calls = [
@@ -483,18 +471,18 @@
     for i, (blocks, counts) in enumerate(calls):
         sofar = pairs(own_rows, rowa, rsp, blocks, counts, sofar, i == len(calls) - 1)
     stay, gone, term = sofar
-    term, moved = merge(term, swap(term, "kc", 1))
-    x_both = swap(hold(x_far, (term,)), "kc", 1)
+    term, moved, x_sent = merge(term, swap(term, "kc", 1), x_far)
+    x_both = swap(x_sent, "kc", 1)
     group_b = prepare(x_far, x_both, w_first, share, order, (term,))
     lscale = loss_gain / math.sqrt(probe_width)
-    dfeat = finish(-lscale, term, swap(moved, "kc", 2), inv_row, (group_b[1],))
     stay = stay + swap(hold(gone, (term,)), "kc", 1)
-    parts = grads(dfeat, w2t, group_a, group_b, (2, 1, 1, 1, 1, 1, 1) if order else None, share)
+    pieces = (2, 1, 1, 1, 1, 1, 1) if order else None
+    parts = grads(-lscale, term, swap(moved, "kc", 2), inv_row, w2t, group_a, group_b, pieces, share)
     far = swap(hold(stay[own_rows:], (parts[0],)), "kc", 2)
     if order:
         two, three = relay(swap(parts[0], "kr", 1), parts[3:5], (BF16, BF16))
-        (one,) = relay(swap(parts[1], "kr", 1), parts[5:6], (BF16,), (two, far))
-        got = [parts[6], swap(two, "enc", 2), swap(three, "enc", 3), swap(one, "enc", 1), swap(parts[2], "kr", 1)]
+        (one,) = relay(swap(parts[1], "kr", 1), parts[5:6], (BF16,), (three, far))
+        got = [swap(three, "enc", 3), swap(two, "enc", 2), parts[6], swap(one, "enc", 1), swap(parts[2], "kr", 1)]
     else:
         flat = lax.all_to_all(parts[0], ("enc", "kr"), 0, 0, tiled=True)
         got = list(flat.astype(F32).reshape(lines, share, hid + feat))

time: 54 us -> 53.1 us (0.983)
  waiting for transfers between devices: 11.2 us -> 9.63 us
  starting transfers between devices: 23.3 us -> 24.1 us
    ppermute x21, waiting for transfers between devices: 11.2 us -> 9.63 us  [swap(): return lax.ppermute(x, axis, [(i, i ^ mask) for i in range(size)])]
    ppermute x21, starting transfers between devices: 23.3 us -> 24.1 us  [swap(): return lax.ppermute(x, axis, [(i, i ^ mask) for i in range(size)])]
    pallas_call x3 -> x2, Pallas kernels: 1.67 us -> 1.66 us  [the longest x1 1.56 us: grads(): pl.pallas_call(lambda *refs: grads_body(pieces, share, scale, *refs), in_...]
  transfers between devices with their start and end apart: 21 -> 21, of which waited for: 8 -> 9; matrix products, arithmetic and copies ran while one was open for 1% -> 1% of each run, Pallas kernels for 30% -> 30%
where the time goes in v5:
time: 53.1 us; the launch traced here: 53 us
  starting transfers between devices  24.1 us (45%)
  Pallas kernels  16.8 us (32%)
  waiting for transfers between devices  9.63 us (18%)
  local copies, waits for them, and re-layouts  0.95 us (2%)
  between operations  0.86 us (2%)
  other arithmetic  0.66 us (1%)
    ppermute x21, starting transfers between devices, swap(): return lax.ppermute(x, axis, [(i, i ^ mask) for i in range(size)])  24.1 us
    ppermute x21, waiting for transfers between devices, swap(): return lax.ppermute(x, axis, [(i, i ^ mask) for i in range(size)])  9.63 us
    pallas_call x4, Pallas kernels, pairs(): pl.pallas_call(lambda *refs: pair_body(own_rows, counts, first, last, *re...  5.47 us
    pallas_call x2, Pallas kernels, prepare(): pl.pallas_call(lambda *refs: prepare_body(share, order, *refs), in_specs=...  4.76 us
    pallas_call x1, Pallas kernels, encode(): pl.pallas_call(encode_body, in_specs=[HBM] * 6, out_specs=VMEM, out_shape...  3.52 us
    pallas_call x1, Pallas kernels, grads(): pl.pallas_call(lambda *refs: grads_body(pieces, share, scale, *refs), in_...  1.56 us
  transfers between devices with their start and end apart: 21, of which 9 were waited for; matrix products, arithmetic and copies ran while one was open for 1% of the time, Pallas kernels for 30%

profile of v5, /device:TPU:0, one launch (start us, length us, event | category | flops | bytes accessed | tf_op | source)
XLA Modules:
  0.0 53.0 jit_solution(6637970185925300530)
XLA Ops:
  0.6 0.0 copy-start.1
  0.6 0.0 copy-start
  0.7 0.5 collective-permute-start.4
  1.2 3.5 %encode.1.refs_3_.refs_0_ = bf16[480,128]{1,0:T(8,128)(2,1)} custom-call(bf16[192,1024]{1,0:T(8,128)(2,1)} %refs_0_.1, bf16[1024,1024]{1,0:T(8,128)(2,1)} %refs_2_.3, bf16[64,1024]{1,0:T(8,128)(2,1)} %bitcast.2, f32[1,64]{1,0:T(1,128)} %bitcast.4, bf16[192,128]{1,0:T(8,128)(2,1)} %probe_hbm.1, bf16[192,128]{1,0:T(8,128)(2,1)} %solve_hbm.1), custom_call_target="tpu_custom_call" | custom-call | tf_op jit(solution)/shard_map/encode/pallas_call | solution.py:86
  4.7 3.6 %collective-permute-start.2 = (bf16[480,128]{1,0:T(8,128)(2,1)}, bf16[480,128]{1,0:T(8,128)(2,1)S(1)}, u32[]{:S(2)}, u32[]{:S(2)}) collective-permute-start(bf16[480,128]{1,0:T(8,128)(2,1)} %encode.1.refs_3_.refs_0_), channel_id=1, source_target_pairs={{0,16},{8,24},{16,0},{24,8},{1,17},{9,25},{17,1},{25,9},{2,18},{10... | collective-permute-start | bytes 368648 | tf_op jit(solution)/shard_map/ppermute | solution.py:31
  8.3 1.5 %collective-permute-start.3 = (bf16[480,128]{1,0:T(8,128)(2,1)}, bf16[480,128]{1,0:T(8,128)(2,1)S(1)}, u32[]{:S(2)}, u32[]{:S(2)}) collective-permute-start(bf16[480,128]{1,0:T(8,128)(2,1)} %encode.1.refs_3_.refs_0_), channel_id=1, source_target_pairs={{0,4},{4,0},{1,5},{5,1},{2,6},{6,2},{3,7},{7,3},{8,12},{12,8},{9,1... | collective-permute-start | bytes 368648 | tf_op jit(solution)/shard_map/ppermute | solution.py:31
  9.8 1.5 %collective-permute-start = (bf16[480,128]{1,0:T(8,128)(2,1)}, bf16[480,128]{1,0:T(8,128)(2,1)S(1)}, u32[]{:S(2)}, u32[]{:S(2)}) collective-permute-start(bf16[480,128]{1,0:T(8,128)(2,1)} %encode.1.refs_3_.refs_0_), channel_id=1, source_target_pairs={{0,2},{1,3},{2,0},{3,1},{4,6},{5,7},{6,4},{7,5},{8,10},{9,11},{10,... | collective-permute-start | bytes 368648 | tf_op jit(solution)/shard_map/ppermute | solution.py:31
  11.3 1.6 %collective-permute-start.1 = (bf16[480,128]{1,0:T(8,128)(2,1)}, bf16[480,128]{1,0:T(8,128)(2,1)S(1)}, u32[]{:S(2)}, u32[]{:S(2)}) collective-permute-start(bf16[480,128]{1,0:T(8,128)(2,1)} %encode.1.refs_3_.refs_0_), channel_id=1, source_target_pairs={{0,8},{8,0},{16,24},{24,16},{1,9},{9,1},{17,25},{25,17},{2,10},{10... | collective-permute-start | bytes 368648 | tf_op jit(solution)/shard_map/ppermute | solution.py:31
  12.9 0.0 collective-permute-done.4.refs_1_
  12.9 0.0 copy-done.1
  12.9 0.0 copy-done
  12.9 0.0 copy-start.2
  12.9 0.9 %copy-done.2 = bf16[480,128]{1,0:T(8,128)(2,1)S(1)} copy-done((bf16[480,128]{1,0:T(8,128)(2,1)S(1)}, bf16[480,128]{1,0:T(8,128)(2,1)}, u32[]{:S(2)}) %copy-start.2) | copy-done | bytes 122904
  13.8 2.4 %prepare.2 = (f32[384,1024]{1,0:T(8,128)S(1)}, bf16[256,384]{1,0:T(8,128)(2,1)S(1)}, bf16[256,384]{1,0:T(8,128)(2,1)S(1)}) custom-call(bf16[192,1024]{1,0:T(8,128)(2,1)S(1)} %copy-done.1, bf16[192,1024]{1,0:T(8,128)(2,1)S(1)} %collective-permute-done.4.refs_1_, bf16[1024,1024]{1,0:T(8,128)(2,1)S(1)} %copy-done, bf16[480,128]{1,0:T(8,128)(2,1)S(1)} %copy-done.2), custom_call_target="tpu_custom_call" | custom-call | flops 1 | bytes 1048576 | tf_op jit(solution)/shard_map/prepare/pallas_call | solution.py:278
  16.2 0.0 collective-permute-done.2.refs_1_.refs_3_
  16.2 0.0 collective-permute-done.3.refs_2_.refs_3_
  16.2 0.0 collective-permute-done.refs_3_.refs_1_
  16.2 1.4 %collective-permute-done.1.refs_0_.refs_2_ = bf16[480,128]{1,0:T(8,128)(2,1)S(1)} collective-permute-done((bf16[480,128]{1,0:T(8,128)(2,1)}, bf16[480,128]{1,0:T(8,128)(2,1)S(1)}, u32[]{:S(2)}, u32[]{:S(2)}) %collective-permute-start.1) | collective-permute-done | bytes 122912 | tf_op jit(solution)/shard_map/ppermute | solution.py:31
  17.6 0.0 copy-done.3
  17.7 0.1 collective-permute-start.5
  17.8 0.7 %collective-permute-start.8 = (bf16[960,128]{1,0:T(8,128)(2,1)S(1)}, bf16[960,128]{1,0:T(8,128)(2,1)S(1)}, u32[]{:S(2)}, u32[]{:S(2)}) collective-permute-start(bf16[960,128]{1,0:T(8,128)(2,1)S(1)} %gate.2.refs_2_), channel_id=1, source_target_pairs={{0,4},{4,0},{1,5},{5,1},{2,6},{6,2},{3,7},{7,3},{8,12},{12,8},{9,1... | collective-permute-start | bytes 737288 | tf_op jit(solution)/shard_map/ppermute | solution.py:31
  18.5 0.6 %collective-permute-start.10 = (bf16[192,1024]{1,0:T(8,128)(2,1)S(1)}, bf16[192,1024]{1,0:T(8,128)(2,1)S(1)}, u32[]{:S(2)}, u32[]{:S(2)}) collective-permute-start(bf16[192,1024]{1,0:T(8,128)(2,1)S(1)} %copy-done.1), channel_id=1, source_target_pairs={{0,2},{1,3},{2,0},{3,1},{4,6},{5,7},{6,4},{7,5},{8,10},{9,11},{10,... | collective-permute-start | bytes 1179656 | tf_op jit(solution)/shard_map/ppermute | solution.py:31
  19.1 0.9 %collective-permute-start.6 = (bf16[480,128]{1,0:T(8,128)(2,1)S(1)}, bf16[480,128]{1,0:T(8,128)(2,1)S(1)}, u32[]{:S(2)}, u32[]{:S(2)}) collective-permute-start(bf16[480,128]{1,0:T(8,128)(2,1)S(1)} %collective-permute-done.2.refs_1_.refs_3_), channel_id=1, source_target_pairs={{0,8},{8,0},{16,24},{24,16},{1,9},{9,1},{17,25},{25,17},{2,10},{10... | collective-permute-start | bytes 368648 | tf_op jit(solution)/shard_map/ppermute | solution.py:31
  20.0 1.8 %collective-permute-start.7 = (bf16[480,128]{1,0:T(8,128)(2,1)S(1)}, bf16[480,128]{1,0:T(8,128)(2,1)S(1)}, u32[]{:S(2)}, u32[]{:S(2)}) collective-permute-start(bf16[480,128]{1,0:T(8,128)(2,1)S(1)} %collective-permute-done.3.refs_2_.refs_3_), channel_id=1, source_target_pairs={{0,24},{8,16},{16,8},{24,0},{1,25},{9,17},{17,9},{25,1},{2,26},{10... | collective-permute-start | bytes 368648 | tf_op jit(solution)/shard_map/ppermute | solution.py:31
  21.8 0.0 collective-permute-done.5.refs_1_
  21.8 0.5 %rows.1 = (bf16[768,256]{1,0:T(8,128)(2,1)S(1)}, bf16[768,256]{1,0:T(8,128)(2,1)S(1)}) custom-call(bf16[960,128]{1,0:T(8,128)(2,1)S(1)} %gate.3.refs_0_.refs_2_, bf16[960,128]{1,0:T(8,128)(2,1)S(1)} %collective-permute-done.5.refs_1_), custom_call_target="tpu_custom_call" | custom-call | tf_op jit(solution)/shard_map/rows/pallas_call | solution.py:159
  22.3 1.3 %pairs.4 = (f32[768,128]{1,0:T(8,128)S(1)}, f32[768,64]{1,0:T(8,128)S(1)}, f32[768,128]{1,0:T(8,128)S(1)}) custom-call(bf16[768,256]{1,0:T(8,128)(2,1)S(1)} %get-tuple-element.38.refs_0_, bf16[768,256]{1,0:T(8,128)(2,1)S(1)} %get-tuple-element.39.refs_1_, bf16[960,128]{1,0:T(8,128)(2,1)S(1)} %gate.3.refs_0_.refs_2_, ...), custom_call_target="tpu_custom_call" | custom-call | flops 1 | bytes 884736 | tf_op jit(solution)/shard_map/pairs/pallas_call | solution.py:229
  23.6 1.4 %pairs.5 = (f32[768,128]{1,0:T(8,128)S(1)}, f32[768,64]{1,0:T(8,128)S(1)}, f32[768,128]{1,0:T(8,128)S(1)}) custom-call(bf16[768,256]{1,0:T(8,128)(2,1)S(1)} %get-tuple-element.38.refs_0_, bf16[768,256]{1,0:T(8,128)(2,1)S(1)} %get-tuple-element.39.refs_1_, bf16[480,128]{1,0:T(8,128)(2,1)S(1)} %collective-permute-done.1.refs_0_.refs_2_, ...), custom_call_target="tpu_custom_call" | custom-call | flops 1 | bytes 884736 | tf_op jit(solution)/shard_map/pairs/pallas_call | solution.py:229
  25.0 1.1 %collective-permute-done.8.refs_2_ = bf16[960,128]{1,0:T(8,128)(2,1)S(1)} collective-permute-done((bf16[960,128]{1,0:T(8,128)(2,1)S(1)}, bf16[960,128]{1,0:T(8,128)(2,1)S(1)}, u32[]{:S(2)}, u32[]{:S(2)}) %collective-permute-start.8) | collective-permute-done | bytes 245792 | tf_op jit(solution)/shard_map/ppermute | solution.py:31
  26.1 1.4 %pairs.6 = (f32[768,128]{1,0:T(8,128)S(1)}, f32[768,64]{1,0:T(8,128)S(1)}, f32[768,128]{1,0:T(8,128)S(1)}) custom-call(bf16[768,256]{1,0:T(8,128)(2,1)S(1)} %get-tuple-element.38.refs_0_, bf16[768,256]{1,0:T(8,128)(2,1)S(1)} %get-tuple-element.39.refs_1_, bf16[960,128]{1,0:T(8,128)(2,1)S(1)} %collective-permute-done.8.refs_2_, ...), custom_call_target="tpu_custom_call" | custom-call | flops 1 | bytes 884736 | tf_op jit(solution)/shard_map/pairs/pallas_call | solution.py:229
  27.5 0.0 collective-permute-done.6.refs_2_
  27.5 0.4 collective-permute-done.7.refs_3_
  27.9 1.4 %pairs.7 = (f32[384,128]{1,0:T(8,128)S(1)}, f32[384,128]{1,0:T(8,128)S(1)}, f32[384,128]{1,0:T(8,128)S(1)}) custom-call(bf16[768,256]{1,0:T(8,128)(2,1)S(1)} %get-tuple-element.38.refs_0_, bf16[768,256]{1,0:T(8,128)(2,1)S(1)} %get-tuple-element.39.refs_1_, bf16[480,128]{1,0:T(8,128)(2,1)S(1)} %collective-permute-done.6.refs_2_, ...), custom_call_target="tpu_custom_call" | custom-call | flops 1 | bytes 884736 | tf_op jit(solution)/shard_map/pairs/pallas_call | solution.py:229
  29.3 0.1 collective-permute-start.9
  29.4 0.3 collective-permute-done.10.x_ref.refs_0_
  29.7 1.1 %collective-permute-done.9.got_ref = f32[384,128]{1,0:T(8,128)S(1)} collective-permute-done((f32[384,128]{1,0:T(8,128)S(1)}, f32[384,128]{1,0:T(8,128)S(1)}, u32[]{:S(2)}, u32[]{:S(2)}) %collective-permute-start.9) | collective-permute-done | bytes 196640 | tf_op jit(solution)/shard_map/ppermute | solution.py:31
  30.8 0.1 merge.1
  30.9 0.2 collective-permute-start.13
  31.1 0.0 copy-start.4
  31.1 0.0 copy-start.5
  31.1 0.4 collective-permute-start.11
  31.6 1.3 %collective-permute-start.12 = (bf16[384,128]{1,0:T(8,128)(2,1)S(1)}, bf16[384,128]{1,0:T(8,128)(2,1)S(1)}, u32[]{:S(2)}, u32[]{:S(2)}) collective-permute-start(bf16[384,128]{1,0:T(8,128)(2,1)S(1)} %get-tuple-element.53), channel_id=1, source_target_pairs={{0,2},{1,3},{2,0},{3,1},{4,6},{5,7},{6,4},{7,5},{8,10},{9,11},{10,... | collective-permute-start | bytes 294920 | tf_op jit(solution)/shard_map/ppermute | solution.py:31
  32.9 0.0 collective-permute-done.13.refs_1_
  32.9 2.4 %prepare.3 = (f32[384,1024]{1,0:T(8,128)S(1)}, bf16[256,384]{1,0:T(8,128)(2,1)S(1)}, bf16[256,384]{1,0:T(8,128)(2,1)S(1)}) custom-call(bf16[192,1024]{1,0:T(8,128)(2,1)S(1)} %collective-permute-done.10.x_ref.refs_0_, bf16[192,1024]{1,0:T(8,128)(2,1)S(1)} %collective-permute-done.13.refs_1_, bf16[1024,1024]{1,0:T(8,128)(2,1)S(1)} %copy-done, ...), custom_call_target="tpu_custom_call" | custom-call | flops 1 | bytes 1048576 | tf_op jit(solution)/shard_map/prepare/pallas_call | solution.py:278
  35.2 1.2 %collective-permute-done.12.refs_1_ = bf16[384,128]{1,0:T(8,128)(2,1)S(1)} collective-permute-done((bf16[384,128]{1,0:T(8,128)(2,1)S(1)}, bf16[384,128]{1,0:T(8,128)(2,1)S(1)}, u32[]{:S(2)}, u32[]{:S(2)}) %collective-permute-start.12) | collective-permute-done | bytes 98336 | tf_op jit(solution)/shard_map/ppermute | solution.py:31
  36.4 0.0 copy-done.4
  36.4 1.6 %grads.1 = (bf16[544,128]{1,0:T(8,128)(2,1)S(1)}, bf16[272,128]{1,0:T(8,128)(2,1)S(1)}, bf16[272,128]{1,0:T(8,128)(2,1)S(1)}, bf16[272,128]{1,0:T(8,128)(2,1)S(1...) custom-call(f32[384,128]{1,0:T(8,128)S(1)} %get-tuple-element.52.refs_0_.refs_3_, ...), custom_call_target="tpu_custom_call" | custom-call | tf_op jit(solution)/shard_map/grads/pallas_call | solution.py:356
  38.0 1.4 %collective-permute-start.15 = (bf16[544,128]{1,0:T(8,128)(2,1)S(1)}, bf16[544,128]{1,0:T(8,128)(2,1)S(1)}, u32[]{:S(2)}, u32[]{:S(2)}) collective-permute-start(bf16[544,128]{1,0:T(8,128)(2,1)S(1)} %get-tuple-element.60.refs_0_), channel_id=1, source_target_pairs={{0,4},{4,0},{1,5},{5,1},{2,6},{6,2},{3,7},{7,3},{8,12},{12,8},{9,1... | collective-permute-start | bytes 417800 | tf_op jit(solution)/shard_map/ppermute | solution.py:31
  39.3 0.0 collective-permute-done.11
  39.4 1.4 %collective-permute-start.14 = (f32[192,128]{1,0:T(8,128)S(1)}, f32[192,128]{1,0:T(8,128)S(1)}, u32[]{:S(2)}, u32[]{:S(2)}) collective-permute-start(f32[192,128]{1,0:T(8,128)S(1)} %hold.3), channel_id=1, source_target_pairs={{0,2},{1,3},{2,0},{3,1},{4,6},{5,7},{6,4},{7,5},{8,10},{9,11},{10,... | collective-permute-start | bytes 294920 | tf_op jit(solution)/shard_map/ppermute | solution.py:31
  40.8 0.6 %collective-permute-start.18 = (bf16[272,128]{1,0:T(8,128)(2,1)S(1)}, bf16[272,128]{1,0:T(8,128)(2,1)S(1)}, u32[]{:S(2)}, u32[]{:S(2)}) collective-permute-start(bf16[272,128]{1,0:T(8,128)(2,1)S(1)} %get-tuple-element.66), channel_id=1, source_target_pairs={{0,4},{4,0},{1,5},{5,1},{2,6},{6,2},{3,7},{7,3},{8,12},{12,8},{9,1... | collective-permute-start | bytes 208904 | tf_op jit(solution)/shard_map/ppermute | solution.py:31
  41.5 1.4 %collective-permute-start.20 = (bf16[272,128]{1,0:T(8,128)(2,1)S(1)}, bf16[272,128]{1,0:T(8,128)(2,1)S(1)}, u32[]{:S(2)}, u32[]{:S(2)}) collective-permute-start(bf16[272,128]{1,0:T(8,128)(2,1)S(1)} %get-tuple-element.68), channel_id=1, source_target_pairs={{0,4},{4,0},{1,5},{5,1},{2,6},{6,2},{3,7},{7,3},{8,12},{12,8},{9,1... | collective-permute-start | bytes 208904 | tf_op jit(solution)/shard_map/ppermute | solution.py:31
  42.9 1.2 %collective-permute-done.15.refs_0_ = bf16[544,128]{1,0:T(8,128)(2,1)S(1)} collective-permute-done((bf16[544,128]{1,0:T(8,128)(2,1)S(1)}, bf16[544,128]{1,0:T(8,128)(2,1)S(1)}, u32[]{:S(2)}, u32[]{:S(2)}) %collective-permute-start.15) | collective-permute-done | bytes 139296 | tf_op jit(solution)/shard_map/ppermute | solution.py:31
  44.1 2.8 %collective-permute-start.16 = (bf16[272,128]{1,0:T(8,128)(2,1)S(1)}, bf16[272,128]{1,0:T(8,128)(2,1)S(1)}, u32[]{:S(2)}, u32[]{:S(2)}) collective-permute-start(bf16[272,128]{1,0:T(8,128)(2,1)S(1)} %get-tuple-element.63.refs_2_), channel_id=1, source_target_pairs={{0,24},{8,16},{16,8},{24,0},{1,25},{9,17},{17,9},{25,1},{2,26},{10... | collective-permute-start | bytes 208904 | tf_op jit(solution)/shard_map/ppermute | solution.py:31
  46.9 0.0 collective-permute-done.18.refs_0_
  46.9 0.0 collective-permute-done.14.refs_3_
  46.9 0.1 collective-permute-start.19
  47.0 1.7 %collective-permute-start.17 = (bf16[272,128]{1,0:T(8,128)(2,1)S(1)}, bf16[272,128]{1,0:T(8,128)(2,1)S(1)}, u32[]{:S(2)}, u32[]{:S(2)}) collective-permute-start(bf16[272,128]{1,0:T(8,128)(2,1)S(1)} %get-tuple-element.64), channel_id=1, source_target_pairs={{0,16},{8,24},{16,0},{24,8},{1,17},{9,25},{17,1},{25,9},{2,18},{10... | collective-permute-start | bytes 208904 | tf_op jit(solution)/shard_map/ppermute | solution.py:31
  48.7 0.6 %fusion.1 = bf16[192,128]{1,0:T(8,128)(2,1)} fusion(f32[192,128]{1,0:T(8,128)S(1)} %collective-permute-done.14.refs_3_, f32[384,128]{1,0:T(8,128)S(1)} %add.6), kind=kLoop, calls=%fused_computation.2 | loop fusion | flops 73728 | bytes 245760 | tf_op jit(solution)/shard_map/convert_element_type | solution.py:492
  49.3 0.0 collective-permute-done.20.refs_4_
  49.3 2.2 %collective-permute-done.19.refs_3_ = bf16[272,128]{1,0:T(8,128)(2,1)S(1)} collective-permute-done((bf16[272,128]{1,0:T(8,128)(2,1)S(1)}, bf16[272,128]{1,0:T(8,128)(2,1)S(1)}, u32[]{:S(2)}, u32[]{:S(2)}) %collective-permute-start.19) | collective-permute-done | bytes 69664 | tf_op jit(solution)/shard_map/ppermute | solution.py:31
  51.5 0.0 collective-permute-done.16.refs_0_
  51.5 0.8 %collective-permute-done.17.refs_1_ = bf16[272,128]{1,0:T(8,128)(2,1)S(1)} collective-permute-done((bf16[272,128]{1,0:T(8,128)(2,1)S(1)}, bf16[272,128]{1,0:T(8,128)(2,1)S(1)}, u32[]{:S(2)}, u32[]{:S(2)}) %collective-permute-start.17) | collective-permute-done | bytes 69664 | tf_op jit(solution)/shard_map/ppermute | solution.py:31
  52.3 0.7 %total.1 = (f32[32,1024]{1,0:T(8,128)}, f32[32,64]{1,0:T(8,128)}) custom-call(bf16[272,128]{1,0:T(8,128)(2,1)S(1)} %collective-permute-done.16.refs_0_, bf16[272,128]{1,0:T(8,128)(2,1)S(1)} %collective-permute-done.17.refs_1_, bf16[272,128]{1,0:T(8,128)(2,1)S(1)} %get-tuple-element.65.refs_2_, bf16[272,128]{1,0:T(8,128)(2,1)S(1)} %collective-permute-done.19.refs_3_, ...), custom_call_target="tpu_custom_call" | custom-call | tf_op jit(solution)/shard_map/total/pallas_call | solution.py:406
  (10 shorter events, 0.2 us)
Async XLA Ops:
  0.6 12.3 %copy-start.1 = (bf16[192,1024]{1,0:T(8,128)(2,1)S(1)}, bf16[192,1024]{1,0:T(8,128)(2,1)}, u32[]{:S(2)}) copy-start(bf16[192,1024]{1,0:T(8,128)(2,1)} %refs_0_.1) | copy-start | bytes 1179652
  0.6 12.3 %copy-start = (bf16[1024,1024]{1,0:T(8,128)(2,1)S(1)}, bf16[1024,1024]{1,0:T(8,128)(2,1)}, u32[]{:S(2)}) copy-start(bf16[1024,1024]{1,0:T(8,128)(2,1)} %refs_2_.3) | copy-start | bytes 6291460
  0.7 12.2 %collective-permute-start.4 = (bf16[192,1024]{1,0:T(8,128)(2,1)}, bf16[192,1024]{1,0:T(8,128)(2,1)S(1)}, u32[]{:S(2)}, u32[]{:S(2)}) collective-permute-start(bf16[192,1024]{1,0:T(8,128)(2,1)} %refs_0_.1), channel_id=1, source_target_pairs={{0,1},{1,0},{2,3},{3,2},{4,5},{5,4},{6,7},{7,6},{8,9},{9,8},{10,11... | collective-permute-start | bytes 1179656 | tf_op jit(solution)/shard_map/ppermute | solution.py:31
  4.7 11.5 %collective-permute-start.2 = (bf16[480,128]{1,0:T(8,128)(2,1)}, bf16[480,128]{1,0:T(8,128)(2,1)S(1)}, u32[]{:S(2)}, u32[]{:S(2)}) collective-permute-start(bf16[480,128]{1,0:T(8,128)(2,1)} %encode.1.refs_3_.refs_0_), channel_id=1, source_target_pairs={{0,16},{8,24},{16,0},{24,8},{1,17},{9,25},{17,1},{25,9},{2,18},{10... | collective-permute-start | bytes 368648 | tf_op jit(solution)/shard_map/ppermute | solution.py:31
  8.3 7.9 %collective-permute-start.3 = (bf16[480,128]{1,0:T(8,128)(2,1)}, bf16[480,128]{1,0:T(8,128)(2,1)S(1)}, u32[]{:S(2)}, u32[]{:S(2)}) collective-permute-start(bf16[480,128]{1,0:T(8,128)(2,1)} %encode.1.refs_3_.refs_0_), channel_id=1, source_target_pairs={{0,4},{4,0},{1,5},{5,1},{2,6},{6,2},{3,7},{7,3},{8,12},{12,8},{9,1... | collective-permute-start | bytes 368648 | tf_op jit(solution)/shard_map/ppermute | solution.py:31
  9.8 6.4 %collective-permute-start = (bf16[480,128]{1,0:T(8,128)(2,1)}, bf16[480,128]{1,0:T(8,128)(2,1)S(1)}, u32[]{:S(2)}, u32[]{:S(2)}) collective-permute-start(bf16[480,128]{1,0:T(8,128)(2,1)} %encode.1.refs_3_.refs_0_), channel_id=1, source_target_pairs={{0,2},{1,3},{2,0},{3,1},{4,6},{5,7},{6,4},{7,5},{8,10},{9,11},{10,... | collective-permute-start | bytes 368648 | tf_op jit(solution)/shard_map/ppermute | solution.py:31
  11.3 6.3 %collective-permute-start.1 = (bf16[480,128]{1,0:T(8,128)(2,1)}, bf16[480,128]{1,0:T(8,128)(2,1)S(1)}, u32[]{:S(2)}, u32[]{:S(2)}) collective-permute-start(bf16[480,128]{1,0:T(8,128)(2,1)} %encode.1.refs_3_.refs_0_), channel_id=1, source_target_pairs={{0,8},{8,0},{16,24},{24,16},{1,9},{9,1},{17,25},{25,17},{2,10},{10... | collective-permute-start | bytes 368648 | tf_op jit(solution)/shard_map/ppermute | solution.py:31
  12.9 0.9 %copy-start.2 = (bf16[480,128]{1,0:T(8,128)(2,1)S(1)}, bf16[480,128]{1,0:T(8,128)(2,1)}, u32[]{:S(2)}) copy-start(bf16[480,128]{1,0:T(8,128)(2,1)} %encode.1.refs_3_.refs_0_) | copy-start | bytes 368644
  13.8 3.8 %copy-start.3 = (bf16[480,128]{1,0:T(8,128)(2,1)S(1)}, bf16[480,128]{1,0:T(8,128)(2,1)}, u32[]{:S(2)}) copy-start(bf16[480,128]{1,0:T(8,128)(2,1)} %encode.1.refs_3_.refs_0_) | copy-start | bytes 368644
  17.7 4.1 %collective-permute-start.5 = (bf16[960,128]{1,0:T(8,128)(2,1)S(1)}, bf16[960,128]{1,0:T(8,128)(2,1)S(1)}, u32[]{:S(2)}, u32[]{:S(2)}) collective-permute-start(bf16[960,128]{1,0:T(8,128)(2,1)S(1)} %gate.3.refs_0_.refs_2_), channel_id=1, source_target_pairs={{0,1},{1,0},{2,3},{3,2},{4,5},{5,4},{6,7},{7,6},{8,9},{9,8},{10,11... | collective-permute-start | bytes 737288 | tf_op jit(solution)/shard_map/ppermute | solution.py:31
  17.8 8.4 %collective-permute-start.8 = (bf16[960,128]{1,0:T(8,128)(2,1)S(1)}, bf16[960,128]{1,0:T(8,128)(2,1)S(1)}, u32[]{:S(2)}, u32[]{:S(2)}) collective-permute-start(bf16[960,128]{1,0:T(8,128)(2,1)S(1)} %gate.2.refs_2_), channel_id=1, source_target_pairs={{0,4},{4,0},{1,5},{5,1},{2,6},{6,2},{3,7},{7,3},{8,12},{12,8},{9,1... | collective-permute-start | bytes 737288 | tf_op jit(solution)/shard_map/ppermute | solution.py:31
  18.5 11.2 %collective-permute-start.10 = (bf16[192,1024]{1,0:T(8,128)(2,1)S(1)}, bf16[192,1024]{1,0:T(8,128)(2,1)S(1)}, u32[]{:S(2)}, u32[]{:S(2)}) collective-permute-start(bf16[192,1024]{1,0:T(8,128)(2,1)S(1)} %copy-done.1), channel_id=1, source_target_pairs={{0,2},{1,3},{2,0},{3,1},{4,6},{5,7},{6,4},{7,5},{8,10},{9,11},{10,... | collective-permute-start | bytes 1179656 | tf_op jit(solution)/shard_map/ppermute | solution.py:31
  19.1 8.4 %collective-permute-start.6 = (bf16[480,128]{1,0:T(8,128)(2,1)S(1)}, bf16[480,128]{1,0:T(8,128)(2,1)S(1)}, u32[]{:S(2)}, u32[]{:S(2)}) collective-permute-start(bf16[480,128]{1,0:T(8,128)(2,1)S(1)} %collective-permute-done.2.refs_1_.refs_3_), channel_id=1, source_target_pairs={{0,8},{8,0},{16,24},{24,16},{1,9},{9,1},{17,25},{25,17},{2,10},{10... | collective-permute-start | bytes 368648 | tf_op jit(solution)/shard_map/ppermute | solution.py:31
  20.0 7.9 %collective-permute-start.7 = (bf16[480,128]{1,0:T(8,128)(2,1)S(1)}, bf16[480,128]{1,0:T(8,128)(2,1)S(1)}, u32[]{:S(2)}, u32[]{:S(2)}) collective-permute-start(bf16[480,128]{1,0:T(8,128)(2,1)S(1)} %collective-permute-done.3.refs_2_.refs_3_), channel_id=1, source_target_pairs={{0,24},{8,16},{16,8},{24,0},{1,25},{9,17},{17,9},{25,1},{2,26},{10... | collective-permute-start | bytes 368648 | tf_op jit(solution)/shard_map/ppermute | solution.py:31
  29.3 1.5 %collective-permute-start.9 = (f32[384,128]{1,0:T(8,128)S(1)}, f32[384,128]{1,0:T(8,128)S(1)}, u32[]{:S(2)}, u32[]{:S(2)}) collective-permute-start(f32[384,128]{1,0:T(8,128)S(1)} %get-tuple-element.51.term_ref), channel_id=1, source_target_pairs={{0,1},{1,0},{2,3},{3,2},{4,5},{5,4},{6,7},{7,6},{8,9},{9,8},{10,11... | collective-permute-start | bytes 589832 | tf_op jit(solution)/shard_map/ppermute | solution.py:31
  30.9 2.0 %collective-permute-start.13 = (bf16[192,1024]{1,0:T(8,128)(2,1)S(1)}, bf16[192,1024]{1,0:T(8,128)(2,1)S(1)}, u32[]{:S(2)}, u32[]{:S(2)}) collective-permute-start(bf16[192,1024]{1,0:T(8,128)(2,1)S(1)} %get-tuple-element.56), channel_id=1, source_target_pairs={{0,1},{1,0},{2,3},{3,2},{4,5},{5,4},{6,7},{7,6},{8,9},{9,8},{10,11... | collective-permute-start | bytes 1179656 | tf_op jit(solution)/shard_map/ppermute | solution.py:31
  31.1 5.3 %copy-start.4 = (bf16[1024,64]{0,1:T(8,128)(2,1)S(1)}, bf16[1024,64]{0,1:T(8,128)(2,1)}, u32[]{:S(2)}) copy-start(bf16[1024,64]{0,1:T(8,128)(2,1)} %param.8) | copy-start | bytes 393220
  31.1 5.3 %copy-start.5 = (f32[64]{0:T(128)S(1)}, f32[64]{0:T(128)}, u32[]{:S(2)}) copy-start(f32[64]{0:T(128)} %param.9) | copy-start | bytes 772
  31.1 8.2 %collective-permute-start.11 = (f32[384,128]{1,0:T(8,128)S(1)}, f32[384,128]{1,0:T(8,128)S(1)}, u32[]{:S(2)}, u32[]{:S(2)}) collective-permute-start(f32[384,128]{1,0:T(8,128)S(1)} %hold.2), channel_id=1, source_target_pairs={{0,1},{1,0},{2,3},{3,2},{4,5},{5,4},{6,7},{7,6},{8,9},{9,8},{10,11... | collective-permute-start | bytes 589832 | tf_op jit(solution)/shard_map/ppermute | solution.py:31
  31.6 4.8 %collective-permute-start.12 = (bf16[384,128]{1,0:T(8,128)(2,1)S(1)}, bf16[384,128]{1,0:T(8,128)(2,1)S(1)}, u32[]{:S(2)}, u32[]{:S(2)}) collective-permute-start(bf16[384,128]{1,0:T(8,128)(2,1)S(1)} %get-tuple-element.53), channel_id=1, source_target_pairs={{0,2},{1,3},{2,0},{3,1},{4,6},{5,7},{6,4},{7,5},{8,10},{9,11},{10,... | collective-permute-start | bytes 294920 | tf_op jit(solution)/shard_map/ppermute | solution.py:31
  38.0 6.1 %collective-permute-start.15 = (bf16[544,128]{1,0:T(8,128)(2,1)S(1)}, bf16[544,128]{1,0:T(8,128)(2,1)S(1)}, u32[]{:S(2)}, u32[]{:S(2)}) collective-permute-start(bf16[544,128]{1,0:T(8,128)(2,1)S(1)} %get-tuple-element.60.refs_0_), channel_id=1, source_target_pairs={{0,4},{4,0},{1,5},{5,1},{2,6},{6,2},{3,7},{7,3},{8,12},{12,8},{9,1... | collective-permute-start | bytes 417800 | tf_op jit(solution)/shard_map/ppermute | solution.py:31
  39.4 7.5 %collective-permute-start.14 = (f32[192,128]{1,0:T(8,128)S(1)}, f32[192,128]{1,0:T(8,128)S(1)}, u32[]{:S(2)}, u32[]{:S(2)}) collective-permute-start(f32[192,128]{1,0:T(8,128)S(1)} %hold.3), channel_id=1, source_target_pairs={{0,2},{1,3},{2,0},{3,1},{4,6},{5,7},{6,4},{7,5},{8,10},{9,11},{10,... | collective-permute-start | bytes 294920 | tf_op jit(solution)/shard_map/ppermute | solution.py:31
  40.8 6.0 %collective-permute-start.18 = (bf16[272,128]{1,0:T(8,128)(2,1)S(1)}, bf16[272,128]{1,0:T(8,128)(2,1)S(1)}, u32[]{:S(2)}, u32[]{:S(2)}) collective-permute-start(bf16[272,128]{1,0:T(8,128)(2,1)S(1)} %get-tuple-element.66), channel_id=1, source_target_pairs={{0,4},{4,0},{1,5},{5,1},{2,6},{6,2},{3,7},{7,3},{8,12},{12,8},{9,1... | collective-permute-start | bytes 208904 | tf_op jit(solution)/shard_map/ppermute | solution.py:31
  41.5 7.8 %collective-permute-start.20 = (bf16[272,128]{1,0:T(8,128)(2,1)S(1)}, bf16[272,128]{1,0:T(8,128)(2,1)S(1)}, u32[]{:S(2)}, u32[]{:S(2)}) collective-permute-start(bf16[272,128]{1,0:T(8,128)(2,1)S(1)} %get-tuple-element.68), channel_id=1, source_target_pairs={{0,4},{4,0},{1,5},{5,1},{2,6},{6,2},{3,7},{7,3},{8,12},{12,8},{9,1... | collective-permute-start | bytes 208904 | tf_op jit(solution)/shard_map/ppermute | solution.py:31
  44.1 7.4 %collective-permute-start.16 = (bf16[272,128]{1,0:T(8,128)(2,1)S(1)}, bf16[272,128]{1,0:T(8,128)(2,1)S(1)}, u32[]{:S(2)}, u32[]{:S(2)}) collective-permute-start(bf16[272,128]{1,0:T(8,128)(2,1)S(1)} %get-tuple-element.63.refs_2_), channel_id=1, source_target_pairs={{0,24},{8,16},{16,8},{24,0},{1,25},{9,17},{17,9},{25,1},{2,26},{10... | collective-permute-start | bytes 208904 | tf_op jit(solution)/shard_map/ppermute | solution.py:31
  46.9 4.6 %collective-permute-start.19 = (bf16[272,128]{1,0:T(8,128)(2,1)S(1)}, bf16[272,128]{1,0:T(8,128)(2,1)S(1)}, u32[]{:S(2)}, u32[]{:S(2)}) collective-permute-start(bf16[272,128]{1,0:T(8,128)(2,1)S(1)} %relay.3), channel_id=1, source_target_pairs={{0,8},{8,0},{16,24},{24,16},{1,9},{9,1},{17,25},{25,17},{2,10},{10... | collective-permute-start | bytes 208904 | tf_op jit(solution)/shard_map/ppermute | solution.py:31
  47.0 5.3 %collective-permute-start.17 = (bf16[272,128]{1,0:T(8,128)(2,1)S(1)}, bf16[272,128]{1,0:T(8,128)(2,1)S(1)}, u32[]{:S(2)}, u32[]{:S(2)}) collective-permute-start(bf16[272,128]{1,0:T(8,128)(2,1)S(1)} %get-tuple-element.64), channel_id=1, source_target_pairs={{0,16},{8,24},{16,0},{24,8},{1,17},{9,25},{17,1},{25,9},{2,18},{10... | collective-permute-start | bytes 208904 | tf_op jit(solution)/shard_map/ppermute | solution.py:31

commit v6 on v5

--- a/solution.py
+++ b/solution.py
@@ -35,6 +35,15 @@
     deep, tall = lax.axis_size("enc"), lax.axis_size("kr")
     pairs_of = [(i, ((i // tall) ^ deep_mask) * tall + ((i % tall) ^ tall_mask)) for i in range(deep * tall)]
     return lax.ppermute(x, ("enc", "kr"), pairs_of)
+
+
+def swap_split(x, near, far):
+    deep, tall, line = lax.axis_size("enc"), lax.axis_size("kr"), lax.axis_size("kc")
+    pairs_of = []
+    for i in range(deep * tall * line):
+        masks = far if i % 2 else near
+        pairs_of.append((i, ((i // line // tall) ^ masks[0]) * tall * line + ((i // line % tall) ^ masks[1]) * line + i % line))
+    return lax.ppermute(x, ("enc", "kr", "kc"), pairs_of)
 
 
 def params(limit=VMEM_LIMIT):
@@ -136,6 +145,28 @@
     )(*blocks, *after)
 
 
+def route_body(choices, *refs):
+    outs = refs[-len(choices) :]
+    odd = lax.rem(lax.axis_index("kc"), 2)
+    for side in (0, 1):
+
+        @pl.when(odd == side)
+        def _():
+            for choice, out_ref in zip(choices, outs):
+                out_ref[...] = refs[choice[side]][...]
+
+
+def route(blocks, choices, after):
+    return pl.pallas_call(
+        lambda *refs: route_body(choices, *refs),
+        in_specs=[VMEM] * len(blocks) + [ANY] * len(after),
+        out_specs=(VMEM,) * len(choices),
+        out_shape=(jax.ShapeDtypeStruct(blocks[0].shape, BF16),) * len(choices),
+        compiler_params=params(),
+        name="gate",
+    )(*blocks, *after)
+
+
 def rows_body(own_rows, count, *refs):
     row_refs, (rowa_ref, rsp_ref) = refs[:count], refs[-2:]
     blocks = [block for ref in row_refs for block in block_parts(ref, own_rows)]
@@ -178,13 +209,12 @@
     feat = probe // 2
     rows = rowa_ref.shape[0]
     blocks = [block for ref, n in zip(col_refs, counts) for block in block_parts(ref, own_rows)[:n]]
-    group = 2
+    p_all, s_all, u_all = (jnp.concatenate([block[i] for block in blocks], axis=0) for i in range(3))
+    cols = len(blocks) * own_rows
+    tile = 256 if cols % 256 == 0 else 2 * own_rows
     v, m, sums = (None, None, None) if first else (v_in[...], m_in[...], s_in[...])
-    for b in range(0, len(blocks), group):
-        pieces = blocks[b : b + group]
-        p = jnp.concatenate([q[0] for q in pieces], axis=0)
-        s = jnp.concatenate([q[1] for q in pieces], axis=0)
-        u = jnp.concatenate([q[2] for q in pieces], axis=0)
+    for b in range(0, cols, tile):
+        p, s, u = p_all[b : b + tile], s_all[b : b + tile], u_all[b : b + tile]
         u32 = u.astype(F32)
         sq = u32 * u32
         hi = sq.astype(BF16)
@@ -446,14 +476,14 @@
     tall_masks = range(1, tall)
     if order:
         z_one, z_two, y_own = swap(own, "enc", 1), swap(own, "enc", 2), swap(own, "kr", 1)
-        (z_both,) = gate(([z_one, z_two],), (y_own, far_row, group_a[1]))
-        (row_both,) = gate(([own, far_row],), (z_both,))
+        a, b, c, d = route([z_one, z_two, y_own], [(0, 1), (1, 2), (1, 0), (2, 1)], (far_row, group_a[1]))
+        (row_both,) = gate(([own, far_row],), (a,))
         core_both = swap(row_both, "kc", 1)
+        over = (0, 1)
         calls = [
-            ([row_both, y_own], [1, 1]),
-            ([z_one, z_two], [1, 1]),
-            ([swap(z_both, "kr", 1)], [2]),
-            ([swap(z_two, "enc", 1), swap(y_own, "enc", 3)], [1, 1]),
+            ([row_both, y_own, z_one, z_two], [1, 1, 1, 1]),
+            ([swap_split(a, over, (1, 0)), swap_split(b, over, (3, 0))], [1, 1]),
+            ([swap_split(c, (1, 0), over), swap_split(d, (3, 0), over)], [1, 1]),
         ]
     else:
         columns = [own]

time: 53.1 us -> 52.9 us (level)
  starting transfers between devices: 24.1 us -> 25.7 us
  waiting for transfers between devices: 9.63 us -> 8.09 us
    ppermute x0 -> x4, starting transfers between devices: none -> 4.48 us  [swap_split(): return lax.ppermute(x, ('enc', 'kr', 'kc'), pairs_of)]
    ppermute x21 -> x18, starting transfers between devices: 24.1 us -> 21.3 us  [swap(): return lax.ppermute(x, axis, [(i, i ^ mask) for i in range(size)])]
    ppermute x21 -> x18, waiting for transfers between devices: 9.63 us -> 7.4 us  [swap(): return lax.ppermute(x, axis, [(i, i ^ mask) for i in range(size)])]
    ppermute x0 -> x4, waiting for transfers between devices: none -> 0.69 us  [swap_split(): return lax.ppermute(x, ('enc', 'kr', 'kc'), pairs_of)]
    pallas_call x4 -> x3, Pallas kernels: 5.47 us -> 4.92 us  [pairs(): pl.pallas_call(lambda *refs: pair_body(own_rows, counts, first, last, *re...]
  transfers between devices with their start and end apart: 21 -> 22, of which waited for: 9 -> 9; matrix products, arithmetic and copies ran while one was open for 1% -> 1% of each run, Pallas kernels for 30% -> 29%
where the time goes in v6:
time: 52.9 us; the launch traced here: 52.7 us
  starting transfers between devices  25.7 us (49%)
  Pallas kernels  16.4 us (31%)
  waiting for transfers between devices  8.09 us (15%)
  local copies, waits for them, and re-layouts  0.95 us (2%)
  between operations  0.85 us (2%)
  other arithmetic  0.67 us (1%)
    ppermute x18, starting transfers between devices, swap(): return lax.ppermute(x, axis, [(i, i ^ mask) for i in range(size)])  21.3 us
    ppermute x18, waiting for transfers between devices, swap(): return lax.ppermute(x, axis, [(i, i ^ mask) for i in range(size)])  7.4 us
    pallas_call x3, Pallas kernels, pairs(): pl.pallas_call(lambda *refs: pair_body(own_rows, counts, first, last, *re...  4.92 us
    pallas_call x2, Pallas kernels, prepare(): pl.pallas_call(lambda *refs: prepare_body(share, order, *refs), in_specs=...  4.76 us
    ppermute x4, starting transfers between devices, swap_split(): return lax.ppermute(x, ('enc', 'kr', 'kc'), pairs_of)  4.48 us
    pallas_call x1, Pallas kernels, encode(): pl.pallas_call(encode_body, in_specs=[HBM] * 6, out_specs=VMEM, out_shape...  3.52 us
    pallas_call x1, Pallas kernels, grads(): pl.pallas_call(lambda *refs: grads_body(pieces, share, scale, *refs), in_...  1.56 us
  transfers between devices with their start and end apart: 22, of which 9 were waited for; matrix products, arithmetic and copies ran while one was open for 1% of the time, Pallas kernels for 29%

profile of v6, /device:TPU:0, one launch (start us, length us, event | category | flops | bytes accessed | tf_op | source)
XLA Modules:
  0.0 52.7 jit_solution(1690092126761635840)
XLA Ops:
  0.6 0.0 copy-start.1
  0.6 0.0 copy-start
  0.7 0.5 collective-permute-start.4
  1.2 3.5 %encode.1.refs_3_.refs_0_ = bf16[480,128]{1,0:T(8,128)(2,1)} custom-call(bf16[192,1024]{1,0:T(8,128)(2,1)} %refs_0_.1, bf16[1024,1024]{1,0:T(8,128)(2,1)} %refs_2_.3, bf16[64,1024]{1,0:T(8,128)(2,1)} %bitcast.2, f32[1,64]{1,0:T(1,128)} %bitcast.4, bf16[192,128]{1,0:T(8,128)(2,1)} %probe_hbm.1, bf16[192,128]{1,0:T(8,128)(2,1)} %solve_hbm.1), custom_call_target="tpu_custom_call" | custom-call | tf_op jit(solution)/shard_map/encode/pallas_call | solution.py:95
  4.7 2.5 %collective-permute-start = (bf16[480,128]{1,0:T(8,128)(2,1)}, bf16[480,128]{1,0:T(8,128)(2,1)S(1)}, u32[]{:S(2)}, u32[]{:S(2)}) collective-permute-start(bf16[480,128]{1,0:T(8,128)(2,1)} %encode.1.refs_3_.refs_0_), channel_id=1, source_target_pairs={{0,2},{1,3},{2,0},{3,1},{4,6},{5,7},{6,4},{7,5},{8,10},{9,11},{10,... | collective-permute-start | bytes 368648 | tf_op jit(solution)/shard_map/ppermute | solution.py:31
  7.2 1.6 %collective-permute-start.1 = (bf16[480,128]{1,0:T(8,128)(2,1)}, bf16[480,128]{1,0:T(8,128)(2,1)S(1)}, u32[]{:S(2)}, u32[]{:S(2)}) collective-permute-start(bf16[480,128]{1,0:T(8,128)(2,1)} %encode.1.refs_3_.refs_0_), channel_id=1, source_target_pairs={{0,8},{8,0},{16,24},{24,16},{1,9},{9,1},{17,25},{25,17},{2,10},{10... | collective-permute-start | bytes 368648 | tf_op jit(solution)/shard_map/ppermute | solution.py:31
  8.8 2.6 %collective-permute-start.2 = (bf16[480,128]{1,0:T(8,128)(2,1)}, bf16[480,128]{1,0:T(8,128)(2,1)S(1)}, u32[]{:S(2)}, u32[]{:S(2)}) collective-permute-start(bf16[480,128]{1,0:T(8,128)(2,1)} %encode.1.refs_3_.refs_0_), channel_id=1, source_target_pairs={{0,16},{8,24},{16,0},{24,8},{1,17},{9,25},{17,1},{25,9},{2,18},{10... | collective-permute-start | bytes 368648 | tf_op jit(solution)/shard_map/ppermute | solution.py:31
  11.4 1.5 %collective-permute-start.3 = (bf16[480,128]{1,0:T(8,128)(2,1)}, bf16[480,128]{1,0:T(8,128)(2,1)S(1)}, u32[]{:S(2)}, u32[]{:S(2)}) collective-permute-start(bf16[480,128]{1,0:T(8,128)(2,1)} %encode.1.refs_3_.refs_0_), channel_id=1, source_target_pairs={{0,4},{4,0},{1,5},{5,1},{2,6},{6,2},{3,7},{7,3},{8,12},{12,8},{9,1... | collective-permute-start | bytes 368648 | tf_op jit(solution)/shard_map/ppermute | solution.py:31
  12.9 0.0 collective-permute-done.4.refs_1_
  12.9 0.0 copy-done.1
  12.9 0.0 copy-done
  12.9 0.0 copy-start.2
  12.9 0.9 %copy-done.2 = bf16[480,128]{1,0:T(8,128)(2,1)S(1)} copy-done((bf16[480,128]{1,0:T(8,128)(2,1)S(1)}, bf16[480,128]{1,0:T(8,128)(2,1)}, u32[]{:S(2)}) %copy-start.2) | copy-done | bytes 122904
  13.8 2.4 %prepare.2 = (f32[384,1024]{1,0:T(8,128)S(1)}, bf16[256,384]{1,0:T(8,128)(2,1)S(1)}, bf16[256,384]{1,0:T(8,128)(2,1)S(1)}) custom-call(bf16[192,1024]{1,0:T(8,128)(2,1)S(1)} %copy-done.1, bf16[192,1024]{1,0:T(8,128)(2,1)S(1)} %collective-permute-done.4.refs_1_, bf16[1024,1024]{1,0:T(8,128)(2,1)S(1)} %copy-done, bf16[480,128]{1,0:T(8,128)(2,1)S(1)} %copy-done.2), custom_call_target="tpu_custom_call" | custom-call | flops 1 | bytes 1048576 | tf_op jit(solution)/shard_map/prepare/pallas_call | solution.py:308
  16.2 0.0 collective-permute-done.refs_3_.refs_1_
  16.2 0.0 collective-permute-done.1.refs_0_.refs_4_
  16.2 1.4 %collective-permute-done.2.refs_1_.refs_5_ = bf16[480,128]{1,0:T(8,128)(2,1)S(1)} collective-permute-done((bf16[480,128]{1,0:T(8,128)(2,1)}, bf16[480,128]{1,0:T(8,128)(2,1)S(1)}, u32[]{:S(2)}, u32[]{:S(2)}) %collective-permute-start.2) | collective-permute-done | bytes 122912 | tf_op jit(solution)/shard_map/ppermute | solution.py:31
  17.6 0.0 collective-permute-done.3.refs_2_.refs_3_
  17.6 0.2 gate.2
  17.9 0.1 collective-permute-start.5
  18.0 0.6 %collective-permute-start.11 = (bf16[192,1024]{1,0:T(8,128)(2,1)S(1)}, bf16[192,1024]{1,0:T(8,128)(2,1)S(1)}, u32[]{:S(2)}, u32[]{:S(2)}) collective-permute-start(bf16[192,1024]{1,0:T(8,128)(2,1)S(1)} %copy-done.1), channel_id=1, source_target_pairs={{0,2},{1,3},{2,0},{3,1},{4,6},{5,7},{6,4},{7,5},{8,10},{9,11},{10,... | collective-permute-start | bytes 1179656 | tf_op jit(solution)/shard_map/ppermute | solution.py:31
  18.6 1.5 %collective-permute-start.8 = (bf16[480,128]{1,0:T(8,128)(2,1)S(1)}, bf16[480,128]{1,0:T(8,128)(2,1)S(1)}, u32[]{:S(2)}, u32[]{:S(2)}) collective-permute-start(bf16[480,128]{1,0:T(8,128)(2,1)S(1)} %get-tuple-element.39.refs_2_), channel_id=1, source_target_pairs={{0,4},{1,9},{2,6},{3,11},{4,0},{5,13},{6,2},{7,15},{8,12},{9,1},{1... | collective-permute-start | bytes 368648 | tf_op jit(solution)/shard_map/ppermute | solution.py:46
  20.1 0.5 collective-permute-start.9
  20.6 0.4 collective-permute-start.6
  21.0 0.0 collective-permute-done.5.refs_1_
  21.0 2.0 %collective-permute-start.7 = (bf16[480,128]{1,0:T(8,128)(2,1)S(1)}, bf16[480,128]{1,0:T(8,128)(2,1)S(1)}, u32[]{:S(2)}, u32[]{:S(2)}) collective-permute-start(bf16[480,128]{1,0:T(8,128)(2,1)S(1)} %get-tuple-element.43), channel_id=1, source_target_pairs={{0,24},{1,5},{2,26},{3,7},{4,28},{5,1},{6,30},{7,3},{8,16},{9,13},... | collective-permute-start | bytes 368648 | tf_op jit(solution)/shard_map/ppermute | solution.py:46
  23.1 0.5 %rows.1 = (bf16[768,256]{1,0:T(8,128)(2,1)S(1)}, bf16[768,256]{1,0:T(8,128)(2,1)S(1)}) custom-call(bf16[960,128]{1,0:T(8,128)(2,1)S(1)} %gate.3.refs_0_.refs_2_, bf16[960,128]{1,0:T(8,128)(2,1)S(1)} %collective-permute-done.5.refs_1_), custom_call_target="tpu_custom_call" | custom-call | tf_op jit(solution)/shard_map/rows/pallas_call | solution.py:190
  23.6 2.1 %pairs.3 = (f32[768,128]{1,0:T(8,128)S(1)}, f32[768,64]{1,0:T(8,128)S(1)}, f32[768,128]{1,0:T(8,128)S(1)}) custom-call(bf16[768,256]{1,0:T(8,128)(2,1)S(1)} %get-tuple-element.40.refs_0_, bf16[768,256]{1,0:T(8,128)(2,1)S(1)} %get-tuple-element.41.refs_1_, bf16[960,128]{1,0:T(8,128)(2,1)S(1)} %gate.3.refs_0_.refs_2_, ...), custom_call_target="tpu_custom_call" | custom-call | flops 1 | bytes 1179648 | tf_op jit(solution)/shard_map/pairs/pallas_call | solution.py:259
  25.7 0.0 collective-permute-done.8.refs_2_
  25.7 0.5 %collective-permute-done.9.refs_3_ = bf16[480,128]{1,0:T(8,128)(2,1)S(1)} collective-permute-done((bf16[480,128]{1,0:T(8,128)(2,1)S(1)}, bf16[480,128]{1,0:T(8,128)(2,1)S(1)}, u32[]{:S(2)}, u32[]{:S(2)}) %collective-permute-start.9) | collective-permute-done | bytes 122912 | tf_op jit(solution)/shard_map/ppermute | solution.py:46
  26.3 1.4 %pairs.4 = (f32[768,128]{1,0:T(8,128)S(1)}, f32[768,64]{1,0:T(8,128)S(1)}, f32[768,128]{1,0:T(8,128)S(1)}) custom-call(bf16[768,256]{1,0:T(8,128)(2,1)S(1)} %get-tuple-element.40.refs_0_, bf16[768,256]{1,0:T(8,128)(2,1)S(1)} %get-tuple-element.41.refs_1_, bf16[480,128]{1,0:T(8,128)(2,1)S(1)} %collective-permute-done.8.refs_2_, ...), custom_call_target="tpu_custom_call" | custom-call | flops 1 | bytes 884736 | tf_op jit(solution)/shard_map/pairs/pallas_call | solution.py:259
  27.6 0.0 collective-permute-done.6.refs_2_
  27.7 0.2 collective-permute-done.7.refs_3_
  27.8 1.4 %pairs.5 = (f32[384,128]{1,0:T(8,128)S(1)}, f32[384,128]{1,0:T(8,128)S(1)}, f32[384,128]{1,0:T(8,128)S(1)}) custom-call(bf16[768,256]{1,0:T(8,128)(2,1)S(1)} %get-tuple-element.40.refs_0_, bf16[768,256]{1,0:T(8,128)(2,1)S(1)} %get-tuple-element.41.refs_1_, bf16[480,128]{1,0:T(8,128)(2,1)S(1)} %collective-permute-done.6.refs_2_, ...), custom_call_target="tpu_custom_call" | custom-call | flops 1 | bytes 884736 | tf_op jit(solution)/shard_map/pairs/pallas_call | solution.py:259
  29.2 0.1 collective-permute-start.10
  29.3 0.2 collective-permute-done.11.x_ref.refs_0_
  29.5 1.3 %collective-permute-done.10.got_ref = f32[384,128]{1,0:T(8,128)S(1)} collective-permute-done((f32[384,128]{1,0:T(8,128)S(1)}, f32[384,128]{1,0:T(8,128)S(1)}, u32[]{:S(2)}, u32[]{:S(2)}) %collective-permute-start.10) | collective-permute-done | bytes 196640 | tf_op jit(solution)/shard_map/ppermute | solution.py:31
  30.7 0.1 merge.1
  30.8 0.2 collective-permute-start.14
  31.1 0.0 copy-start.4
  31.1 0.0 copy-start.5
  31.1 0.4 collective-permute-start.12
  31.5 1.5 %collective-permute-start.13 = (bf16[384,128]{1,0:T(8,128)(2,1)S(1)}, bf16[384,128]{1,0:T(8,128)(2,1)S(1)}, u32[]{:S(2)}, u32[]{:S(2)}) collective-permute-start(bf16[384,128]{1,0:T(8,128)(2,1)S(1)} %get-tuple-element.55), channel_id=1, source_target_pairs={{0,2},{1,3},{2,0},{3,1},{4,6},{5,7},{6,4},{7,5},{8,10},{9,11},{10,... | collective-permute-start | bytes 294920 | tf_op jit(solution)/shard_map/ppermute | solution.py:31
  33.0 0.0 collective-permute-done.14.refs_1_
  33.0 2.4 %prepare.3 = (f32[384,1024]{1,0:T(8,128)S(1)}, bf16[256,384]{1,0:T(8,128)(2,1)S(1)}, bf16[256,384]{1,0:T(8,128)(2,1)S(1)}) custom-call(bf16[192,1024]{1,0:T(8,128)(2,1)S(1)} %collective-permute-done.11.x_ref.refs_0_, bf16[192,1024]{1,0:T(8,128)(2,1)S(1)} %collective-permute-done.14.refs_1_, bf16[1024,1024]{1,0:T(8,128)(2,1)S(1)} %copy-done, ...), custom_call_target="tpu_custom_call" | custom-call | flops 1 | bytes 1048576 | tf_op jit(solution)/shard_map/prepare/pallas_call | solution.py:308
  35.4 1.0 %collective-permute-done.13.refs_1_ = bf16[384,128]{1,0:T(8,128)(2,1)S(1)} collective-permute-done((bf16[384,128]{1,0:T(8,128)(2,1)S(1)}, bf16[384,128]{1,0:T(8,128)(2,1)S(1)}, u32[]{:S(2)}, u32[]{:S(2)}) %collective-permute-start.13) | collective-permute-done | bytes 98336 | tf_op jit(solution)/shard_map/ppermute | solution.py:31
  36.4 1.6 %grads.1 = (bf16[544,128]{1,0:T(8,128)(2,1)S(1)}, bf16[272,128]{1,0:T(8,128)(2,1)S(1)}, bf16[272,128]{1,0:T(8,128)(2,1)S(1)}, bf16[272,128]{1,0:T(8,128)(2,1)S(1...) custom-call(f32[384,128]{1,0:T(8,128)S(1)} %get-tuple-element.54.refs_0_.refs_3_, ...), custom_call_target="tpu_custom_call" | custom-call | tf_op jit(solution)/shard_map/grads/pallas_call | solution.py:386
  37.9 1.6 %collective-permute-start.16 = (bf16[544,128]{1,0:T(8,128)(2,1)S(1)}, bf16[544,128]{1,0:T(8,128)(2,1)S(1)}, u32[]{:S(2)}, u32[]{:S(2)}) collective-permute-start(bf16[544,128]{1,0:T(8,128)(2,1)S(1)} %get-tuple-element.62.refs_0_), channel_id=1, source_target_pairs={{0,4},{4,0},{1,5},{5,1},{2,6},{6,2},{3,7},{7,3},{8,12},{12,8},{9,1... | collective-permute-start | bytes 417800 | tf_op jit(solution)/shard_map/ppermute | solution.py:31
  39.5 0.0 collective-permute-done.12
  39.6 1.6 %collective-permute-start.15 = (f32[192,128]{1,0:T(8,128)S(1)}, f32[192,128]{1,0:T(8,128)S(1)}, u32[]{:S(2)}, u32[]{:S(2)}) collective-permute-start(f32[192,128]{1,0:T(8,128)S(1)} %hold.3), channel_id=1, source_target_pairs={{0,2},{1,3},{2,0},{3,1},{4,6},{5,7},{6,4},{7,5},{8,10},{9,11},{10,... | collective-permute-start | bytes 294920 | tf_op jit(solution)/shard_map/ppermute | solution.py:31
  41.1 0.5 collective-permute-start.19
  41.6 1.5 %collective-permute-start.21 = (bf16[272,128]{1,0:T(8,128)(2,1)S(1)}, bf16[272,128]{1,0:T(8,128)(2,1)S(1)}, u32[]{:S(2)}, u32[]{:S(2)}) collective-permute-start(bf16[272,128]{1,0:T(8,128)(2,1)S(1)} %get-tuple-element.70), channel_id=1, source_target_pairs={{0,4},{4,0},{1,5},{5,1},{2,6},{6,2},{3,7},{7,3},{8,12},{12,8},{9,1... | collective-permute-start | bytes 208904 | tf_op jit(solution)/shard_map/ppermute | solution.py:31
  43.2 0.5 collective-permute-done.16.refs_0_
  43.7 3.1 %collective-permute-start.17 = (bf16[272,128]{1,0:T(8,128)(2,1)S(1)}, bf16[272,128]{1,0:T(8,128)(2,1)S(1)}, u32[]{:S(2)}, u32[]{:S(2)}) collective-permute-start(bf16[272,128]{1,0:T(8,128)(2,1)S(1)} %get-tuple-element.65.refs_2_), channel_id=1, source_target_pairs={{0,24},{8,16},{16,8},{24,0},{1,25},{9,17},{17,9},{25,1},{2,26},{10... | collective-permute-start | bytes 208904 | tf_op jit(solution)/shard_map/ppermute | solution.py:31
  46.8 0.0 collective-permute-start.18
  46.8 0.0 collective-permute-done.19.refs_0_
  46.8 0.0 collective-permute-done.15.refs_3_
  46.8 1.4 %collective-permute-start.20 = (bf16[272,128]{1,0:T(8,128)(2,1)S(1)}, bf16[272,128]{1,0:T(8,128)(2,1)S(1)}, u32[]{:S(2)}, u32[]{:S(2)}) collective-permute-start(bf16[272,128]{1,0:T(8,128)(2,1)S(1)} %relay.3), channel_id=1, source_target_pairs={{0,8},{8,0},{16,24},{24,16},{1,9},{9,1},{17,25},{25,17},{2,10},{10... | collective-permute-start | bytes 208904 | tf_op jit(solution)/shard_map/ppermute | solution.py:31
  48.2 0.6 %fusion.1 = bf16[192,128]{1,0:T(8,128)(2,1)} fusion(f32[192,128]{1,0:T(8,128)S(1)} %collective-permute-done.15.refs_3_, f32[384,128]{1,0:T(8,128)S(1)} %add.6), kind=kLoop, calls=%fused_computation.2 | loop fusion | flops 73728 | bytes 245760 | tf_op jit(solution)/shard_map/convert_element_type | solution.py:522
  48.9 0.0 collective-permute-done.21.refs_4_
  48.9 1.7 %collective-permute-done.17.refs_0_ = bf16[272,128]{1,0:T(8,128)(2,1)S(1)} collective-permute-done((bf16[272,128]{1,0:T(8,128)(2,1)S(1)}, bf16[272,128]{1,0:T(8,128)(2,1)S(1)}, u32[]{:S(2)}, u32[]{:S(2)}) %collective-permute-start.17) | collective-permute-done | bytes 69664 | tf_op jit(solution)/shard_map/ppermute | solution.py:31
  50.5 1.5 %collective-permute-done.18.refs_1_ = bf16[272,128]{1,0:T(8,128)(2,1)S(1)} collective-permute-done((bf16[272,128]{1,0:T(8,128)(2,1)S(1)}, bf16[272,128]{1,0:T(8,128)(2,1)S(1)}, u32[]{:S(2)}, u32[]{:S(2)}) %collective-permute-start.18) | collective-permute-done | bytes 69664 | tf_op jit(solution)/shard_map/ppermute | solution.py:31
  52.0 0.0 collective-permute-done.20.refs_3_
  52.0 0.7 %total.1 = (f32[32,1024]{1,0:T(8,128)}, f32[32,64]{1,0:T(8,128)}) custom-call(bf16[272,128]{1,0:T(8,128)(2,1)S(1)} %collective-permute-done.17.refs_0_, bf16[272,128]{1,0:T(8,128)(2,1)S(1)} %collective-permute-done.18.refs_1_, bf16[272,128]{1,0:T(8,128)(2,1)S(1)} %get-tuple-element.67.refs_2_, bf16[272,128]{1,0:T(8,128)(2,1)S(1)} %collective-permute-done.20.refs_3_, ...), custom_call_target="tpu_custom_call" | custom-call | tf_op jit(solution)/shard_map/total/pallas_call | solution.py:436
  (11 shorter events, 0.1 us)
Async XLA Ops:
  0.6 12.3 %copy-start.1 = (bf16[192,1024]{1,0:T(8,128)(2,1)S(1)}, bf16[192,1024]{1,0:T(8,128)(2,1)}, u32[]{:S(2)}) copy-start(bf16[192,1024]{1,0:T(8,128)(2,1)} %refs_0_.1) | copy-start | bytes 1179652
  0.6 12.3 %copy-start = (bf16[1024,1024]{1,0:T(8,128)(2,1)S(1)}, bf16[1024,1024]{1,0:T(8,128)(2,1)}, u32[]{:S(2)}) copy-start(bf16[1024,1024]{1,0:T(8,128)(2,1)} %refs_2_.3) | copy-start | bytes 6291460
  0.7 12.2 %collective-permute-start.4 = (bf16[192,1024]{1,0:T(8,128)(2,1)}, bf16[192,1024]{1,0:T(8,128)(2,1)S(1)}, u32[]{:S(2)}, u32[]{:S(2)}) collective-permute-start(bf16[192,1024]{1,0:T(8,128)(2,1)} %refs_0_.1), channel_id=1, source_target_pairs={{0,1},{1,0},{2,3},{3,2},{4,5},{5,4},{6,7},{7,6},{8,9},{9,8},{10,11... | collective-permute-start | bytes 1179656 | tf_op jit(solution)/shard_map/ppermute | solution.py:31
  4.7 11.5 %collective-permute-start = (bf16[480,128]{1,0:T(8,128)(2,1)}, bf16[480,128]{1,0:T(8,128)(2,1)S(1)}, u32[]{:S(2)}, u32[]{:S(2)}) collective-permute-start(bf16[480,128]{1,0:T(8,128)(2,1)} %encode.1.refs_3_.refs_0_), channel_id=1, source_target_pairs={{0,2},{1,3},{2,0},{3,1},{4,6},{5,7},{6,4},{7,5},{8,10},{9,11},{10,... | collective-permute-start | bytes 368648 | tf_op jit(solution)/shard_map/ppermute | solution.py:31
  7.2 9.0 %collective-permute-start.1 = (bf16[480,128]{1,0:T(8,128)(2,1)}, bf16[480,128]{1,0:T(8,128)(2,1)S(1)}, u32[]{:S(2)}, u32[]{:S(2)}) collective-permute-start(bf16[480,128]{1,0:T(8,128)(2,1)} %encode.1.refs_3_.refs_0_), channel_id=1, source_target_pairs={{0,8},{8,0},{16,24},{24,16},{1,9},{9,1},{17,25},{25,17},{2,10},{10... | collective-permute-start | bytes 368648 | tf_op jit(solution)/shard_map/ppermute | solution.py:31
  8.8 8.8 %collective-permute-start.2 = (bf16[480,128]{1,0:T(8,128)(2,1)}, bf16[480,128]{1,0:T(8,128)(2,1)S(1)}, u32[]{:S(2)}, u32[]{:S(2)}) collective-permute-start(bf16[480,128]{1,0:T(8,128)(2,1)} %encode.1.refs_3_.refs_0_), channel_id=1, source_target_pairs={{0,16},{8,24},{16,0},{24,8},{1,17},{9,25},{17,1},{25,9},{2,18},{10... | collective-permute-start | bytes 368648 | tf_op jit(solution)/shard_map/ppermute | solution.py:31
  11.4 6.2 %collective-permute-start.3 = (bf16[480,128]{1,0:T(8,128)(2,1)}, bf16[480,128]{1,0:T(8,128)(2,1)S(1)}, u32[]{:S(2)}, u32[]{:S(2)}) collective-permute-start(bf16[480,128]{1,0:T(8,128)(2,1)} %encode.1.refs_3_.refs_0_), channel_id=1, source_target_pairs={{0,4},{4,0},{1,5},{5,1},{2,6},{6,2},{3,7},{7,3},{8,12},{12,8},{9,1... | collective-permute-start | bytes 368648 | tf_op jit(solution)/shard_map/ppermute | solution.py:31
  12.9 0.9 %copy-start.2 = (bf16[480,128]{1,0:T(8,128)(2,1)S(1)}, bf16[480,128]{1,0:T(8,128)(2,1)}, u32[]{:S(2)}) copy-start(bf16[480,128]{1,0:T(8,128)(2,1)} %encode.1.refs_3_.refs_0_) | copy-start | bytes 368644
  13.8 4.0 %copy-start.3 = (bf16[480,128]{1,0:T(8,128)(2,1)S(1)}, bf16[480,128]{1,0:T(8,128)(2,1)}, u32[]{:S(2)}) copy-start(bf16[480,128]{1,0:T(8,128)(2,1)} %encode.1.refs_3_.refs_0_) | copy-start | bytes 368644
  17.9 3.1 %collective-permute-start.5 = (bf16[960,128]{1,0:T(8,128)(2,1)S(1)}, bf16[960,128]{1,0:T(8,128)(2,1)S(1)}, u32[]{:S(2)}, u32[]{:S(2)}) collective-permute-start(bf16[960,128]{1,0:T(8,128)(2,1)S(1)} %gate.3.refs_0_.refs_2_), channel_id=1, source_target_pairs={{0,1},{1,0},{2,3},{3,2},{4,5},{5,4},{6,7},{7,6},{8,9},{9,8},{10,11... | collective-permute-start | bytes 737288 | tf_op jit(solution)/shard_map/ppermute | solution.py:31
  18.0 11.5 %collective-permute-start.11 = (bf16[192,1024]{1,0:T(8,128)(2,1)S(1)}, bf16[192,1024]{1,0:T(8,128)(2,1)S(1)}, u32[]{:S(2)}, u32[]{:S(2)}) collective-permute-start(bf16[192,1024]{1,0:T(8,128)(2,1)S(1)} %copy-done.1), channel_id=1, source_target_pairs={{0,2},{1,3},{2,0},{3,1},{4,6},{5,7},{6,4},{7,5},{8,10},{9,11},{10,... | collective-permute-start | bytes 1179656 | tf_op jit(solution)/shard_map/ppermute | solution.py:31
  18.6 7.2 %collective-permute-start.8 = (bf16[480,128]{1,0:T(8,128)(2,1)S(1)}, bf16[480,128]{1,0:T(8,128)(2,1)S(1)}, u32[]{:S(2)}, u32[]{:S(2)}) collective-permute-start(bf16[480,128]{1,0:T(8,128)(2,1)S(1)} %get-tuple-element.39.refs_2_), channel_id=1, source_target_pairs={{0,4},{1,9},{2,6},{3,11},{4,0},{5,13},{6,2},{7,15},{8,12},{9,1},{1... | collective-permute-start | bytes 368648 | tf_op jit(solution)/shard_map/ppermute | solution.py:46
  20.1 6.2 %collective-permute-start.9 = (bf16[480,128]{1,0:T(8,128)(2,1)S(1)}, bf16[480,128]{1,0:T(8,128)(2,1)S(1)}, u32[]{:S(2)}, u32[]{:S(2)}) collective-permute-start(bf16[480,128]{1,0:T(8,128)(2,1)S(1)} %get-tuple-element.44), channel_id=1, source_target_pairs={{0,4},{1,25},{2,6},{3,27},{4,0},{5,29},{6,2},{7,31},{8,12},{9,17},... | collective-permute-start | bytes 368648 | tf_op jit(solution)/shard_map/ppermute | solution.py:46
  20.6 7.1 %collective-permute-start.6 = (bf16[480,128]{1,0:T(8,128)(2,1)S(1)}, bf16[480,128]{1,0:T(8,128)(2,1)S(1)}, u32[]{:S(2)}, u32[]{:S(2)}) collective-permute-start(bf16[480,128]{1,0:T(8,128)(2,1)S(1)} %get-tuple-element.42), channel_id=1, source_target_pairs={{0,8},{1,5},{2,10},{3,7},{4,12},{5,1},{6,14},{7,3},{8,0},{9,13},{1... | collective-permute-start | bytes 368648 | tf_op jit(solution)/shard_map/ppermute | solution.py:46
  21.0 6.8 %collective-permute-start.7 = (bf16[480,128]{1,0:T(8,128)(2,1)S(1)}, bf16[480,128]{1,0:T(8,128)(2,1)S(1)}, u32[]{:S(2)}, u32[]{:S(2)}) collective-permute-start(bf16[480,128]{1,0:T(8,128)(2,1)S(1)} %get-tuple-element.43), channel_id=1, source_target_pairs={{0,24},{1,5},{2,26},{3,7},{4,28},{5,1},{6,30},{7,3},{8,16},{9,13},... | collective-permute-start | bytes 368648 | tf_op jit(solution)/shard_map/ppermute | solution.py:46
  29.2 1.5 %collective-permute-start.10 = (f32[384,128]{1,0:T(8,128)S(1)}, f32[384,128]{1,0:T(8,128)S(1)}, u32[]{:S(2)}, u32[]{:S(2)}) collective-permute-start(f32[384,128]{1,0:T(8,128)S(1)} %get-tuple-element.53.term_ref), channel_id=1, source_target_pairs={{0,1},{1,0},{2,3},{3,2},{4,5},{5,4},{6,7},{7,6},{8,9},{9,8},{10,11... | collective-permute-start | bytes 589832 | tf_op jit(solution)/shard_map/ppermute | solution.py:31
  30.8 2.2 %collective-permute-start.14 = (bf16[192,1024]{1,0:T(8,128)(2,1)S(1)}, bf16[192,1024]{1,0:T(8,128)(2,1)S(1)}, u32[]{:S(2)}, u32[]{:S(2)}) collective-permute-start(bf16[192,1024]{1,0:T(8,128)(2,1)S(1)} %get-tuple-element.58), channel_id=1, source_target_pairs={{0,1},{1,0},{2,3},{3,2},{4,5},{5,4},{6,7},{7,6},{8,9},{9,8},{10,11... | collective-permute-start | bytes 1179656 | tf_op jit(solution)/shard_map/ppermute | solution.py:31
  31.1 5.3 %copy-start.4 = (bf16[1024,64]{0,1:T(8,128)(2,1)S(1)}, bf16[1024,64]{0,1:T(8,128)(2,1)}, u32[]{:S(2)}) copy-start(bf16[1024,64]{0,1:T(8,128)(2,1)} %param.8) | copy-start | bytes 393220
  31.1 5.3 %copy-start.5 = (f32[64]{0:T(128)S(1)}, f32[64]{0:T(128)}, u32[]{:S(2)}) copy-start(f32[64]{0:T(128)} %param.9) | copy-start | bytes 772
  31.1 8.4 %collective-permute-start.12 = (f32[384,128]{1,0:T(8,128)S(1)}, f32[384,128]{1,0:T(8,128)S(1)}, u32[]{:S(2)}, u32[]{:S(2)}) collective-permute-start(f32[384,128]{1,0:T(8,128)S(1)} %hold.2), channel_id=1, source_target_pairs={{0,1},{1,0},{2,3},{3,2},{4,5},{5,4},{6,7},{7,6},{8,9},{9,8},{10,11... | collective-permute-start | bytes 589832 | tf_op jit(solution)/shard_map/ppermute | solution.py:31
  31.5 4.8 %collective-permute-start.13 = (bf16[384,128]{1,0:T(8,128)(2,1)S(1)}, bf16[384,128]{1,0:T(8,128)(2,1)S(1)}, u32[]{:S(2)}, u32[]{:S(2)}) collective-permute-start(bf16[384,128]{1,0:T(8,128)(2,1)S(1)} %get-tuple-element.55), channel_id=1, source_target_pairs={{0,2},{1,3},{2,0},{3,1},{4,6},{5,7},{6,4},{7,5},{8,10},{9,11},{10,... | collective-permute-start | bytes 294920 | tf_op jit(solution)/shard_map/ppermute | solution.py:31
  37.9 5.7 %collective-permute-start.16 = (bf16[544,128]{1,0:T(8,128)(2,1)S(1)}, bf16[544,128]{1,0:T(8,128)(2,1)S(1)}, u32[]{:S(2)}, u32[]{:S(2)}) collective-permute-start(bf16[544,128]{1,0:T(8,128)(2,1)S(1)} %get-tuple-element.62.refs_0_), channel_id=1, source_target_pairs={{0,4},{4,0},{1,5},{5,1},{2,6},{6,2},{3,7},{7,3},{8,12},{12,8},{9,1... | collective-permute-start | bytes 417800 | tf_op jit(solution)/shard_map/ppermute | solution.py:31
  39.6 7.2 %collective-permute-start.15 = (f32[192,128]{1,0:T(8,128)S(1)}, f32[192,128]{1,0:T(8,128)S(1)}, u32[]{:S(2)}, u32[]{:S(2)}) collective-permute-start(f32[192,128]{1,0:T(8,128)S(1)} %hold.3), channel_id=1, source_target_pairs={{0,2},{1,3},{2,0},{3,1},{4,6},{5,7},{6,4},{7,5},{8,10},{9,11},{10,... | collective-permute-start | bytes 294920 | tf_op jit(solution)/shard_map/ppermute | solution.py:31
  41.1 5.7 %collective-permute-start.19 = (bf16[272,128]{1,0:T(8,128)(2,1)S(1)}, bf16[272,128]{1,0:T(8,128)(2,1)S(1)}, u32[]{:S(2)}, u32[]{:S(2)}) collective-permute-start(bf16[272,128]{1,0:T(8,128)(2,1)S(1)} %get-tuple-element.68), channel_id=1, source_target_pairs={{0,4},{4,0},{1,5},{5,1},{2,6},{6,2},{3,7},{7,3},{8,12},{12,8},{9,1... | collective-permute-start | bytes 208904 | tf_op jit(solution)/shard_map/ppermute | solution.py:31
  41.6 7.2 %collective-permute-start.21 = (bf16[272,128]{1,0:T(8,128)(2,1)S(1)}, bf16[272,128]{1,0:T(8,128)(2,1)S(1)}, u32[]{:S(2)}, u32[]{:S(2)}) collective-permute-start(bf16[272,128]{1,0:T(8,128)(2,1)S(1)} %get-tuple-element.70), channel_id=1, source_target_pairs={{0,4},{4,0},{1,5},{5,1},{2,6},{6,2},{3,7},{7,3},{8,12},{12,8},{9,1... | collective-permute-start | bytes 208904 | tf_op jit(solution)/shard_map/ppermute | solution.py:31
  43.7 6.9 %collective-permute-start.17 = (bf16[272,128]{1,0:T(8,128)(2,1)S(1)}, bf16[272,128]{1,0:T(8,128)(2,1)S(1)}, u32[]{:S(2)}, u32[]{:S(2)}) collective-permute-start(bf16[272,128]{1,0:T(8,128)(2,1)S(1)} %get-tuple-element.65.refs_2_), channel_id=1, source_target_pairs={{0,24},{8,16},{16,8},{24,0},{1,25},{9,17},{17,9},{25,1},{2,26},{10... | collective-permute-start | bytes 208904 | tf_op jit(solution)/shard_map/ppermute | solution.py:31
  46.8 5.2 %collective-permute-start.18 = (bf16[272,128]{1,0:T(8,128)(2,1)S(1)}, bf16[272,128]{1,0:T(8,128)(2,1)S(1)}, u32[]{:S(2)}, u32[]{:S(2)}) collective-permute-start(bf16[272,128]{1,0:T(8,128)(2,1)S(1)} %get-tuple-element.66), channel_id=1, source_target_pairs={{0,16},{8,24},{16,0},{24,8},{1,17},{9,25},{17,1},{25,9},{2,18},{10... | collective-permute-start | bytes 208904 | tf_op jit(solution)/shard_map/ppermute | solution.py:31
  46.8 5.2 %collective-permute-start.20 = (bf16[272,128]{1,0:T(8,128)(2,1)S(1)}, bf16[272,128]{1,0:T(8,128)(2,1)S(1)}, u32[]{:S(2)}, u32[]{:S(2)}) collective-permute-start(bf16[272,128]{1,0:T(8,128)(2,1)S(1)} %relay.3), channel_id=1, source_target_pairs={{0,8},{8,0},{16,24},{24,16},{1,9},{9,1},{17,25},{25,17},{2,10},{10... | collective-permute-start | bytes 208904 | tf_op jit(solution)/shard_map/ppermute | solution.py:31

commit v7 on v6

--- a/solution.py
+++ b/solution.py
@@ -59,15 +59,25 @@
     w2_copy = pltpu.make_async_copy(w2t_hbm, w2t_ref, sems.at[1])
     probe_copy = pltpu.make_async_copy(probe_hbm, out_ref.at[pl.ds(0, rows), :], sems.at[2])
     solve_copy = pltpu.make_async_copy(solve_hbm, out_ref.at[pl.ds(rows, rows), :], sems.at[3])
+    deep = width // 2
     w1_copies = [
-        pltpu.make_async_copy(w1_hbm.at[:, pl.ds(j * block, block)], w1_ref.at[:, pl.ds(j * block, block)], sems.at[4 + j])
+        [
+            pltpu.make_async_copy(
+                w1_hbm.at[pl.ds(n * deep, deep), pl.ds(j * block, block)],
+                w1_ref.at[pl.ds(n * deep, deep), pl.ds(j * block, block)],
+                sems.at[4 + 2 * j + n],
+            )
+            for n in range(2)
+        ]
         for j in range(parts)
     ]
     x_copy.start()
-    w1_copies[0].start()
+    for copy in w1_copies[0]:
+        copy.start()
     w2_copy.start()
-    for copy in w1_copies[1:]:
-        copy.start()
+    for copies in w1_copies[1:]:
+        for copy in copies:
+            copy.start()
     inv_copy = pltpu.make_async_copy(inv_hbm, inv_ref, sems.at[8])
     inv_copy.start()
     probe_copy.start()
@@ -76,7 +86,8 @@
     acc = None
     for j in range(parts):
         at = slice(j * block, (j + 1) * block)
-        w1_copies[j].wait()
+        for copy in w1_copies[j]:
+            copy.wait()
         pre = dot_nn(x_ref[...], w1_ref[:, at])
         hidden = (pre * jax.nn.sigmoid(pre)).astype(BF16)
         if j == 0:
@@ -209,12 +220,13 @@
     feat = probe // 2
     rows = rowa_ref.shape[0]
     blocks = [block for ref, n in zip(col_refs, counts) for block in block_parts(ref, own_rows)[:n]]
-    p_all, s_all, u_all = (jnp.concatenate([block[i] for block in blocks], axis=0) for i in range(3))
-    cols = len(blocks) * own_rows
-    tile = 256 if cols % 256 == 0 else 2 * own_rows
+    group = 2
     v, m, sums = (None, None, None) if first else (v_in[...], m_in[...], s_in[...])
-    for b in range(0, cols, tile):
-        p, s, u = p_all[b : b + tile], s_all[b : b + tile], u_all[b : b + tile]
+    for b in range(0, len(blocks), group):
+        pieces = blocks[b : b + group]
+        p = jnp.concatenate([q[0] for q in pieces], axis=0)
+        s = jnp.concatenate([q[1] for q in pieces], axis=0)
+        u = jnp.concatenate([q[2] for q in pieces], axis=0)
         u32 = u.astype(F32)
         sq = u32 * u32
         hi = sq.astype(BF16)
@@ -481,7 +493,8 @@
         core_both = swap(row_both, "kc", 1)
         over = (0, 1)
         calls = [
-            ([row_both, y_own, z_one, z_two], [1, 1, 1, 1]),
+            ([row_both, y_own], [1, 1]),
+            ([z_one, z_two], [1, 1]),
             ([swap_split(a, over, (1, 0)), swap_split(b, over, (3, 0))], [1, 1]),
             ([swap_split(c, (1, 0), over), swap_split(d, (3, 0), over)], [1, 1]),
         ]

time: 52.9 us -> 52.9 us (level)
  Pallas kernels: 16.4 us -> 17 us
  waiting for transfers between devices: 8.09 us -> 7.49 us
    ppermute x4, waiting for transfers between devices: 0.69 us -> 0.1 us  [swap_split(): return lax.ppermute(x, ('enc', 'kr', 'kc'), pairs_of)]
    pallas_call x3 -> x4, Pallas kernels: 4.92 us -> 5.49 us  [pairs(): pl.pallas_call(lambda *refs: pair_body(own_rows, counts, first, last, *re...]
  transfers between devices with their start and end apart: 22 -> 22, of which waited for: 9 -> 8; matrix products, arithmetic and copies ran while one was open for 1% -> 1% of each run, Pallas kernels for 29% -> 30%
where the time goes in v7:
time: 52.9 us; the launch traced here: 52.7 us
  starting transfers between devices  25.8 us (49%)
  Pallas kernels  17 us (32%)
  waiting for transfers between devices  7.49 us (14%)
  local copies, waits for them, and re-layouts  0.95 us (2%)
  between operations  0.87 us (2%)
  other arithmetic  0.67 us (1%)
    ppermute x18, starting transfers between devices, swap(): return lax.ppermute(x, axis, [(i, i ^ mask) for i in range(size)])  21.3 us
    ppermute x18, waiting for transfers between devices, swap(): return lax.ppermute(x, axis, [(i, i ^ mask) for i in range(size)])  7.39 us
    pallas_call x4, Pallas kernels, pairs(): pl.pallas_call(lambda *refs: pair_body(own_rows, counts, first, last, *re...  5.49 us
    pallas_call x2, Pallas kernels, prepare(): pl.pallas_call(lambda *refs: prepare_body(share, order, *refs), in_specs=...  4.76 us
    ppermute x4, starting transfers between devices, swap_split(): return lax.ppermute(x, ('enc', 'kr', 'kc'), pairs_of)  4.49 us
    pallas_call x1, Pallas kernels, encode(): pl.pallas_call(encode_body, in_specs=[HBM] * 6, out_specs=VMEM, out_shape...  3.49 us
    pallas_call x1, Pallas kernels, grads(): pl.pallas_call(lambda *refs: grads_body(pieces, share, scale, *refs), in_...  1.56 us
  transfers between devices with their start and end apart: 22, of which 8 were waited for; matrix products, arithmetic and copies ran while one was open for 1% of the time, Pallas kernels for 30%

profile of v7, /device:TPU:0, one launch (start us, length us, event | category | flops | bytes accessed | tf_op | source)
XLA Modules:
  0.0 52.7 jit_solution(16084986895944388012)
XLA Ops:
  0.6 0.0 copy-start.1
  0.6 0.0 copy-start
  0.7 0.5 collective-permute-start.4
  1.2 3.5 %encode.1.refs_3_.refs_0_ = bf16[480,128]{1,0:T(8,128)(2,1)} custom-call(bf16[192,1024]{1,0:T(8,128)(2,1)} %refs_0_.1, bf16[1024,1024]{1,0:T(8,128)(2,1)} %refs_2_.3, bf16[64,1024]{1,0:T(8,128)(2,1)} %bitcast.2, f32[1,64]{1,0:T(1,128)} %bitcast.4, bf16[192,128]{1,0:T(8,128)(2,1)} %probe_hbm.1, bf16[192,128]{1,0:T(8,128)(2,1)} %solve_hbm.1), custom_call_target="tpu_custom_call" | custom-call | tf_op jit(solution)/shard_map/encode/pallas_call | solution.py:106
  4.7 2.5 %collective-permute-start = (bf16[480,128]{1,0:T(8,128)(2,1)}, bf16[480,128]{1,0:T(8,128)(2,1)S(1)}, u32[]{:S(2)}, u32[]{:S(2)}) collective-permute-start(bf16[480,128]{1,0:T(8,128)(2,1)} %encode.1.refs_3_.refs_0_), channel_id=1, source_target_pairs={{0,2},{1,3},{2,0},{3,1},{4,6},{5,7},{6,4},{7,5},{8,10},{9,11},{10,... | collective-permute-start | bytes 368648 | tf_op jit(solution)/shard_map/ppermute | solution.py:31
  7.2 1.6 %collective-permute-start.1 = (bf16[480,128]{1,0:T(8,128)(2,1)}, bf16[480,128]{1,0:T(8,128)(2,1)S(1)}, u32[]{:S(2)}, u32[]{:S(2)}) collective-permute-start(bf16[480,128]{1,0:T(8,128)(2,1)} %encode.1.refs_3_.refs_0_), channel_id=1, source_target_pairs={{0,8},{8,0},{16,24},{24,16},{1,9},{9,1},{17,25},{25,17},{2,10},{10... | collective-permute-start | bytes 368648 | tf_op jit(solution)/shard_map/ppermute | solution.py:31
  8.8 2.6 %collective-permute-start.2 = (bf16[480,128]{1,0:T(8,128)(2,1)}, bf16[480,128]{1,0:T(8,128)(2,1)S(1)}, u32[]{:S(2)}, u32[]{:S(2)}) collective-permute-start(bf16[480,128]{1,0:T(8,128)(2,1)} %encode.1.refs_3_.refs_0_), channel_id=1, source_target_pairs={{0,16},{8,24},{16,0},{24,8},{1,17},{9,25},{17,1},{25,9},{2,18},{10... | collective-permute-start | bytes 368648 | tf_op jit(solution)/shard_map/ppermute | solution.py:31
  11.4 1.5 %collective-permute-start.3 = (bf16[480,128]{1,0:T(8,128)(2,1)}, bf16[480,128]{1,0:T(8,128)(2,1)S(1)}, u32[]{:S(2)}, u32[]{:S(2)}) collective-permute-start(bf16[480,128]{1,0:T(8,128)(2,1)} %encode.1.refs_3_.refs_0_), channel_id=1, source_target_pairs={{0,4},{4,0},{1,5},{5,1},{2,6},{6,2},{3,7},{7,3},{8,12},{12,8},{9,1... | collective-permute-start | bytes 368648 | tf_op jit(solution)/shard_map/ppermute | solution.py:31
  12.9 0.0 collective-permute-done.4.refs_1_
  12.9 0.0 copy-start.2
  12.9 0.9 %copy-done.2 = bf16[480,128]{1,0:T(8,128)(2,1)S(1)} copy-done((bf16[480,128]{1,0:T(8,128)(2,1)S(1)}, bf16[480,128]{1,0:T(8,128)(2,1)}, u32[]{:S(2)}) %copy-start.2) | copy-done | bytes 122904
  13.8 2.4 %prepare.2 = (f32[384,1024]{1,0:T(8,128)S(1)}, bf16[256,384]{1,0:T(8,128)(2,1)S(1)}, bf16[256,384]{1,0:T(8,128)(2,1)S(1)}) custom-call(bf16[192,1024]{1,0:T(8,128)(2,1)S(1)} %copy-done.1, bf16[192,1024]{1,0:T(8,128)(2,1)S(1)} %collective-permute-done.4.refs_1_, bf16[1024,1024]{1,0:T(8,128)(2,1)S(1)} %copy-done, bf16[480,128]{1,0:T(8,128)(2,1)S(1)} %copy-done.2), custom_call_target="tpu_custom_call" | custom-call | flops 1 | bytes 1048576 | tf_op jit(solution)/shard_map/prepare/pallas_call | solution.py:320
  16.2 0.0 collective-permute-done.refs_3_.refs_1_
  16.2 0.0 collective-permute-done.1.refs_0_.refs_2_
  16.2 1.4 %collective-permute-done.2.refs_1_.refs_3_ = bf16[480,128]{1,0:T(8,128)(2,1)S(1)} collective-permute-done((bf16[480,128]{1,0:T(8,128)(2,1)}, bf16[480,128]{1,0:T(8,128)(2,1)S(1)}, u32[]{:S(2)}, u32[]{:S(2)}) %collective-permute-start.2) | collective-permute-done | bytes 122912 | tf_op jit(solution)/shard_map/ppermute | solution.py:31
  17.6 0.0 collective-permute-done.3.refs_2_.refs_3_
  17.6 0.2 gate.2
  17.9 0.1 collective-permute-start.5
  17.9 0.6 %collective-permute-start.11 = (bf16[192,1024]{1,0:T(8,128)(2,1)S(1)}, bf16[192,1024]{1,0:T(8,128)(2,1)S(1)}, u32[]{:S(2)}, u32[]{:S(2)}) collective-permute-start(bf16[192,1024]{1,0:T(8,128)(2,1)S(1)} %copy-done.1), channel_id=1, source_target_pairs={{0,2},{1,3},{2,0},{3,1},{4,6},{5,7},{6,4},{7,5},{8,10},{9,11},{10,... | collective-permute-start | bytes 1179656 | tf_op jit(solution)/shard_map/ppermute | solution.py:31
  18.5 1.5 %collective-permute-start.8 = (bf16[480,128]{1,0:T(8,128)(2,1)S(1)}, bf16[480,128]{1,0:T(8,128)(2,1)S(1)}, u32[]{:S(2)}, u32[]{:S(2)}) collective-permute-start(bf16[480,128]{1,0:T(8,128)(2,1)S(1)} %get-tuple-element.42.refs_2_), channel_id=1, source_target_pairs={{0,4},{1,9},{2,6},{3,11},{4,0},{5,13},{6,2},{7,15},{8,12},{9,1},{1... | collective-permute-start | bytes 368648 | tf_op jit(solution)/shard_map/ppermute | solution.py:46
  20.0 0.5 collective-permute-start.9
  20.6 0.4 collective-permute-start.6
  21.0 0.0 collective-permute-done.5.refs_1_
  21.0 2.0 %collective-permute-start.7 = (bf16[480,128]{1,0:T(8,128)(2,1)S(1)}, bf16[480,128]{1,0:T(8,128)(2,1)S(1)}, u32[]{:S(2)}, u32[]{:S(2)}) collective-permute-start(bf16[480,128]{1,0:T(8,128)(2,1)S(1)} %get-tuple-element.46), channel_id=1, source_target_pairs={{0,24},{1,5},{2,26},{3,7},{4,28},{5,1},{6,30},{7,3},{8,16},{9,13},... | collective-permute-start | bytes 368648 | tf_op jit(solution)/shard_map/ppermute | solution.py:46
  23.0 0.5 %rows.1 = (bf16[768,256]{1,0:T(8,128)(2,1)S(1)}, bf16[768,256]{1,0:T(8,128)(2,1)S(1)}) custom-call(bf16[960,128]{1,0:T(8,128)(2,1)S(1)} %gate.3.refs_0_.refs_2_, bf16[960,128]{1,0:T(8,128)(2,1)S(1)} %collective-permute-done.5.refs_1_), custom_call_target="tpu_custom_call" | custom-call | tf_op jit(solution)/shard_map/rows/pallas_call | solution.py:201
  23.6 1.3 %pairs.4 = (f32[768,128]{1,0:T(8,128)S(1)}, f32[768,64]{1,0:T(8,128)S(1)}, f32[768,128]{1,0:T(8,128)S(1)}) custom-call(bf16[768,256]{1,0:T(8,128)(2,1)S(1)} %get-tuple-element.43.refs_0_, bf16[768,256]{1,0:T(8,128)(2,1)S(1)} %get-tuple-element.44.refs_1_, bf16[960,128]{1,0:T(8,128)(2,1)S(1)} %gate.3.refs_0_.refs_2_, ...), custom_call_target="tpu_custom_call" | custom-call | flops 1 | bytes 884736 | tf_op jit(solution)/shard_map/pairs/pallas_call | solution.py:271
  24.9 1.4 %pairs.5 = (f32[768,128]{1,0:T(8,128)S(1)}, f32[768,64]{1,0:T(8,128)S(1)}, f32[768,128]{1,0:T(8,128)S(1)}) custom-call(bf16[768,256]{1,0:T(8,128)(2,1)S(1)} %get-tuple-element.43.refs_0_, bf16[768,256]{1,0:T(8,128)(2,1)S(1)} %get-tuple-element.44.refs_1_, bf16[480,128]{1,0:T(8,128)(2,1)S(1)} %collective-permute-done.1.refs_0_.refs_2_, ...), custom_call_target="tpu_custom_call" | custom-call | flops 1 | bytes 884736 | tf_op jit(solution)/shard_map/pairs/pallas_call | solution.py:271
  26.3 0.0 collective-permute-done.8.refs_2_
  26.3 0.0 collective-permute-done.9.refs_3_
  26.3 1.4 %pairs.6 = (f32[768,128]{1,0:T(8,128)S(1)}, f32[768,64]{1,0:T(8,128)S(1)}, f32[768,128]{1,0:T(8,128)S(1)}) custom-call(bf16[768,256]{1,0:T(8,128)(2,1)S(1)} %get-tuple-element.43.refs_0_, bf16[768,256]{1,0:T(8,128)(2,1)S(1)} %get-tuple-element.44.refs_1_, bf16[480,128]{1,0:T(8,128)(2,1)S(1)} %collective-permute-done.8.refs_2_, ...), custom_call_target="tpu_custom_call" | custom-call | flops 1 | bytes 884736 | tf_op jit(solution)/shard_map/pairs/pallas_call | solution.py:271
  27.7 0.0 collective-permute-done.6.refs_2_
  27.7 0.1 collective-permute-done.7.refs_3_
  27.8 1.4 %pairs.7 = (f32[384,128]{1,0:T(8,128)S(1)}, f32[384,128]{1,0:T(8,128)S(1)}, f32[384,128]{1,0:T(8,128)S(1)}) custom-call(bf16[768,256]{1,0:T(8,128)(2,1)S(1)} %get-tuple-element.43.refs_0_, bf16[768,256]{1,0:T(8,128)(2,1)S(1)} %get-tuple-element.44.refs_1_, bf16[480,128]{1,0:T(8,128)(2,1)S(1)} %collective-permute-done.6.refs_2_, ...), custom_call_target="tpu_custom_call" | custom-call | flops 1 | bytes 884736 | tf_op jit(solution)/shard_map/pairs/pallas_call | solution.py:271
  29.2 0.1 collective-permute-start.10
  29.3 0.2 collective-permute-done.11.x_ref.refs_0_
  29.5 1.2 %collective-permute-done.10.got_ref = f32[384,128]{1,0:T(8,128)S(1)} collective-permute-done((f32[384,128]{1,0:T(8,128)S(1)}, f32[384,128]{1,0:T(8,128)S(1)}, u32[]{:S(2)}, u32[]{:S(2)}) %collective-permute-start.10) | collective-permute-done | bytes 196640 | tf_op jit(solution)/shard_map/ppermute | solution.py:31
  30.7 0.1 merge.1
  30.8 0.2 collective-permute-start.14
  31.0 0.0 copy-start.4
  31.0 0.0 copy-start.5
  31.1 0.4 collective-permute-start.12
  31.5 1.5 %collective-permute-start.13 = (bf16[384,128]{1,0:T(8,128)(2,1)S(1)}, bf16[384,128]{1,0:T(8,128)(2,1)S(1)}, u32[]{:S(2)}, u32[]{:S(2)}) collective-permute-start(bf16[384,128]{1,0:T(8,128)(2,1)S(1)} %get-tuple-element.61), channel_id=1, source_target_pairs={{0,2},{1,3},{2,0},{3,1},{4,6},{5,7},{6,4},{7,5},{8,10},{9,11},{10,... | collective-permute-start | bytes 294920 | tf_op jit(solution)/shard_map/ppermute | solution.py:31
  33.0 0.0 collective-permute-done.14.refs_1_
  33.0 2.4 %prepare.3 = (f32[384,1024]{1,0:T(8,128)S(1)}, bf16[256,384]{1,0:T(8,128)(2,1)S(1)}, bf16[256,384]{1,0:T(8,128)(2,1)S(1)}) custom-call(bf16[192,1024]{1,0:T(8,128)(2,1)S(1)} %collective-permute-done.11.x_ref.refs_0_, bf16[192,1024]{1,0:T(8,128)(2,1)S(1)} %collective-permute-done.14.refs_1_, bf16[1024,1024]{1,0:T(8,128)(2,1)S(1)} %copy-done, ...), custom_call_target="tpu_custom_call" | custom-call | flops 1 | bytes 1048576 | tf_op jit(solution)/shard_map/prepare/pallas_call | solution.py:320
  35.4 1.0 %collective-permute-done.13.refs_1_ = bf16[384,128]{1,0:T(8,128)(2,1)S(1)} collective-permute-done((bf16[384,128]{1,0:T(8,128)(2,1)S(1)}, bf16[384,128]{1,0:T(8,128)(2,1)S(1)}, u32[]{:S(2)}, u32[]{:S(2)}) %collective-permute-start.13) | collective-permute-done | bytes 98336 | tf_op jit(solution)/shard_map/ppermute | solution.py:31
  36.3 0.0 copy-done.5
  36.3 1.6 %grads.1 = (bf16[544,128]{1,0:T(8,128)(2,1)S(1)}, bf16[272,128]{1,0:T(8,128)(2,1)S(1)}, bf16[272,128]{1,0:T(8,128)(2,1)S(1)}, bf16[272,128]{1,0:T(8,128)(2,1)S(1...) custom-call(f32[384,128]{1,0:T(8,128)S(1)} %get-tuple-element.60.refs_0_.refs_3_, ...), custom_call_target="tpu_custom_call" | custom-call | tf_op jit(solution)/shard_map/grads/pallas_call | solution.py:398
  37.9 1.6 %collective-permute-start.16 = (bf16[544,128]{1,0:T(8,128)(2,1)S(1)}, bf16[544,128]{1,0:T(8,128)(2,1)S(1)}, u32[]{:S(2)}, u32[]{:S(2)}) collective-permute-start(bf16[544,128]{1,0:T(8,128)(2,1)S(1)} %get-tuple-element.68.refs_0_), channel_id=1, source_target_pairs={{0,4},{4,0},{1,5},{5,1},{2,6},{6,2},{3,7},{7,3},{8,12},{12,8},{9,1... | collective-permute-start | bytes 417800 | tf_op jit(solution)/shard_map/ppermute | solution.py:31
  39.5 0.0 collective-permute-done.12
  39.6 1.6 %collective-permute-start.15 = (f32[192,128]{1,0:T(8,128)S(1)}, f32[192,128]{1,0:T(8,128)S(1)}, u32[]{:S(2)}, u32[]{:S(2)}) collective-permute-start(f32[192,128]{1,0:T(8,128)S(1)} %hold.3), channel_id=1, source_target_pairs={{0,2},{1,3},{2,0},{3,1},{4,6},{5,7},{6,4},{7,5},{8,10},{9,11},{10,... | collective-permute-start | bytes 294920 | tf_op jit(solution)/shard_map/ppermute | solution.py:31
  41.1 0.5 collective-permute-start.19
  41.6 1.5 %collective-permute-start.21 = (bf16[272,128]{1,0:T(8,128)(2,1)S(1)}, bf16[272,128]{1,0:T(8,128)(2,1)S(1)}, u32[]{:S(2)}, u32[]{:S(2)}) collective-permute-start(bf16[272,128]{1,0:T(8,128)(2,1)S(1)} %get-tuple-element.76), channel_id=1, source_target_pairs={{0,4},{4,0},{1,5},{5,1},{2,6},{6,2},{3,7},{7,3},{8,12},{12,8},{9,1... | collective-permute-start | bytes 208904 | tf_op jit(solution)/shard_map/ppermute | solution.py:31
  43.1 0.4 collective-permute-done.16.refs_0_
  43.6 3.1 %collective-permute-start.17 = (bf16[272,128]{1,0:T(8,128)(2,1)S(1)}, bf16[272,128]{1,0:T(8,128)(2,1)S(1)}, u32[]{:S(2)}, u32[]{:S(2)}) collective-permute-start(bf16[272,128]{1,0:T(8,128)(2,1)S(1)} %get-tuple-element.71.refs_2_), channel_id=1, source_target_pairs={{0,24},{8,16},{16,8},{24,0},{1,25},{9,17},{17,9},{25,1},{2,26},{10... | collective-permute-start | bytes 208904 | tf_op jit(solution)/shard_map/ppermute | solution.py:31
  46.8 0.0 collective-permute-start.18
  46.8 0.0 collective-permute-done.19.refs_0_
  46.8 0.0 collective-permute-done.15.refs_3_
  46.8 1.4 %collective-permute-start.20 = (bf16[272,128]{1,0:T(8,128)(2,1)S(1)}, bf16[272,128]{1,0:T(8,128)(2,1)S(1)}, u32[]{:S(2)}, u32[]{:S(2)}) collective-permute-start(bf16[272,128]{1,0:T(8,128)(2,1)S(1)} %relay.3), channel_id=1, source_target_pairs={{0,8},{8,0},{16,24},{24,16},{1,9},{9,1},{17,25},{25,17},{2,10},{10... | collective-permute-start | bytes 208904 | tf_op jit(solution)/shard_map/ppermute | solution.py:31
  48.2 0.6 %fusion.1 = bf16[192,128]{1,0:T(8,128)(2,1)} fusion(f32[192,128]{1,0:T(8,128)S(1)} %collective-permute-done.15.refs_3_, f32[384,128]{1,0:T(8,128)S(1)} %add.6), kind=kLoop, calls=%fused_computation.2 | loop fusion | flops 73728 | bytes 245760 | tf_op jit(solution)/shard_map/convert_element_type | solution.py:535
  48.8 0.0 collective-permute-done.21.refs_4_
  48.8 1.8 %collective-permute-done.17.refs_0_ = bf16[272,128]{1,0:T(8,128)(2,1)S(1)} collective-permute-done((bf16[272,128]{1,0:T(8,128)(2,1)S(1)}, bf16[272,128]{1,0:T(8,128)(2,1)S(1)}, u32[]{:S(2)}, u32[]{:S(2)}) %collective-permute-start.17) | collective-permute-done | bytes 69664 | tf_op jit(solution)/shard_map/ppermute | solution.py:31
  50.6 1.4 %collective-permute-done.18.refs_1_ = bf16[272,128]{1,0:T(8,128)(2,1)S(1)} collective-permute-done((bf16[272,128]{1,0:T(8,128)(2,1)S(1)}, bf16[272,128]{1,0:T(8,128)(2,1)S(1)}, u32[]{:S(2)}, u32[]{:S(2)}) %collective-permute-start.18) | collective-permute-done | bytes 69664 | tf_op jit(solution)/shard_map/ppermute | solution.py:31
  52.0 0.0 collective-permute-done.20.refs_3_
  52.0 0.7 %total.1 = (f32[32,1024]{1,0:T(8,128)}, f32[32,64]{1,0:T(8,128)}) custom-call(bf16[272,128]{1,0:T(8,128)(2,1)S(1)} %collective-permute-done.17.refs_0_, bf16[272,128]{1,0:T(8,128)(2,1)S(1)} %collective-permute-done.18.refs_1_, bf16[272,128]{1,0:T(8,128)(2,1)S(1)} %get-tuple-element.73.refs_2_, bf16[272,128]{1,0:T(8,128)(2,1)S(1)} %collective-permute-done.20.refs_3_, ...), custom_call_target="tpu_custom_call" | custom-call | tf_op jit(solution)/shard_map/total/pallas_call | solution.py:448
  (12 shorter events, 0.1 us)
Async XLA Ops:
  0.6 12.2 %copy-start.1 = (bf16[192,1024]{1,0:T(8,128)(2,1)S(1)}, bf16[192,1024]{1,0:T(8,128)(2,1)}, u32[]{:S(2)}) copy-start(bf16[192,1024]{1,0:T(8,128)(2,1)} %refs_0_.1) | copy-start | bytes 1179652
  0.6 12.2 %copy-start = (bf16[1024,1024]{1,0:T(8,128)(2,1)S(1)}, bf16[1024,1024]{1,0:T(8,128)(2,1)}, u32[]{:S(2)}) copy-start(bf16[1024,1024]{1,0:T(8,128)(2,1)} %refs_2_.3) | copy-start | bytes 6291460
  0.7 12.2 %collective-permute-start.4 = (bf16[192,1024]{1,0:T(8,128)(2,1)}, bf16[192,1024]{1,0:T(8,128)(2,1)S(1)}, u32[]{:S(2)}, u32[]{:S(2)}) collective-permute-start(bf16[192,1024]{1,0:T(8,128)(2,1)} %refs_0_.1), channel_id=1, source_target_pairs={{0,1},{1,0},{2,3},{3,2},{4,5},{5,4},{6,7},{7,6},{8,9},{9,8},{10,11... | collective-permute-start | bytes 1179656 | tf_op jit(solution)/shard_map/ppermute | solution.py:31
  4.7 11.5 %collective-permute-start = (bf16[480,128]{1,0:T(8,128)(2,1)}, bf16[480,128]{1,0:T(8,128)(2,1)S(1)}, u32[]{:S(2)}, u32[]{:S(2)}) collective-permute-start(bf16[480,128]{1,0:T(8,128)(2,1)} %encode.1.refs_3_.refs_0_), channel_id=1, source_target_pairs={{0,2},{1,3},{2,0},{3,1},{4,6},{5,7},{6,4},{7,5},{8,10},{9,11},{10,... | collective-permute-start | bytes 368648 | tf_op jit(solution)/shard_map/ppermute | solution.py:31
  7.2 9.0 %collective-permute-start.1 = (bf16[480,128]{1,0:T(8,128)(2,1)}, bf16[480,128]{1,0:T(8,128)(2,1)S(1)}, u32[]{:S(2)}, u32[]{:S(2)}) collective-permute-start(bf16[480,128]{1,0:T(8,128)(2,1)} %encode.1.refs_3_.refs_0_), channel_id=1, source_target_pairs={{0,8},{8,0},{16,24},{24,16},{1,9},{9,1},{17,25},{25,17},{2,10},{10... | collective-permute-start | bytes 368648 | tf_op jit(solution)/shard_map/ppermute | solution.py:31
  8.8 8.8 %collective-permute-start.2 = (bf16[480,128]{1,0:T(8,128)(2,1)}, bf16[480,128]{1,0:T(8,128)(2,1)S(1)}, u32[]{:S(2)}, u32[]{:S(2)}) collective-permute-start(bf16[480,128]{1,0:T(8,128)(2,1)} %encode.1.refs_3_.refs_0_), channel_id=1, source_target_pairs={{0,16},{8,24},{16,0},{24,8},{1,17},{9,25},{17,1},{25,9},{2,18},{10... | collective-permute-start | bytes 368648 | tf_op jit(solution)/shard_map/ppermute | solution.py:31
  11.4 6.2 %collective-permute-start.3 = (bf16[480,128]{1,0:T(8,128)(2,1)}, bf16[480,128]{1,0:T(8,128)(2,1)S(1)}, u32[]{:S(2)}, u32[]{:S(2)}) collective-permute-start(bf16[480,128]{1,0:T(8,128)(2,1)} %encode.1.refs_3_.refs_0_), channel_id=1, source_target_pairs={{0,4},{4,0},{1,5},{5,1},{2,6},{6,2},{3,7},{7,3},{8,12},{12,8},{9,1... | collective-permute-start | bytes 368648 | tf_op jit(solution)/shard_map/ppermute | solution.py:31
  12.9 0.9 %copy-start.2 = (bf16[480,128]{1,0:T(8,128)(2,1)S(1)}, bf16[480,128]{1,0:T(8,128)(2,1)}, u32[]{:S(2)}) copy-start(bf16[480,128]{1,0:T(8,128)(2,1)} %encode.1.refs_3_.refs_0_) | copy-start | bytes 368644
  13.8 4.0 %copy-start.3 = (bf16[480,128]{1,0:T(8,128)(2,1)S(1)}, bf16[480,128]{1,0:T(8,128)(2,1)}, u32[]{:S(2)}) copy-start(bf16[480,128]{1,0:T(8,128)(2,1)} %encode.1.refs_3_.refs_0_) | copy-start | bytes 368644
  17.9 3.1 %collective-permute-start.5 = (bf16[960,128]{1,0:T(8,128)(2,1)S(1)}, bf16[960,128]{1,0:T(8,128)(2,1)S(1)}, u32[]{:S(2)}, u32[]{:S(2)}) collective-permute-start(bf16[960,128]{1,0:T(8,128)(2,1)S(1)} %gate.3.refs_0_.refs_2_), channel_id=1, source_target_pairs={{0,1},{1,0},{2,3},{3,2},{4,5},{5,4},{6,7},{7,6},{8,9},{9,8},{10,11... | collective-permute-start | bytes 737288 | tf_op jit(solution)/shard_map/ppermute | solution.py:31
  17.9 11.5 %collective-permute-start.11 = (bf16[192,1024]{1,0:T(8,128)(2,1)S(1)}, bf16[192,1024]{1,0:T(8,128)(2,1)S(1)}, u32[]{:S(2)}, u32[]{:S(2)}) collective-permute-start(bf16[192,1024]{1,0:T(8,128)(2,1)S(1)} %copy-done.1), channel_id=1, source_target_pairs={{0,2},{1,3},{2,0},{3,1},{4,6},{5,7},{6,4},{7,5},{8,10},{9,11},{10,... | collective-permute-start | bytes 1179656 | tf_op jit(solution)/shard_map/ppermute | solution.py:31
  18.5 7.8 %collective-permute-start.8 = (bf16[480,128]{1,0:T(8,128)(2,1)S(1)}, bf16[480,128]{1,0:T(8,128)(2,1)S(1)}, u32[]{:S(2)}, u32[]{:S(2)}) collective-permute-start(bf16[480,128]{1,0:T(8,128)(2,1)S(1)} %get-tuple-element.42.refs_2_), channel_id=1, source_target_pairs={{0,4},{1,9},{2,6},{3,11},{4,0},{5,13},{6,2},{7,15},{8,12},{9,1},{1... | collective-permute-start | bytes 368648 | tf_op jit(solution)/shard_map/ppermute | solution.py:46
  20.0 6.2 %collective-permute-start.9 = (bf16[480,128]{1,0:T(8,128)(2,1)S(1)}, bf16[480,128]{1,0:T(8,128)(2,1)S(1)}, u32[]{:S(2)}, u32[]{:S(2)}) collective-permute-start(bf16[480,128]{1,0:T(8,128)(2,1)S(1)} %get-tuple-element.47), channel_id=1, source_target_pairs={{0,4},{1,25},{2,6},{3,27},{4,0},{5,29},{6,2},{7,31},{8,12},{9,17},... | collective-permute-start | bytes 368648 | tf_op jit(solution)/shard_map/ppermute | solution.py:46
  20.6 7.1 %collective-permute-start.6 = (bf16[480,128]{1,0:T(8,128)(2,1)S(1)}, bf16[480,128]{1,0:T(8,128)(2,1)S(1)}, u32[]{:S(2)}, u32[]{:S(2)}) collective-permute-start(bf16[480,128]{1,0:T(8,128)(2,1)S(1)} %get-tuple-element.45), channel_id=1, source_target_pairs={{0,8},{1,5},{2,10},{3,7},{4,12},{5,1},{6,14},{7,3},{8,0},{9,13},{1... | collective-permute-start | bytes 368648 | tf_op jit(solution)/shard_map/ppermute | solution.py:46
  21.0 6.8 %collective-permute-start.7 = (bf16[480,128]{1,0:T(8,128)(2,1)S(1)}, bf16[480,128]{1,0:T(8,128)(2,1)S(1)}, u32[]{:S(2)}, u32[]{:S(2)}) collective-permute-start(bf16[480,128]{1,0:T(8,128)(2,1)S(1)} %get-tuple-element.46), channel_id=1, source_target_pairs={{0,24},{1,5},{2,26},{3,7},{4,28},{5,1},{6,30},{7,3},{8,16},{9,13},... | collective-permute-start | bytes 368648 | tf_op jit(solution)/shard_map/ppermute | solution.py:46
  29.2 1.5 %collective-permute-start.10 = (f32[384,128]{1,0:T(8,128)S(1)}, f32[384,128]{1,0:T(8,128)S(1)}, u32[]{:S(2)}, u32[]{:S(2)}) collective-permute-start(f32[384,128]{1,0:T(8,128)S(1)} %get-tuple-element.59.term_ref), channel_id=1, source_target_pairs={{0,1},{1,0},{2,3},{3,2},{4,5},{5,4},{6,7},{7,6},{8,9},{9,8},{10,11... | collective-permute-start | bytes 589832 | tf_op jit(solution)/shard_map/ppermute | solution.py:31
  30.8 2.2 %collective-permute-start.14 = (bf16[192,1024]{1,0:T(8,128)(2,1)S(1)}, bf16[192,1024]{1,0:T(8,128)(2,1)S(1)}, u32[]{:S(2)}, u32[]{:S(2)}) collective-permute-start(bf16[192,1024]{1,0:T(8,128)(2,1)S(1)} %get-tuple-element.64), channel_id=1, source_target_pairs={{0,1},{1,0},{2,3},{3,2},{4,5},{5,4},{6,7},{7,6},{8,9},{9,8},{10,11... | collective-permute-start | bytes 1179656 | tf_op jit(solution)/shard_map/ppermute | solution.py:31
  31.0 5.3 %copy-start.4 = (bf16[1024,64]{0,1:T(8,128)(2,1)S(1)}, bf16[1024,64]{0,1:T(8,128)(2,1)}, u32[]{:S(2)}) copy-start(bf16[1024,64]{0,1:T(8,128)(2,1)} %param.8) | copy-start | bytes 393220
  31.0 5.3 %copy-start.5 = (f32[64]{0:T(128)S(1)}, f32[64]{0:T(128)}, u32[]{:S(2)}) copy-start(f32[64]{0:T(128)} %param.9) | copy-start | bytes 772
  31.1 8.4 %collective-permute-start.12 = (f32[384,128]{1,0:T(8,128)S(1)}, f32[384,128]{1,0:T(8,128)S(1)}, u32[]{:S(2)}, u32[]{:S(2)}) collective-permute-start(f32[384,128]{1,0:T(8,128)S(1)} %hold.2), channel_id=1, source_target_pairs={{0,1},{1,0},{2,3},{3,2},{4,5},{5,4},{6,7},{7,6},{8,9},{9,8},{10,11... | collective-permute-start | bytes 589832 | tf_op jit(solution)/shard_map/ppermute | solution.py:31
  31.5 4.8 %collective-permute-start.13 = (bf16[384,128]{1,0:T(8,128)(2,1)S(1)}, bf16[384,128]{1,0:T(8,128)(2,1)S(1)}, u32[]{:S(2)}, u32[]{:S(2)}) collective-permute-start(bf16[384,128]{1,0:T(8,128)(2,1)S(1)} %get-tuple-element.61), channel_id=1, source_target_pairs={{0,2},{1,3},{2,0},{3,1},{4,6},{5,7},{6,4},{7,5},{8,10},{9,11},{10,... | collective-permute-start | bytes 294920 | tf_op jit(solution)/shard_map/ppermute | solution.py:31
  37.9 5.7 %collective-permute-start.16 = (bf16[544,128]{1,0:T(8,128)(2,1)S(1)}, bf16[544,128]{1,0:T(8,128)(2,1)S(1)}, u32[]{:S(2)}, u32[]{:S(2)}) collective-permute-start(bf16[544,128]{1,0:T(8,128)(2,1)S(1)} %get-tuple-element.68.refs_0_), channel_id=1, source_target_pairs={{0,4},{4,0},{1,5},{5,1},{2,6},{6,2},{3,7},{7,3},{8,12},{12,8},{9,1... | collective-permute-start | bytes 417800 | tf_op jit(solution)/shard_map/ppermute | solution.py:31
  39.6 7.2 %collective-permute-start.15 = (f32[192,128]{1,0:T(8,128)S(1)}, f32[192,128]{1,0:T(8,128)S(1)}, u32[]{:S(2)}, u32[]{:S(2)}) collective-permute-start(f32[192,128]{1,0:T(8,128)S(1)} %hold.3), channel_id=1, source_target_pairs={{0,2},{1,3},{2,0},{3,1},{4,6},{5,7},{6,4},{7,5},{8,10},{9,11},{10,... | collective-permute-start | bytes 294920 | tf_op jit(solution)/shard_map/ppermute | solution.py:31
  41.1 5.7 %collective-permute-start.19 = (bf16[272,128]{1,0:T(8,128)(2,1)S(1)}, bf16[272,128]{1,0:T(8,128)(2,1)S(1)}, u32[]{:S(2)}, u32[]{:S(2)}) collective-permute-start(bf16[272,128]{1,0:T(8,128)(2,1)S(1)} %get-tuple-element.74), channel_id=1, source_target_pairs={{0,4},{4,0},{1,5},{5,1},{2,6},{6,2},{3,7},{7,3},{8,12},{12,8},{9,1... | collective-permute-start | bytes 208904 | tf_op jit(solution)/shard_map/ppermute | solution.py:31
  41.6 7.2 %collective-permute-start.21 = (bf16[272,128]{1,0:T(8,128)(2,1)S(1)}, bf16[272,128]{1,0:T(8,128)(2,1)S(1)}, u32[]{:S(2)}, u32[]{:S(2)}) collective-permute-start(bf16[272,128]{1,0:T(8,128)(2,1)S(1)} %get-tuple-element.76), channel_id=1, source_target_pairs={{0,4},{4,0},{1,5},{5,1},{2,6},{6,2},{3,7},{7,3},{8,12},{12,8},{9,1... | collective-permute-start | bytes 208904 | tf_op jit(solution)/shard_map/ppermute | solution.py:31
  43.6 7.0 %collective-permute-start.17 = (bf16[272,128]{1,0:T(8,128)(2,1)S(1)}, bf16[272,128]{1,0:T(8,128)(2,1)S(1)}, u32[]{:S(2)}, u32[]{:S(2)}) collective-permute-start(bf16[272,128]{1,0:T(8,128)(2,1)S(1)} %get-tuple-element.71.refs_2_), channel_id=1, source_target_pairs={{0,24},{8,16},{16,8},{24,0},{1,25},{9,17},{17,9},{25,1},{2,26},{10... | collective-permute-start | bytes 208904 | tf_op jit(solution)/shard_map/ppermute | solution.py:31
  46.8 5.2 %collective-permute-start.18 = (bf16[272,128]{1,0:T(8,128)(2,1)S(1)}, bf16[272,128]{1,0:T(8,128)(2,1)S(1)}, u32[]{:S(2)}, u32[]{:S(2)}) collective-permute-start(bf16[272,128]{1,0:T(8,128)(2,1)S(1)} %get-tuple-element.72), channel_id=1, source_target_pairs={{0,16},{8,24},{16,0},{24,8},{1,17},{9,25},{17,1},{25,9},{2,18},{10... | collective-permute-start | bytes 208904 | tf_op jit(solution)/shard_map/ppermute | solution.py:31
  46.8 5.2 %collective-permute-start.20 = (bf16[272,128]{1,0:T(8,128)(2,1)S(1)}, bf16[272,128]{1,0:T(8,128)(2,1)S(1)}, u32[]{:S(2)}, u32[]{:S(2)}) collective-permute-start(bf16[272,128]{1,0:T(8,128)(2,1)S(1)} %relay.3), channel_id=1, source_target_pairs={{0,8},{8,0},{16,24},{24,16},{1,9},{9,1},{17,25},{25,17},{2,10},{10... | collective-permute-start | bytes 208904 | tf_op jit(solution)/shard_map/ppermute | solution.py:31
